TPU v7x, 32 devices: a whole 2x2x4 slice. The times are simulated.
32 devices in a mesh: walkers: 8 (over z, y), orb: 4 (over x, core).
Axes of the slice: x: 2, y: 2, z: 4, core: 2. Of those that a mesh axis runs over, the one named last changes fastest.
Arguments:
- inverse: float32 [32, 2, 128, 128], P('walkers', None, 'orb'), as said below
- slater: float32 [32, 2, 128, 128], P('walkers', None, 'orb'), may hold values from -1 to 3, as said below
- positions: float32 [32, 3, 256], P('walkers'), may hold values from -2 to 10
- displacements: float32 [32, 3, 256], P('walkers'), may hold values from -0.6 to 0.6
- move_order: int32 [32, 2, 128], P('walkers'), may hold values from 0 to 127, each once within a row
- accepted: int32 [32, 2, 32], P('walkers'), may hold values 0 or 1
- counts: int32 [32], P('walkers'), may hold values from 0 to 2, as said below
- log_amp: float32 [32], P('walkers'), may hold values from -4 to 4
- centers: float32 [3, 1024], replicated, may hold values from 0 to 8
- exponents: float32 [1024], replicated, may hold values from 0.3 to 3
- orbitals: float32 [2, 128, 1024], P(None, 'orb'), may hold values from -0.36 to 0.36
- jastrow: float32 [4], replicated, may hold values from 0.2 to 0.6
Outputs:
- inverse_new: float32 [32, 2, 128, 128], P('walkers', None, 'orb')
- slater_new: float32 [32, 2, 128, 128], P('walkers', None, 'orb')
- positions_new: float32 [32, 3, 256], P('walkers')
- log_amp_new: float32 [32], P('walkers')
- local_energy_new: float32 [32], P('walkers')
- energy_mean: float32 [], replicated
Inputs may be any that keep to these rules, and one draw needn't show every extreme that they name: For every walker and spin, inverse is the inverse of the transpose of slater: the sum over o of slater[w, s, o, e] * inverse[w, s, o, f] is 1 when e = f and 0 otherwise, up to float32 rounding. `slater`: orbital values at the current positions. All counts sum to 32; for every whole m, the counts of the first m * 4 walkers sum to a value within 2 of m * 4, and both ends of that band are reached.
All inputs are finite; a program needn't handle non-finite values. No bound on the sum of `accepted` on one device may be relied on, other than what follows from the above.
Results may differ from a plain program's by a relative error of at most 0.0003.
Values sent between devices are 32-bit elements; how exact they have to be, the bound alone decides.
No kernel may reach another device: no remote copies, remote signals or barrier semaphores. Data moves between devices by JAX's collectives and lax.ppermute only.
A program may use at most 64 MiB of HBM per device.

v0:
```python
import jax
import jax.numpy as jnp
from jax import lax
from jax.sharding import PartitionSpec as P

NEL = 128
K = 32
MOVES = 32


highest = lax.Precision.HIGHEST


def entering(part, axis, combine, identity):
    place = lax.axis_index(axis)
    gathered = lax.all_gather(part, axis)
    state = jnp.zeros_like(part) + jnp.asarray(identity, part.dtype)

    def one(lap, state):
        return combine(state, lax.dynamic_index_in_dim(gathered, lap, 0, False))

    return lax.fori_loop(0, place, one, state)


def with_halo(cells, sides, width):
    for axis, dim in sides:
        count = lax.axis_size(axis)
        ends = count - 1
        head = lax.slice_in_dim(cells, 0, width, axis=dim)
        tail = lax.slice_in_dim(cells, cells.shape[dim] - width, cells.shape[dim], axis=dim)
        cells = jnp.concatenate(
            [
                lax.ppermute(tail, axis, [(i, (i + 1) % count) for i in range(ends)]),
                cells,
                lax.ppermute(head, axis, [((i + 1) % count, i) for i in range(ends)]),
            ],
            axis=dim,
        )
    return cells


def basis_values(points, centers, exponents):
    squares = jnp.zeros((centers.shape[1], points.shape[1]), jnp.float32)
    for component in range(3):
        offset = points[component][None, :] - centers[component][:, None]
        squares = squares + offset * offset
    return jnp.exp(-exponents[:, None] * squares)


def orbital_change(points, steps, centers, exponents, orbitals):
    count = points.shape[1] // 2
    differ = basis_values(points + steps, centers, exponents) - basis_values(
        points, centers, exponents
    )
    spin_up = jnp.dot(
        orbitals[0], differ[:, :count], precision=highest, preferred_element_type=jnp.float32
    )
    spin_down = jnp.dot(
        orbitals[1], differ[:, count:], precision=highest, preferred_element_type=jnp.float32
    )
    return jnp.stack([spin_up, spin_down])


def pair_terms(before, after, jastrow):
    total = before.shape[1]
    old_squares = jnp.zeros((total, total), jnp.float32)
    new_squares = jnp.zeros((total, total), jnp.float32)
    for component in range(3):
        old_offset = before[component][:, None] - before[component][None, :]
        new_offset = after[component][:, None] - after[component][None, :]
        old_squares = old_squares + old_offset * old_offset
        new_squares = new_squares + new_offset * new_offset
    spins = jnp.arange(total) // (total // 2)
    same = spins[:, None] == spins[None, :]
    height = jnp.where(same, jastrow[0], jastrow[1])
    falloff = jnp.where(same, jastrow[2], jastrow[3])
    old_dist = jnp.sqrt(old_squares)
    new_dist = jnp.sqrt(new_squares)
    change = jnp.sum(
        height * (new_dist / (1.0 + falloff * new_dist) - old_dist / (1.0 + falloff * old_dist))
    )
    soft = jnp.sum(1.0 / jnp.sqrt(new_squares + 1.0))
    return (change, soft)


def eliminate(coupling, change):
    size = coupling.shape[-1]
    matrix = jnp.concatenate([coupling, change], axis=-1)
    labels = jnp.arange(size)

    def sweep(index, carry):
        matrix, logsum = carry
        pivot_row = lax.dynamic_slice_in_dim(matrix, index, 1, matrix.ndim - 2)
        pivot = lax.dynamic_slice_in_dim(pivot_row, index, 1, matrix.ndim - 1)
        pivot_row = pivot_row / pivot
        column_now = lax.dynamic_slice_in_dim(matrix, index, 1, matrix.ndim - 1)
        mine = (labels == index)[:, None]
        matrix = jnp.where(mine, pivot_row, matrix - column_now * pivot_row)
        return (matrix, logsum + jnp.log(jnp.abs(pivot[..., 0, 0])))

    start = (matrix, jnp.zeros(coupling.shape[:-2], jnp.float32))
    matrix, logsum = lax.fori_loop(0, size, sweep, start)
    return (matrix[..., size:], logsum)


def run_windows(proposed, current, move_order, accepted):
    labels = jnp.arange(NEL)
    chosen = move_order[:, :, 0:K]
    one_hot = (labels[None, None, :, None] == chosen[:, :, None, :]).astype(jnp.float32)
    proposed_cols = jnp.einsum("wsoe,wsek->wsok", proposed, one_hot, precision=highest)
    local_part = jnp.einsum("wsok,wsoe->wske", proposed_cols, current, precision=highest)
    unit_rows = jnp.swapaxes(one_hot, 2, 3)
    effective = jnp.where(accepted[..., None] == 1, local_part, unit_rows)
    coupling = jnp.einsum("wske,wsel->wskl", effective, one_hot, precision=highest)
    solved, logsum = eliminate(coupling, effective - unit_rows)
    columns = jnp.einsum("wsoe,wsek->wsok", current, one_hot, precision=highest)
    current = current - jnp.einsum("wsok,wske->wsoe", columns, solved, precision=highest)
    return (current, logsum)


def add_counts(earlier, later):
    return earlier + later


def slot_table(first_slot, starts, limits, length):
    slot_ids = first_slot + jnp.arange(length, dtype=jnp.int32)
    inside = (starts[None, :] <= slot_ids[:, None]) & (slot_ids[:, None] < limits[None, :])
    return inside.astype(jnp.float32)


def place_rows(table, matrices, places, scalars):
    return (
        jnp.tensordot(table, matrices, axes=(1, 0), precision=highest),
        jnp.tensordot(table, places, axes=(1, 0), precision=highest),
        jnp.tensordot(table, scalars, axes=(1, 0), precision=highest),
    )


def body(
    inverse,
    slater,
    positions,
    displacements,
    move_order,
    accepted,
    counts,
    log_amp,
    centers,
    exponents,
    orbitals,
    jastrow,
):
    walkers_here = inverse.shape[0]

    def per_walker(pair):
        return orbital_change(pair[0], pair[1], centers, exponents, orbitals)

    orbital_shift = lax.map(per_walker, (positions, displacements))
    labels = jnp.arange(NEL)
    placed = (move_order[:, :, :MOVES, None] == labels[None, None, None, :]).astype(jnp.float32)
    applied = jnp.einsum("wsk,wske->wse", accepted.astype(jnp.float32), placed, precision=highest)
    positions_now = positions + displacements * applied.reshape(walkers_here, 1, 2 * NEL)
    group = lax.axis_size("orb")
    subset = walkers_here // group
    begin = lax.axis_index("orb") * subset
    inverse_whole, slater_whole, shift_whole = (
        lax.all_to_all(inverse, "orb", split_axis=0, concat_axis=2, tiled=True),
        lax.all_to_all(slater, "orb", split_axis=0, concat_axis=2, tiled=True),
        lax.all_to_all(orbital_shift, "orb", split_axis=0, concat_axis=2, tiled=True),
    )
    order_sub = lax.dynamic_slice_in_dim(move_order, begin, subset, 0)
    flags_sub = lax.dynamic_slice_in_dim(accepted, begin, subset, 0)
    applied_sub = lax.dynamic_slice_in_dim(applied, begin, subset, 0)
    current_whole, logdet_sub = run_windows(
        slater_whole + shift_whole, inverse_whole, order_sub, flags_sub
    )
    slater_done = slater_whole + shift_whole * applied_sub[:, :, None, :]
    logdet_tiled = jnp.broadcast_to(logdet_sub[:, :, None, None], (subset, 2, group, 1))
    current, slater_now, logdet_all = (
        lax.all_to_all(current_whole, "orb", split_axis=2, concat_axis=0, tiled=True),
        lax.all_to_all(slater_done, "orb", split_axis=2, concat_axis=0, tiled=True),
        lax.all_to_all(logdet_tiled, "orb", split_axis=2, concat_axis=0, tiled=True),
    )
    logdet = logdet_all[:, :, 0, 0]

    def walker_pairs(pair):
        return pair_terms(pair[0], pair[1], jastrow)

    jastrow_change, soft_total = lax.map(walker_pairs, (positions, positions_now))
    log_now = log_amp + jnp.sum(logdet, axis=1) + 0.5 * jastrow_change
    energy = (soft_total - 2.0 * NEL) / (2.0 * NEL * (2 * NEL - 1))
    weighted = jnp.sum(counts.astype(jnp.float32) * energy)
    energy_sum = lax.psum(weighted, "walkers")
    energy_mean = energy_sum / (walkers_here * lax.axis_size("walkers"))
    local_total = jnp.sum(counts)
    offset = entering(local_total, "walkers", add_counts, jnp.int32(0))
    limits = offset + jnp.cumsum(counts)
    starts = limits - counts
    matrices = jnp.stack([current, slater_now], axis=1)
    scalars = jnp.stack([log_now, energy], axis=1)
    rank_here = lax.axis_index("walkers")
    first_slot = rank_here * walkers_here
    below = place_rows(
        slot_table(first_slot - walkers_here, starts, limits, walkers_here),
        matrices,
        positions_now,
        scalars,
    )
    stay = place_rows(
        slot_table(first_slot, starts, limits, walkers_here), matrices, positions_now, scalars
    )
    above = place_rows(
        slot_table(first_slot + walkers_here, starts, limits, walkers_here),
        matrices,
        positions_now,
        scalars,
    )
    out_matrices = jnp.concatenate([below[0], above[0]], axis=0)
    out_positions = jnp.concatenate([below[1], above[1]], axis=0)
    out_scalars = jnp.concatenate([below[2], above[2]], axis=0)
    padded = (
        with_halo(out_matrices, (("walkers", 0),), walkers_here),
        with_halo(out_positions, (("walkers", 0),), walkers_here),
        with_halo(out_scalars, (("walkers", 0),), walkers_here),
    )
    new_matrices = stay[0] + padded[0][:walkers_here] + padded[0][3 * walkers_here :]
    new_positions = stay[1] + padded[1][:walkers_here] + padded[1][3 * walkers_here :]
    new_scalars = stay[2] + padded[2][:walkers_here] + padded[2][3 * walkers_here :]
    return (
        new_matrices[:, 0],
        new_matrices[:, 1],
        new_positions,
        new_scalars[:, 0],
        new_scalars[:, 1],
        energy_mean,
    )


def solution(mesh):
    return jax.shard_map(
        body,
        mesh=mesh,
        in_specs=(
            P("walkers", None, "orb", None),
            P("walkers", None, "orb", None),
            P("walkers", None, None),
            P("walkers", None, None),
            P("walkers", None, None),
            P("walkers", None, None),
            P("walkers"),
            P("walkers"),
            P(),
            P(),
            P(None, "orb", None),
            P(),
        ),
        out_specs=(
            P("walkers", None, "orb", None),
            P("walkers", None, "orb", None),
            P("walkers", None, None),
            P("walkers"),
            P("walkers"),
            P(),
        ),
        check_vma=False,
    )
```

profile of v0, /device:TPU:0, one launch (start us, length us, event | category | flops | bytes accessed | tf_op | source)
XLA Modules:
  0.0 189.3 jit_solution(14136148664941353084)
XLA Ops:
  1.4 26.0 %while.56 = (s32[]{:T(128)}, f32[4,2,32,128]{3,2,1,0:T(8,128)}, f32[1024,1]{0,1:T(1,128)S(1)}, f32[4,3,256]{2,0,1:T(4,128)}, f32[4,3,256]{2,0,1:T(4,128)}, /*ind...) while((s32[]{:T(128)}, f32[4,2,32,128]{3,2,1,0:T(8,128)}, ...), condition=%wide.region_5.6_spmd, body=%wide.region_4.5_spmd.sunk | while | flops 105652992 | bytes 2526369 | solution.py:158
  27.4 4.2 %all-to-all-start.2 = ((f32[4,2,32,128]{3,2,1,0:T(8,128)}), f32[4,2,32,128]{3,2,1,0:T(8,128)S(1)}, u32[]{:S(2)}, u32[]{:S(2)}) async-start(f32[4,2,32,128]{3,2,1,0:T(8,128)} %get-tuple-element.317), calls=%async_computation.2 | async-start | bytes 262144 | tf_op jit(solution)/shard_map/all_to_all | solution.py:169
  32.8 1.4 dynamic-update-slice
  34.4 12.2 %all-reduce = s32[8]{0:T(128)S(1)} all-reduce(s32[8]{0:T(128)S(1)} %dynamic-update-slice), channel_id=1, replica_groups=mesh['walkers'=8,'orb'=4] {'walkers'}, use_global_device_ids=true, to_apply=%add | all-reduce | flops 8 | bytes 64
  49.3 5.3 %collective-permute-start.2 = (f32[4,3,256]{2,0,1:T(4,128)S(1)}, f32[4,3,256]{2,0,1:T(4,128)S(1)}, u32[]{:S(2)}, u32[]{:S(2)}) collective-permute-start(f32[4,3,256]{2,0,1:T(4,128)S(1)} %fusion.36), channel_id=1, source_target_pairs={{0,4},{4,8},{8,12},{12,16},{16,20},{20,24},{24,28},{1,5},{5,9},{9,... | collective-permute-start | bytes 36872 | tf_op jit(solution)/shard_map/ppermute | solution.py:33
  54.7 25.8 %while.57 = (s32[]{:T(128)}, f32[4]{0:T(128)S(1)}, f32[4]{0:T(128)S(1)}, f32[4]{0:T(128)S(1)}, f32[4,3,256]{2,1,0:T(4,128)S(1)}, /*index=5*/f32[4,3,256]{2,0,1:T(4,128)}, s32[]{:T(128)}, s32[]{:T(128)}, s32[]{}, s32[]{}) while((s32[]{:T(128)}, f32[4]{0:T(128)S(1)}, f32[4]{0:T(128)S(1)}, f32[4]{0:T(128)S(1)}, f32[4,3,256]{2,1,0:T(4,128)S(1)}, ...), condition=%wide.region_12.13_spmd, body=%wide.region_9.12_spmd.sunk | while | flops 1968130 | bytes 20717 | solution.py:189
  56.0 3.7 %rsqrt_reduce_fusion.2 = (f32[]{:T(128)}, f32[]{:T(128)}) fusion(f32[256]{0:T(256)S(1)} %bitcast.257, f32[256]{0:T(256)S(1)} %bitcast.256, f32[256]{0:T(256)S(1)} %bitcast.255, f32[256]{0:T(256)S(1)} %bitcast.260, f32[256]{0:T(256)S(1)} %bitcast.259, f32[256]{0:T(256)S(1)} %bitcast.258, f32[]{:T(128)} %bitcast.220, f32[]{:T(128)} %bitcast.221, ...), kind=kLoop, calls=%fused_computation.26.clone.1 | loop fusion | flops 1966078 | bytes 7192 | tf_op jit(solution)/shard_map/while/body/eval_jaxpr/reduce_sum | solution.py:82
  62.5 3.7 %rsqrt_reduce_fusion.2 = (f32[]{:T(128)}, f32[]{:T(128)}) fusion(f32[256]{0:T(256)S(1)} %bitcast.257, f32[256]{0:T(256)S(1)} %bitcast.256, f32[256]{0:T(256)S(1)} %bitcast.255, f32[256]{0:T(256)S(1)} %bitcast.260, f32[256]{0:T(256)S(1)} %bitcast.259, f32[256]{0:T(256)S(1)} %bitcast.258, f32[]{:T(128)} %bitcast.220, f32[]{:T(128)} %bitcast.221, ...), kind=kLoop, calls=%fused_computation.26.clone.1 | loop fusion | flops 1966078 | bytes 7192 | tf_op jit(solution)/shard_map/while/body/eval_jaxpr/reduce_sum | solution.py:82
  68.9 3.7 %rsqrt_reduce_fusion.2 = (f32[]{:T(128)}, f32[]{:T(128)}) fusion(f32[256]{0:T(256)S(1)} %bitcast.257, f32[256]{0:T(256)S(1)} %bitcast.256, f32[256]{0:T(256)S(1)} %bitcast.255, f32[256]{0:T(256)S(1)} %bitcast.260, f32[256]{0:T(256)S(1)} %bitcast.259, f32[256]{0:T(256)S(1)} %bitcast.258, f32[]{:T(128)} %bitcast.220, f32[]{:T(128)} %bitcast.221, ...), kind=kLoop, calls=%fused_computation.26.clone.1 | loop fusion | flops 1966078 | bytes 7192 | tf_op jit(solution)/shard_map/while/body/eval_jaxpr/reduce_sum | solution.py:82
  75.3 3.7 %rsqrt_reduce_fusion.2 = (f32[]{:T(128)}, f32[]{:T(128)}) fusion(f32[256]{0:T(256)S(1)} %bitcast.257, f32[256]{0:T(256)S(1)} %bitcast.256, f32[256]{0:T(256)S(1)} %bitcast.255, f32[256]{0:T(256)S(1)} %bitcast.260, f32[256]{0:T(256)S(1)} %bitcast.259, f32[256]{0:T(256)S(1)} %bitcast.258, f32[]{:T(128)} %bitcast.220, f32[]{:T(128)} %bitcast.221, ...), kind=kLoop, calls=%fused_computation.26.clone.1 | loop fusion | flops 1966078 | bytes 7192 | tf_op jit(solution)/shard_map/while/body/eval_jaxpr/reduce_sum | solution.py:82
  81.0 23.7 %psum.7 = f32[]{:T(128)} all-reduce(f32[]{:T(128)} %get-tuple-element.451), channel_id=1, replica_groups=mesh['walkers'=8,'orb'=4] {'walkers'}, use_global_device_ids=true, to_apply=%region_14.15 | all-reduce | flops 1 | bytes 8 | tf_op jit(solution)/shard_map/psum | solution.py:193
  105.4 3.3 %all-to-all-start.1 = ((f32[4,2,32,128]{3,2,1,0:T(8,128)}), f32[4,2,32,128]{3,2,1,0:T(8,128)S(1)}, u32[]{:S(2)}, u32[]{:S(2)}) async-start(f32[4,2,32,128]{3,2,1,0:T(8,128)} %param.21), calls=%async_computation.1 | async-start | bytes 262144 | tf_op jit(solution)/shard_map/all_to_all | solution.py:168
  109.5 3.8 %all-to-all-done.1 = f32[4,2,32,128]{3,2,1,0:T(8,128)S(1)} async-done(((f32[4,2,32,128]{3,2,1,0:T(8,128)}), f32[4,2,32,128]{3,2,1,0:T(8,128)S(1)}, u32[]{:S(2)}, u32[]{:S(2)}) %all-to-all-start.1) | async-done | bytes 131104 | tf_op jit(solution)/shard_map/all_to_all | solution.py:168
  113.4 3.3 %all-to-all-start = ((f32[4,2,32,128]{3,2,1,0:T(8,128)}), f32[4,2,32,128]{3,2,1,0:T(8,128)S(1)}, u32[]{:S(2)}, u32[]{:S(2)}) async-start(f32[4,2,32,128]{3,2,1,0:T(8,128)} %param.20), calls=%async_computation | async-start | bytes 262144 | tf_op jit(solution)/shard_map/all_to_all | solution.py:167
  117.5 3.8 %all-to-all-done = f32[4,2,32,128]{3,2,1,0:T(8,128)S(1)} async-done(((f32[4,2,32,128]{3,2,1,0:T(8,128)}), f32[4,2,32,128]{3,2,1,0:T(8,128)S(1)}, u32[]{:S(2)}, u32[]{:S(2)}) %all-to-all-start) | async-done | bytes 131104 | tf_op jit(solution)/shard_map/all_to_all | solution.py:167
  123.2 21.5 %while.58 = (s32[]{:T(128)}, f32[1,2,32,160]{1,3,2,0:T(8,128)S(1)}, f32[1,2]{1,0:T(1,128)S(1)}, s32[]{:T(128)}, s32[]{:T(128)}, /*index=5*/s32[]{:T(128)}, s32[]{:T(128)}) while((s32[]{:T(128)}, f32[1,2,32,160]{1,3,2,0:T(8,128)S(1)}, f32[1,2]{1,0:T(1,128)S(1)}, s32[]{:T(128)}, s32[]{:T(128)}, /*index=5*/s32[]{:T(128)}, ...), condition=%wide.region_7.8_spmd.clone, body=%wide.region_6.7_spmd.clone.sunk | while | flops 31083 | bytes 86795 | solution.py:102
  147.1 6.1 %all_to_all.93 = f32[1,2,4,1]{1,3,0,2:T(1,128)S(1)} all-to-all(f32[1,2,4,1]{1,3,0,2:T(1,128)S(1)} %broadcast_in_dim.134), channel_id=1, replica_groups=mesh['walkers'=8,'orb'=4] {'orb'}, dimensions={2} | all-to-all | bytes 64 | tf_op jit(solution)/shard_map/all_to_all | solution.py:182
  153.2 3.3 %all-to-all-start.4 = ((f32[1,2,128,128]{3,1,0,2:T(2,128)}), f32[1,2,128,128]{3,1,0,2:T(2,128)S(1)}, u32[]{:S(2)}, u32[]{:S(2)}) async-start(f32[1,2,128,128]{3,1,0,2:T(2,128)} %copy.95), calls=%async_computation.4 | async-start | bytes 262144 | tf_op jit(solution)/shard_map/all_to_all | solution.py:181
  156.8 4.3 %all-to-all-done.4 = f32[1,2,128,128]{3,1,0,2:T(2,128)S(1)} async-done(((f32[1,2,128,128]{3,1,0,2:T(2,128)}), f32[1,2,128,128]{3,1,0,2:T(2,128)S(1)}, u32[]{:S(2)}, u32[]{:S(2)}) %all-to-all-start.4) | async-done | bytes 131104 | tf_op jit(solution)/shard_map/all_to_all | solution.py:181
  161.1 3.3 %all-to-all-start.3 = ((f32[1,2,128,128]{3,1,0,2:T(2,128)}), f32[1,2,128,128]{3,1,0,2:T(2,128)S(1)}, u32[]{:S(2)}, u32[]{:S(2)}) async-start(f32[1,2,128,128]{3,1,0,2:T(2,128)} %copy.92), calls=%async_computation.3 | async-start | bytes 262144 | tf_op jit(solution)/shard_map/all_to_all | solution.py:180
  165.9 4.5 %collective-permute-start.4 = (f32[4,2]{0,1:T(2,128)S(1)}, f32[4,2]{0,1:T(2,128)S(1)}, u32[]{:S(2)}, u32[]{:S(2)}) collective-permute-start(f32[4,2]{0,1:T(2,128)S(1)} %fusion.53), channel_id=1, source_target_pairs={{0,4},{4,8},{8,12},{12,16},{16,20},{20,24},{24,28},{1,5},{5,9},{9,... | collective-permute-start | bytes 104 | tf_op jit(solution)/shard_map/ppermute | solution.py:33
  172.8 4.6 %collective-permute-start = (f32[4,2,2,32,128]{4,0,3,2,1:T(4,128)S(1)}, f32[4,2,2,32,128]{4,0,3,2,1:T(4,128)S(1)}, u32[]{:S(2)}, u32[]{:S(2)}) collective-permute-start(f32[4,2,2,32,128]{4,0,3,2,1:T(4,128)S(1)} %fusion.26), channel_id=1, source_target_pairs={{0,4},{4,8},{8,12},{12,16},{16,20},{20,24},{24,28},{1,5},{5,9},{9,... | collective-permute-start | bytes 786440 | tf_op jit(solution)/shard_map/ppermute | solution.py:33
  178.0 3.5 %collective-permute-done.1 = f32[4,2,2,32,128]{4,0,3,2,1:T(4,128)S(1)} collective-permute-done((f32[4,2,2,32,128]{4,0,3,2,1:T(4,128)S(1)}, f32[4,2,2,32,128]{4,0,3,2,1:T(4,128)S(1)}, u32[]{:S(2)}, u32[]{:S(2)}) %collective-permute-start.1) | collective-permute-done | bytes 262176 | tf_op jit(solution)/shard_map/ppermute | solution.py:35
  181.5 4.9 %collective-permute-done = f32[4,2,2,32,128]{4,0,3,2,1:T(4,128)S(1)} collective-permute-done((f32[4,2,2,32,128]{4,0,3,2,1:T(4,128)S(1)}, f32[4,2,2,32,128]{4,0,3,2,1:T(4,128)S(1)}, u32[]{:S(2)}, u32[]{:S(2)}) %collective-permute-start) | collective-permute-done | bytes 262176 | tf_op jit(solution)/shard_map/ppermute | solution.py:33
  (326 shorter events, 74.0 us)
Async XLA Ops:
  1.3 30.2 %copy-start.1 = (s32[4,2,32]{2,1,0:T(2,128)S(1)}, s32[4,2,32]{2,1,0:T(2,128)}, u32[]{:S(2)}) copy-start(s32[4,2,32]{2,1,0:T(2,128)} %param.25) | copy-start | bytes 3076
  1.3 30.3 %copy-start.2 = (s32[4]{0:T(128)S(1)}, s32[4]{0:T(128)}, u32[]{:S(2)}) copy-start(s32[4]{0:T(128)} %param.26) | copy-start | bytes 52
  1.3 30.9 %copy-start.5 = (u32[32]{0:T(128)S(1)}, u32[32]{0:T(128)}, u32[]{:S(2)}) copy-start(u32[32]{0:T(128)} %constant.227) | copy-start | bytes 388
  1.3 45.3 %copy-start.4 = (s32[4,2,128]{2,1,0:T(2,128)S(1)}, s32[4,2,128]{2,1,0:T(2,128)}, u32[]{:S(2)}) copy-start(s32[4,2,128]{2,1,0:T(2,128)} %param.24) | copy-start | bytes 12292
  1.3 53.3 %copy-start = (f32[4]{0:T(128)S(1)}, f32[4]{0:T(128)}, u32[]{:S(2)}) copy-start(f32[4]{0:T(128)} %param.31) | copy-start | bytes 52
  27.4 78.0 %all-to-all-start.2 = ((f32[4,2,32,128]{3,2,1,0:T(8,128)}), f32[4,2,32,128]{3,2,1,0:T(8,128)S(1)}, u32[]{:S(2)}, u32[]{:S(2)}) async-start(f32[4,2,32,128]{3,2,1,0:T(8,128)} %get-tuple-element.317), calls=%async_computation.2 | async-start | bytes 262144 | tf_op jit(solution)/shard_map/all_to_all | solution.py:169
  47.9 60.9 %collective-permute-start.3 = (f32[4,3,256]{2,0,1:T(4,128)S(1)}, f32[4,3,256]{2,0,1:T(4,128)S(1)}, u32[]{:S(2)}, u32[]{:S(2)}) collective-permute-start(f32[4,3,256]{2,0,1:T(4,128)S(1)} %fusion.34), channel_id=1, source_target_pairs={{4,0},{8,4},{12,8},{16,12},{20,16},{24,20},{28,24},{5,1},{9,5},{13... | collective-permute-start | bytes 36872 | tf_op jit(solution)/shard_map/ppermute | solution.py:35
  49.3 59.5 %collective-permute-start.2 = (f32[4,3,256]{2,0,1:T(4,128)S(1)}, f32[4,3,256]{2,0,1:T(4,128)S(1)}, u32[]{:S(2)}, u32[]{:S(2)}) collective-permute-start(f32[4,3,256]{2,0,1:T(4,128)S(1)} %fusion.36), channel_id=1, source_target_pairs={{0,4},{4,8},{8,12},{12,16},{16,20},{20,24},{24,28},{1,5},{5,9},{9,... | collective-permute-start | bytes 36872 | tf_op jit(solution)/shard_map/ppermute | solution.py:33
  105.4 7.9 %all-to-all-start.1 = ((f32[4,2,32,128]{3,2,1,0:T(8,128)}), f32[4,2,32,128]{3,2,1,0:T(8,128)S(1)}, u32[]{:S(2)}, u32[]{:S(2)}) async-start(f32[4,2,32,128]{3,2,1,0:T(8,128)} %param.21), calls=%async_computation.1 | async-start | bytes 262144 | tf_op jit(solution)/shard_map/all_to_all | solution.py:168
  113.4 7.9 %all-to-all-start = ((f32[4,2,32,128]{3,2,1,0:T(8,128)}), f32[4,2,32,128]{3,2,1,0:T(8,128)S(1)}, u32[]{:S(2)}, u32[]{:S(2)}) async-start(f32[4,2,32,128]{3,2,1,0:T(8,128)} %param.20), calls=%async_computation | async-start | bytes 262144 | tf_op jit(solution)/shard_map/all_to_all | solution.py:167
  144.7 11.9 %copy-start.3 = (f32[4]{0:T(128)S(1)}, f32[4]{0:T(128)}, u32[]{:S(2)}) copy-start(f32[4]{0:T(128)} %param.27) | copy-start | bytes 52
  153.2 7.9 %all-to-all-start.4 = ((f32[1,2,128,128]{3,1,0,2:T(2,128)}), f32[1,2,128,128]{3,1,0,2:T(2,128)S(1)}, u32[]{:S(2)}, u32[]{:S(2)}) async-start(f32[1,2,128,128]{3,1,0,2:T(2,128)} %copy.95), calls=%async_computation.4 | async-start | bytes 262144 | tf_op jit(solution)/shard_map/all_to_all | solution.py:181
  161.1 9.4 %all-to-all-start.3 = ((f32[1,2,128,128]{3,1,0,2:T(2,128)}), f32[1,2,128,128]{3,1,0,2:T(2,128)S(1)}, u32[]{:S(2)}, u32[]{:S(2)}) async-start(f32[1,2,128,128]{3,1,0,2:T(2,128)} %copy.92), calls=%async_computation.3 | async-start | bytes 262144 | tf_op jit(solution)/shard_map/all_to_all | solution.py:180
  164.6 12.7 %collective-permute-start.5 = (f32[4,2]{0,1:T(2,128)S(1)}, f32[4,2]{0,1:T(2,128)S(1)}, u32[]{:S(2)}, u32[]{:S(2)}) collective-permute-start(f32[4,2]{0,1:T(2,128)S(1)} %fusion.54), channel_id=1, source_target_pairs={{4,0},{8,4},{12,8},{16,12},{20,16},{24,20},{28,24},{5,1},{9,5},{13... | collective-permute-start | bytes 104 | tf_op jit(solution)/shard_map/ppermute | solution.py:35
  165.9 11.4 %collective-permute-start.4 = (f32[4,2]{0,1:T(2,128)S(1)}, f32[4,2]{0,1:T(2,128)S(1)}, u32[]{:S(2)}, u32[]{:S(2)}) collective-permute-start(f32[4,2]{0,1:T(2,128)S(1)} %fusion.53), channel_id=1, source_target_pairs={{0,4},{4,8},{8,12},{12,16},{16,20},{20,24},{24,28},{1,5},{5,9},{9,... | collective-permute-start | bytes 104 | tf_op jit(solution)/shard_map/ppermute | solution.py:33
  171.5 10.0 %collective-permute-start.1 = (f32[4,2,2,32,128]{4,0,3,2,1:T(4,128)S(1)}, f32[4,2,2,32,128]{4,0,3,2,1:T(4,128)S(1)}, u32[]{:S(2)}, u32[]{:S(2)}) collective-permute-start(f32[4,2,2,32,128]{4,0,3,2,1:T(4,128)S(1)} %fusion.25), channel_id=1, source_target_pairs={{4,0},{8,4},{12,8},{16,12},{20,16},{24,20},{28,24},{5,1},{9,5},{13... | collective-permute-start | bytes 786440 | tf_op jit(solution)/shard_map/ppermute | solution.py:35
  172.8 13.6 %collective-permute-start = (f32[4,2,2,32,128]{4,0,3,2,1:T(4,128)S(1)}, f32[4,2,2,32,128]{4,0,3,2,1:T(4,128)S(1)}, u32[]{:S(2)}, u32[]{:S(2)}) collective-permute-start(f32[4,2,2,32,128]{4,0,3,2,1:T(4,128)S(1)} %fusion.26), channel_id=1, source_target_pairs={{0,4},{4,8},{8,12},{12,16},{16,20},{20,24},{24,28},{1,5},{5,9},{9,... | collective-permute-start | bytes 786440 | tf_op jit(solution)/shard_map/ppermute | solution.py:33
where the time goes:
time: 192 us; the launch traced here: 189 us
  other arithmetic  45.2 us (24%)
  blocking collectives  42 us (22%)
  starting transfers between devices  35.8 us (19%)
  local copies, waits for them, and re-layouts  26.3 us (14%)
  waiting for transfers between devices  20.3 us (11%)
  matrix products  14.7 us (8%)
  between operations  2.8 us (1%)
  loops' own time  2.08 us (1%)
    psum x1, blocking collectives, body(): energy_sum = lax.psum(weighted, 'walkers')  23.7 us
    select_n x32, other arithmetic, sweep(): matrix = jnp.where(mine, pivot_row, matrix - column_now * pivot_row)  16.8 us
    reduce_sum x4, other arithmetic, pair_terms(): soft = jnp.sum(1.0 / jnp.sqrt(new_squares + 1.0))  14.8 us
    ppermute x3, starting transfers between devices, with_halo(): lax.ppermute(tail, axis, [(i, (i + 1) % count) for i in range(ends)])  14.4 us
    unnamed x1, blocking collectives  12.2 us
    slice x12, local copies, waits for them, and re-layouts, basis_values(): offset = points[component][None, :] - centers[component][:, None]  6.32 us
    all_to_all x1, blocking collectives, body(): lax.all_to_all(logdet_tiled, 'orb', split_axis=2, concat_axis=0, tiled=True)  6.08 us
    dynamic_update_slice x8, local copies, waits for them, and re-layouts, body(): lax.map(walker_pairs, (positions, positions_now))  5.6 us
  transfers between devices with their start and end apart: 11, of which 5 were waited for; matrix products, arithmetic and copies ran while one was open for 18% of the time, Pallas kernels for 0%

commit v1 on v0

v1 whole, which is shorter than its diff:
```python
import jax
import jax.numpy as jnp
from jax import lax
from jax.experimental import pallas as pl
from jax.experimental.pallas import tpu as pltpu
from jax.sharding import PartitionSpec as P

F32 = jnp.float32
highest = lax.Precision.HIGHEST
VMEM = pl.BlockSpec(memory_space=pltpu.VMEM)
SMEM = pl.BlockSpec(memory_space=pltpu.SMEM)
LANES = 128
INFO = 8


def nn(a, b):
    return lax.dot_general(
        a, b, (((1,), (0,)), ((), ())), precision=highest, preferred_element_type=F32
    )


def nt(a, b):
    return lax.dot_general(
        a, b, (((1,), (1,)), ((), ())), precision=highest, preferred_element_type=F32
    )


def tn(a, b):
    return lax.dot_general(
        a, b, (((0,), (0,)), ((), ())), precision=highest, preferred_element_type=F32
    )


def turned(rows):
    short = -rows.shape[0] % 8
    if short:
        rows = jnp.concatenate([rows, jnp.zeros((short, rows.shape[1]), F32)], axis=0)
    return jnp.transpose(rows)


def moves_of(order_ref, flags_ref):
    walkers, _, moves = flags_ref.shape
    nel = order_ref.shape[2]
    order = turned(
        jnp.concatenate([order_ref[w] for w in range(walkers)], axis=0).astype(F32)
    )
    flags = jnp.concatenate([flags_ref[w] for w in range(walkers)], axis=0).astype(F32)
    flags = turned(
        jnp.concatenate([flags, jnp.zeros((2 * walkers, nel - moves), F32)], axis=1)
    )
    cols = [order[:moves, i : i + 1] for i in range(2 * walkers)]
    keep = [flags[:moves, i : i + 1] for i in range(2 * walkers)]
    return cols, keep


def one_hots(cols, nel):
    moves = cols[0].shape[0]
    lanes = lax.broadcasted_iota(jnp.int32, (moves, nel), 1).astype(F32)
    return [(c == lanes).astype(F32) for c in cols]


def pick(counts_ref, index):
    walkers = counts_ref.shape[0]
    total = jnp.int32(0)
    source = jnp.int32(0)
    for w in range(walkers):
        total = total + counts_ref[w]
        source = source + (total <= index).astype(jnp.int32)
    return jnp.minimum(source, walkers - 1)


def total_of(counts_ref):
    total = jnp.int32(0)
    for w in range(counts_ref.shape[0]):
        total = total + counts_ref[w]
    return total


def blocks_of(nel):
    return ((0, 0, 1.0), (nel, nel, 1.0), (0, nel, 2.0))


def squares_of(cols, rows, a, b, nel):
    total = None
    for c in range(3):
        offset = cols[c][a : a + nel] - rows[c][:, b : b + nel]
        total = offset * offset if total is None else total + offset * offset
    return total


def energy_kernel(pos_ref, dis_ref, order_ref, flags_ref, counts_ref, now_ref, energy_ref, info_ref):
    walkers, _, both = pos_ref.shape
    nel = both // 2
    cols, keep = moves_of(order_ref, flags_ref)
    hots = one_hots(cols, nel)
    weighted = jnp.zeros((1, 1), F32)
    for w in range(walkers):
        applied = [
            jnp.sum(hots[2 * w + s] * keep[2 * w + s], axis=0, keepdims=True) for s in (0, 1)
        ]
        now = pos_ref[w] + dis_ref[w] * jnp.concatenate(applied, axis=1)
        now_ref[w] = now
        turn = turned(jnp.concatenate([now, jnp.zeros((5, both), F32)], axis=0))
        ncols = [turn[:, c : c + 1] for c in range(3)]
        nrows = [now[c : c + 1] for c in range(3)]
        soft = jnp.zeros((8, nel), F32)
        for a, b, weight in blocks_of(nel):
            squares = squares_of(ncols, nrows, a, b, nel)
            terms = lax.rsqrt(squares + 1.0)
            part = jnp.sum(terms.reshape(nel // 8, 8, nel), axis=0)
            soft = soft + (part if weight == 1.0 else part * weight)
        whole = jnp.sum(jnp.sum(soft, axis=0, keepdims=True), axis=1, keepdims=True)
        energy = (whole - 1.0 * both) / (1.0 * both * (both - 1))
        energy_ref[w : w + 1, :] = jnp.broadcast_to(energy, (1, energy_ref.shape[1]))
        weighted = weighted + energy * counts_ref[w].astype(F32)
    me = lax.axis_index("walkers")
    lanes = lax.broadcasted_iota(jnp.int32, info_ref.shape, 1)
    rows = lax.broadcasted_iota(jnp.int32, info_ref.shape, 0)
    number = total_of(counts_ref).astype(F32)
    info_ref[...] = jnp.where(
        lanes == me,
        jnp.where(rows == 0, number, jnp.where(rows == 1, weighted, 0.0)),
        0.0,
    )


def jastrow_kernel(pos_ref, now_ref, jas_ref, out_ref):
    walkers, _, both = pos_ref.shape
    nel = both // 2
    for w in range(walkers):
        old = pos_ref[w]
        new = now_ref[w]
        turn = turned(jnp.concatenate([old, new, jnp.zeros((2, both), F32)], axis=0))
        ocols = [turn[:, c : c + 1] for c in range(3)]
        ncols = [turn[:, 3 + c : 4 + c] for c in range(3)]
        orows = [old[c : c + 1] for c in range(3)]
        nrows = [new[c : c + 1] for c in range(3)]
        total = jnp.zeros((8, nel), F32)
        for a, b, weight in blocks_of(nel):
            kind = 0 if a == b else 1
            fall = jas_ref[2 + kind]
            osq = squares_of(ocols, orows, a, b, nel)
            nsq = squares_of(ncols, nrows, a, b, nel)
            od = jnp.sqrt(osq)
            nd = jnp.sqrt(nsq)
            terms = (nd - od) / ((1.0 + fall * nd) * (1.0 + fall * od))
            part = jnp.sum(terms.reshape(nel // 8, 8, nel), axis=0)
            total = total + part * (jas_ref[kind] * weight)
        whole = jnp.sum(jnp.sum(total, axis=0, keepdims=True), axis=1, keepdims=True)
        out_ref[w : w + 1, :] = jnp.broadcast_to(0.5 * whole, (1, out_ref.shape[1]))


def partial_kernel(
    pos_ref, dis_ref, order_ref, flags_ref, counts_ref, cen_ref, exp_ref, orb_ref, inv_ref,
    sla_ref, now_ref, energy_ref, part_ref, done_ref, pair_ref, odd_ref, differ_ref,
):
    walkers, _, both = pos_ref.shape
    nel = both // 2
    moves = flags_ref.shape[2]
    basis = cen_ref.shape[1]
    orbs = inv_ref.shape[2]
    cols, keep = moves_of(order_ref, flags_ref)
    hots = one_hots(cols, nel)
    for s in (0, 1):
        table = jnp.concatenate(
            [
                jnp.concatenate(
                    [
                        pos_ref[w, :, s * nel : (s + 1) * nel],
                        dis_ref[w, :, s * nel : (s + 1) * nel],
                        jnp.zeros((2, nel), F32),
                    ],
                    axis=0,
                )
                for w in range(walkers)
            ],
            axis=0,
        )
        points = nt(jnp.concatenate([hots[2 * w + s] for w in range(walkers)], axis=0), table)
        for w in range(walkers):
            mine = points[w * moves : (w + 1) * moves]
            old = [
                jnp.broadcast_to(mine[:, 8 * w + c : 8 * w + c + 1], (moves, LANES))
                for c in range(3)
            ]
            new = [
                jnp.broadcast_to(
                    mine[:, 8 * w + c : 8 * w + c + 1] + mine[:, 8 * w + 3 + c : 8 * w + 4 + c],
                    (moves, LANES),
                )
                for c in range(3)
            ]
            for j in range(0, basis, LANES):
                osq = None
                nsq = None
                for c in range(3):
                    row = cen_ref[c : c + 1, j : j + LANES]
                    do = old[c] - row
                    dn = new[c] - row
                    osq = do * do if osq is None else osq + do * do
                    nsq = dn * dn if nsq is None else nsq + dn * dn
                rate = -exp_ref[:, j : j + LANES]
                differ_ref[s, w * moves : (w + 1) * moves, j : j + LANES] = jnp.exp(
                    rate * nsq
                ) - jnp.exp(rate * osq)
    for s in (0, 1):
        shift = nt(differ_ref[s], orb_ref[s])
        for w in range(walkers):
            i = 2 * w + s
            mine = shift[w * moves : (w + 1) * moves]
            proposed = mine + nt(hots[i], sla_ref[w, s])
            part = nn(proposed, inv_ref[w, s])
            part_ref[i * moves : (i + 1) * moves, :] = part * keep[i]
            done_ref[w, s] = sla_ref[w, s] + tn(mine, hots[i] * keep[i])
    half = walkers // 2
    per = 2 * orbs
    tail = half * per
    width = both // LANES
    parity = lax.rem(lax.axis_index("walkers"), 2)
    number = total_of(counts_ref)
    for pay, goes_up in ((pair_ref, parity == 0), (odd_ref, parity == 1)):
        pay[tail:, :] = jnp.zeros((pay.shape[0] - tail, LANES), F32)
        for j in range(half):
            index = jnp.where(goes_up, number - half + j, j)
            source = pick(counts_ref, index)
            for s in (0, 1):
                pay[j * per + s * orbs : j * per + (s + 1) * orbs, :] = done_ref[source, s]
            spot = now_ref[source]
            for h in range(width):
                at = tail + (j * width + h) * 3
                pay[at : at + 3, :] = spot[:, h * LANES : (h + 1) * LANES]
            at = tail + half * width * 3 + j
            pay[at : at + 1, :] = energy_ref[pl.ds(source, 1), :]


def add_kernel(mine_ref, other_ref, info_ref, info_other_ref, out_ref):
    rows = mine_ref.shape[0]
    out_ref[:rows, :] = mine_ref[...] + other_ref[...]
    out_ref[rows:, :] = info_ref[...] + info_other_ref[...]


def update_kernel(
    sum_ref, got_ref, inv_ref, order_ref, flags_ref, counts_ref, amp_ref, jas_ref,
    cur_ref, log_ref, info_ref, pair_ref, odd_ref,
):
    walkers, _, orbs, nel = inv_ref.shape
    moves = flags_ref.shape[2]
    count = 2 * walkers
    cols, keep = moves_of(order_ref, flags_ref)
    hots = one_hots(cols, nel)
    eye = (
        lax.broadcasted_iota(jnp.int32, (moves, moves), 0)
        == lax.broadcasted_iota(jnp.int32, (moves, moves), 1)
    ).astype(F32)
    tiles = moves // 8
    left = []
    right = []
    columns = []
    for i in range(count):
        at = slice(i * moves, (i + 1) * moves)
        change = sum_ref[at, :] + got_ref[at, :] - hots[i] * keep[i]
        coupling = nt(change, hots[i]) + eye
        columns.append(nt(inv_ref[i // 2, i % 2], hots[i]))
        left.append([coupling[8 * t : 8 * t + 8] for t in range(tiles)])
        right.append([change[8 * t : 8 * t + 8] for t in range(tiles)])
    info_ref[...] = sum_ref[count * moves :, :] + got_ref[count * moves :, :]
    lanes = lax.broadcasted_iota(jnp.int32, (1, nel), 1)
    sub = lax.broadcasted_iota(jnp.int32, (8, nel), 0)
    pivots = [jnp.ones((1, nel), F32) for _ in range(count)]
    for k in range(moves):
        own, line = k // 8, k % 8
        for i in range(count):
            wide = [
                jnp.broadcast_to(left[i][t][:, k : k + 1], (8, nel)) for t in range(tiles)
            ]
            pivot = wide[own][line : line + 1]
            pivots[i] = jnp.where(lanes == k, pivot, pivots[i])
            scale = 1.0 / pivot
            lrow = left[i][own][line : line + 1] * scale[:, :moves]
            rrow = right[i][own][line : line + 1] * scale
            for t in range(tiles):
                nl = left[i][t] - wide[t][:, :moves] * lrow
                nr = right[i][t] - wide[t] * rrow
                if t == own:
                    nl = jnp.where(sub[:, :moves] == line, lrow, nl)
                    nr = jnp.where(sub == line, rrow, nr)
                left[i][t] = nl
                right[i][t] = nr
    for i in range(count):
        solved = jnp.concatenate(right[i], axis=0)
        cur_ref[i // 2, i % 2] = inv_ref[i // 2, i % 2] - nn(columns[i], solved)
    log_ref[...] = jnp.zeros(log_ref.shape, F32)
    for w in range(walkers):
        both = jnp.log(jnp.abs(pivots[2 * w])) + jnp.log(jnp.abs(pivots[2 * w + 1]))
        log_ref[w : w + 1, :] = (
            jnp.broadcast_to(jnp.sum(both, axis=1, keepdims=True), (1, nel))
            + jas_ref[w : w + 1, :]
            + amp_ref[w]
        )
    half = walkers // 2
    per = 2 * orbs
    tail = half * per
    parity = lax.rem(lax.axis_index("walkers"), 2)
    number = total_of(counts_ref)
    for pay, goes_up in ((pair_ref, parity == 0), (odd_ref, parity == 1)):
        pay[tail : tail + INFO, :] = info_ref[...]
        pay[tail + INFO :, :] = jnp.zeros((pay.shape[0] - tail - INFO, LANES), F32)
        for j in range(half):
            index = jnp.where(goes_up, number - half + j, j)
            source = pick(counts_ref, index)
            for s in (0, 1):
                pay[j * per + s * orbs : j * per + (s + 1) * orbs, :] = cur_ref[source, s]
            at = tail + INFO + j
            pay[at : at + 1, :] = log_ref[pl.ds(source, 1), :]


def place_kernel(
    counts_ref, cur_ref, done_ref, now_ref, energy_ref, log_ref, info_ref,
    pair_s_ref, odd_s_ref, pair_i_ref, odd_i_ref,
    inv_out, sla_out, pos_out, log_out, energy_out, mean_out,
):
    walkers, _, orbs, nel = cur_ref.shape
    both = now_ref.shape[2]
    width = both // LANES
    half = walkers // 2
    per = 2 * orbs
    tail = half * per
    me = lax.axis_index("walkers")
    parity = lax.rem(me, 2)
    info = info_ref[...] + pair_i_ref[tail : tail + INFO, :]
    lanes = lax.broadcasted_iota(jnp.int32, (1, info.shape[1]), 1)
    before = jnp.sum(jnp.where(lanes < me, info[0:1], 0.0)).astype(jnp.int32)
    groups = lax.axis_size("walkers")
    mean = jnp.sum(info[1:2], axis=1, keepdims=True)
    mean_out[...] = mean / (1.0 * walkers * groups)
    number = total_of(counts_ref)
    spots = lax.broadcasted_iota(jnp.int32, (1, walkers), 1)

    def put(j, inverse, slater, spot, log, energy):
        for s in (0, 1):
            inv_out[j, s] = inverse(s)
            sla_out[j, s] = slater(s)
        for h in range(width):
            pos_out[j, :, h * LANES : (h + 1) * LANES] = spot(h)
        log_out[...] = jnp.where(spots == j, log[:, :walkers], log_out[...])
        energy_out[...] = jnp.where(spots == j, energy[:, :walkers], energy_out[...])

    log_out[...] = jnp.zeros(log_out.shape, F32)
    energy_out[...] = jnp.zeros(energy_out.shape, F32)
    for j in range(walkers):
        index = me * walkers + j - before
        low = index < 0
        high = index >= number

        @pl.when(jnp.logical_not(low | high))
        def _():
            w = pick(counts_ref, index)
            put(
                j,
                lambda s: cur_ref[w, s],
                lambda s: done_ref[w, s],
                lambda h: now_ref[w, :, h * LANES : (h + 1) * LANES],
                log_ref[pl.ds(w, 1), :],
                energy_ref[pl.ds(w, 1), :],
            )

        def received(late, early):
            i = jnp.clip(jnp.where(low, index + half, index - number), 0, half - 1)
            put(
                j,
                lambda s: late[pl.ds(i * per + s * orbs, orbs), :],
                lambda s: early[pl.ds(i * per + s * orbs, orbs), :],
                lambda h: early[pl.ds(tail + (i * width + h) * 3, 3), :],
                late[pl.ds(tail + INFO + i, 1), :],
                early[pl.ds(tail + half * width * 3 + i, 1), :],
            )

        on_pair = (low & (parity == 1)) | (high & (parity == 0))

        @pl.when(on_pair)
        def _():
            received(pair_i_ref, pair_s_ref)

        @pl.when((low | high) & jnp.logical_not(on_pair))
        def _():
            received(odd_i_ref, odd_s_ref)


def call(kernel, outs, in_specs, scratch=(), flops=0, name=None):
    return pl.pallas_call(
        kernel,
        out_shape=outs,
        in_specs=in_specs,
        out_specs=jax.tree.map(lambda _: VMEM, outs),
        scratch_shapes=list(scratch),
        compiler_params=pltpu.CompilerParams(vmem_limit_bytes=32 * 2**20),
        cost_estimate=pl.CostEstimate(flops=flops, bytes_accessed=2**18, transcendentals=0),
        name=name,
    )


def shape(*dims):
    return jax.ShapeDtypeStruct(dims, F32)


def body(
    inverse, slater, positions, displacements, move_order, accepted, counts, log_amp, centers,
    exponents, orbitals, jastrow,
):
    walkers, _, orbs, nel = inverse.shape
    moves = accepted.shape[2]
    both = positions.shape[2]
    basis = centers.shape[1]
    groups = lax.axis_size("walkers")
    members = lax.axis_size("orb")
    wide = max(LANES, groups)
    half = walkers // 2
    per = 2 * orbs
    count = 2 * walkers
    tall = half * per + 16

    pairs = [(i, i ^ 1) for i in range(groups)]
    odds = [(i, i + 1) for i in range(1, groups - 1, 2)]
    odds = odds + [(b, a) for a, b in odds]

    now, energy, info = call(
        energy_kernel,
        (shape(walkers, 3, both), shape(walkers, LANES), shape(INFO, wide)),
        [VMEM, VMEM, VMEM, VMEM, SMEM],
        flops=10**6,
        name="energy",
    )(positions, displacements, move_order, accepted, counts)

    hops = members * 2
    step = hops
    while step < groups:
        info = info + lax.ppermute(info, "walkers", [(i, i ^ step) for i in range(groups)])
        step *= 2
    joint = [
        (d * members + o, (d ^ (2 * o)) * members + o)
        for d in range(groups)
        for o in range(members)
        if 2 * o < groups
    ]
    info = lax.ppermute(info, ("walkers", "orb"), joint)

    part, done, pair_s, odd_s = call(
        partial_kernel,
        (
            shape(count * moves, nel),
            shape(walkers, 2, orbs, nel),
            shape(tall, LANES),
            shape(tall, LANES),
        ),
        [VMEM, VMEM, VMEM, VMEM, SMEM] + [VMEM] * 7,
        scratch=[pltpu.VMEM((2, walkers * moves, basis), F32)],
        flops=10**6,
        name="partial",
    )(
        positions, displacements, move_order, accepted, counts, centers,
        exponents.reshape(1, basis), orbitals, inverse, slater, now, energy,
    )

    total = part
    step = 1
    while step < members:
        partner = [(o, o ^ step) for o in range(members)]
        if step == 1:
            other = lax.ppermute(part, "orb", partner)
            info_other = lax.ppermute(info, "orb", partner)
            total = call(
                add_kernel,
                shape(count * moves + INFO, nel),
                [VMEM] * 4,
                flops=10**5,
                name="add",
            )(part, other, info, info_other)
        else:
            got = lax.ppermute(total, "orb", partner)
        step *= 2

    change = call(
        jastrow_kernel, shape(walkers, LANES), [VMEM, VMEM, SMEM], flops=10**6, name="jastrow"
    )(positions, now, jastrow)

    pair_s = lax.ppermute(pair_s, "walkers", pairs)
    odd_s = lax.ppermute(odd_s, "walkers", odds)

    current, logs, info, pair_i, odd_i = call(
        update_kernel,
        (
            shape(walkers, 2, orbs, nel),
            shape(8, nel),
            shape(INFO, wide),
            shape(tall, LANES),
            shape(tall, LANES),
        ),
        [VMEM] * 5 + [SMEM, SMEM, VMEM],
        flops=10**6,
        name="update",
    )(total, got, inverse, move_order, accepted, counts, log_amp, change)

    pair_i = lax.ppermute(pair_i, "walkers", pairs)
    odd_i = lax.ppermute(odd_i, "walkers", odds)

    inv_new, sla_new, pos_new, log_new, energy_new, mean = call(
        place_kernel,
        (
            shape(walkers, 2, orbs, nel),
            shape(walkers, 2, orbs, nel),
            shape(walkers, 3, both),
            shape(1, walkers),
            shape(1, walkers),
            shape(1, 1),
        ),
        [SMEM] + [VMEM] * 10,
        flops=10**5,
        name="place",
    )(counts, current, done, now, energy, logs, info, pair_s, odd_s, pair_i, odd_i)
    return (
        inv_new,
        sla_new,
        pos_new,
        log_new.reshape(walkers),
        energy_new.reshape(walkers),
        mean.reshape(()),
    )


def solution(mesh):
    return jax.shard_map(
        body,
        mesh=mesh,
        in_specs=(
            P("walkers", None, "orb", None),
            P("walkers", None, "orb", None),
            P("walkers", None, None),
            P("walkers", None, None),
            P("walkers", None, None),
            P("walkers", None, None),
            P("walkers"),
            P("walkers"),
            P(),
            P(),
            P(None, "orb", None),
            P(),
        ),
        out_specs=(
            P("walkers", None, "orb", None),
            P("walkers", None, "orb", None),
            P("walkers", None, None),
            P("walkers"),
            P("walkers"),
            P(),
        ),
        check_vma=False,
    )
```

time: 192 us -> 45.2 us (0.24)
  the two profiles are of different devices: /device:TPU:0 before, /device:TPU:8 now
where the time goes in v1:
time: 45.2 us; the launch traced here: 44.8 us
  starting transfers between devices  17 us (38%)
  Pallas kernels  15.5 us (34%)
  waiting for transfers between devices  6.03 us (13%)
  local copies, waits for them, and re-layouts  5.46 us (12%)
  between operations  0.78 us (2%)
    unnamed x27, local copies, waits for them, and re-layouts  5.46 us
    pallas_call x1, Pallas kernels, body(): call(partial_kernel, (shape(count * moves, nel), shape(walkers, 2, orbs,...  5 us
    ppermute x1, waiting for transfers between devices, body(): odd_i = lax.ppermute(odd_i, 'walkers', odds)  4.8 us
    pallas_call x1, Pallas kernels, body(): call(update_kernel, (shape(walkers, 2, orbs, nel), shape(8, nel), shape(I...  4.42 us
    ppermute x1, starting transfers between devices, body(): info_other = lax.ppermute(info, 'orb', partner)  4.15 us
    ppermute x1, starting transfers between devices, body(): got = lax.ppermute(total, 'orb', partner)  3.47 us
    ppermute x1, starting transfers between devices, body(): pair_i = lax.ppermute(pair_i, 'walkers', pairs)  2.71 us
    ppermute x1, starting transfers between devices, body(): odd_s = lax.ppermute(odd_s, 'walkers', odds)  2.42 us
  transfers between devices with their start and end apart: 8, of which 3 were waited for; matrix products, arithmetic and copies ran while one was open for 0% of the time, Pallas kernels for 15%

profile of v1, /device:TPU:8, one launch (start us, length us, event | category | flops | bytes accessed | tf_op | source)
XLA Modules:
  0.0 44.8 jit_solution(7603839424798248221)
XLA Ops:
  0.6 0.7 %copy.20.pos_ref = f32[4,3,256]{2,1,0:T(4,128)S(1)} copy(f32[4,3,256]{2,0,1:T(4,128)} %param.14) | data formatting | bytes 24576 | tf_op args[2]
  1.4 0.6 %copy-done.4 = s32[4,2,128]{2,1,0:T(2,128)S(1)} copy-done((s32[4,2,128]{2,1,0:T(2,128)S(1)}, s32[4,2,128]{2,1,0:T(2,128)}, u32[]{:S(2)}) %copy-start.4) | copy-done | bytes 4120
  2.1 0.0 copy-done.5
  2.1 2.3 %energy.1 = (f32[4,3,256]{2,1,0:T(4,128)S(1)}, f32[4,128]{1,0:T(4,128)S(1)}, f32[8,128]{1,0:T(8,128)S(1)}) custom-call(f32[4,3,256]{2,1,0:T(4,128)S(1)} %copy.20.pos_ref, f32[4,3,256]{2,1,0:T(4,128)S(1)} %copy.21.dis_ref, s32[4,2,128]{2,1,0:T(2,128)S(1)} %copy-done.4, s32[4,2,32]{2,1,0:T(2,128)S(1)} %copy-done.5, s32[4]{0:T(128)S(1)} %copy-done.7), custom_call_target="tpu_custom_call" | custom-call | flops 1000000 | bytes 262144 | tf_op jit(solution)/shard_map/energy/pallas_call | solution.py:426
  4.4 0.7 %copy-done.8 = f32[1024]{0:T(1024)S(1)} copy-done((f32[1024]{0:T(1024)S(1)}, f32[1024]{0:T(1024)}, u32[]{:S(2)}) %copy-start.8) | copy-done | bytes 4120
  5.1 0.9 %copy-done = f32[4,2,32,128]{3,2,1,0:T(8,128)S(1)} copy-done((f32[4,2,32,128]{3,2,1,0:T(8,128)S(1)}, f32[4,2,32,128]{3,2,1,0:T(8,128)}, u32[]{:S(2)}) %copy-start) | copy-done | bytes 131096
  6.0 0.9 %copy-done.2 = f32[2,32,1024]{2,1,0:T(8,128)S(1)} copy-done((f32[2,32,1024]{2,1,0:T(8,128)S(1)}, f32[2,32,1024]{2,1,0:T(8,128)}, u32[]{:S(2)}) %copy-start.2) | copy-done | bytes 262168
  7.0 0.9 %copy-done.3 = f32[4,2,32,128]{3,2,1,0:T(8,128)S(1)} copy-done((f32[4,2,32,128]{3,2,1,0:T(8,128)S(1)}, f32[4,2,32,128]{3,2,1,0:T(8,128)}, u32[]{:S(2)}) %copy-start.3) | copy-done | bytes 131096
  7.9 5.0 %partial.1 = (f32[256,128]{1,0:T(8,128)S(1)}, f32[4,2,32,128]{3,2,1,0:T(8,128)S(1)}, f32[144,128]{1,0:T(8,128)S(1)}, f32[144,128]{1,0:T(8,128)S(1)}) custom-call(f32[4,3,256]{2,1,0:T(4,128)S(1)} %copy.20.pos_ref, f32[4,3,256]{2,1,0:T(4,128)S(1)} %copy.21.dis_ref, s32[4,2,128]{2,1,0:T(2,128)S(1)} %copy-done.4, s32[4,2,32]{2,1,0:T(2,128)S(1)} %copy-done.5, ...), custom_call_target="tpu_custom_call" | custom-call | flops 1000000 | bytes 262144 | tf_op jit(solution)/shard_map/partial/pallas_call | solution.py:447
  12.9 0.1 collective-permute-start
  12.9 0.8 %collective-permute-start.1 = (f32[8,128]{1,0:T(8,128)S(1)}, f32[8,128]{1,0:T(8,128)S(1)}, u32[]{:S(2)}, u32[]{:S(2)}) collective-permute-start(f32[8,128]{1,0:T(8,128)S(1)} %get-tuple-element.27), channel_id=1, source_target_pairs={{0,0},{1,9},{2,18},{3,27},{4,4},{5,13},{6,22},{7,31},{8,8},{9,1},{... | collective-permute-start | bytes 12296 | tf_op jit(solution)/shard_map/ppermute | solution.py:445
  13.8 4.1 %collective-permute-start.2 = (f32[8,128]{1,0:T(8,128)S(1)}, f32[8,128]{1,0:T(8,128)S(1)}, u32[]{:S(2)}, u32[]{:S(2)}) collective-permute-start(f32[8,128]{1,0:T(8,128)S(1)} %collective-permute-done.1.info_ref), channel_id=1, source_target_pairs={{0,1},{1,0},{2,3},{3,2},{4,5},{5,4},{6,7},{7,6},{8,9},{9,8},{10,11... | collective-permute-start | bytes 12296 | tf_op jit(solution)/shard_map/ppermute | solution.py:470
  17.9 0.8 %collective-permute-done.2.info_other_ref = f32[8,128]{1,0:T(8,128)S(1)} collective-permute-done((f32[8,128]{1,0:T(8,128)S(1)}, f32[8,128]{1,0:T(8,128)S(1)}, u32[]{:S(2)}, u32[]{:S(2)}) %collective-permute-start.2) | collective-permute-done | bytes 4128 | tf_op jit(solution)/shard_map/ppermute | solution.py:470
  18.8 3.5 %collective-permute-start.3 = (f32[264,128]{1,0:T(8,128)S(1)}, f32[264,128]{1,0:T(8,128)S(1)}, u32[]{:S(2)}, u32[]{:S(2)}) collective-permute-start(f32[264,128]{1,0:T(8,128)S(1)} %add.1.sum_ref), channel_id=1, source_target_pairs={{0,2},{1,3},{2,0},{3,1},{4,6},{5,7},{6,4},{7,5},{8,10},{9,11},{10,... | collective-permute-start | bytes 405512 | tf_op jit(solution)/shard_map/ppermute | solution.py:479
  22.2 1.5 %collective-permute-start.4 = (f32[144,128]{1,0:T(8,128)S(1)}, f32[144,128]{1,0:T(8,128)S(1)}, u32[]{:S(2)}, u32[]{:S(2)}) collective-permute-start(f32[144,128]{1,0:T(8,128)S(1)} %get-tuple-element.32), channel_id=1, source_target_pairs={{0,4},{4,0},{8,12},{12,8},{16,20},{20,16},{24,28},{28,24},{1,5},{5... | collective-permute-start | bytes 221192 | tf_op jit(solution)/shard_map/ppermute | solution.py:486
  23.8 2.4 %collective-permute-start.5 = (f32[144,128]{1,0:T(8,128)S(1)}, f32[144,128]{1,0:T(8,128)S(1)}, u32[]{:S(2)}, u32[]{:S(2)}) collective-permute-start(f32[144,128]{1,0:T(8,128)S(1)} %get-tuple-element.33), channel_id=1, source_target_pairs={{4,8},{12,16},{20,24},{8,4},{16,12},{24,20},{5,9},{13,17},{21,25},... | collective-permute-start | bytes 221192 | tf_op jit(solution)/shard_map/ppermute | solution.py:487
  26.2 2.2 %jastrow.1.jas_ref = f32[4,128]{1,0:T(4,128)S(1)} custom-call(f32[4,3,256]{2,1,0:T(4,128)S(1)} %copy.20.pos_ref, f32[4,3,256]{2,1,0:T(4,128)S(1)} %get-tuple-element.24.now_ref, f32[4]{0:T(128)S(1)} %copy-done.9), custom_call_target="tpu_custom_call" | custom-call | flops 1000000 | bytes 262144 | tf_op jit(solution)/shard_map/jastrow/pallas_call | solution.py:482
  28.4 4.4 %update.1 = (f32[4,2,32,128]{3,2,1,0:T(8,128)S(1)}, f32[8,128]{1,0:T(8,128)S(1)}, f32[8,128]{1,0:T(8,128)S(1)}, f32[144,128]{1,0:T(8,128)S(1)}, f32[144,128]{1,0:T(8,128)S(1)}) custom-call(f32[264,128]{1,0:T(8,128)S(1)} %add.1.sum_ref, f32[264,128]{1,0:T(8,128)S(1)} %collective-permute-done.3.got_ref, f32[4,2,32,128]{3,2,1,0:T(8,128)S(1)} %copy-done.1, ...), custom_call_target="tpu_custom_call" | custom-call | flops 1000000 | bytes 262144 | tf_op jit(solution)/shard_map/update/pallas_call | solution.py:489
  32.8 2.7 %collective-permute-start.6 = (f32[144,128]{1,0:T(8,128)S(1)}, f32[144,128]{1,0:T(8,128)S(1)}, u32[]{:S(2)}, u32[]{:S(2)}) collective-permute-start(f32[144,128]{1,0:T(8,128)S(1)} %get-tuple-element.34), channel_id=1, source_target_pairs={{0,4},{4,0},{8,12},{12,8},{16,20},{20,16},{24,28},{28,24},{1,5},{5... | collective-permute-start | bytes 221192 | tf_op jit(solution)/shard_map/ppermute | solution.py:503
  35.6 1.9 %collective-permute-start.7 = (f32[144,128]{1,0:T(8,128)S(1)}, f32[144,128]{1,0:T(8,128)S(1)}, u32[]{:S(2)}, u32[]{:S(2)}) collective-permute-start(f32[144,128]{1,0:T(8,128)S(1)} %get-tuple-element.35), channel_id=1, source_target_pairs={{4,8},{12,16},{20,24},{8,4},{16,12},{24,20},{5,9},{13,17},{21,25},... | collective-permute-start | bytes 221192 | tf_op jit(solution)/shard_map/ppermute | solution.py:504
  37.5 0.4 collective-permute-done.6.pair_i_ref
  37.9 4.8 %collective-permute-done.7.odd_i_ref = f32[144,128]{1,0:T(8,128)S(1)} collective-permute-done((f32[144,128]{1,0:T(8,128)S(1)}, f32[144,128]{1,0:T(8,128)S(1)}, u32[]{:S(2)}, u32[]{:S(2)}) %collective-permute-start.7) | collective-permute-done | bytes 73760 | tf_op jit(solution)/shard_map/ppermute | solution.py:504
  42.7 1.5 %place.1 = (f32[4,2,32,128]{3,2,1,0:T(8,128)}, f32[4,2,32,128]{3,2,1,0:T(8,128)}, f32[4,3,256]{2,1,0:T(4,128)S(1)}, f32[1,4]{1,0:T(1,128)}, f32[1,4]{1,0:T(1,128)}, /*index=5*/f32[1,1]{1,0:T(1,128)}) custom-call(s32[4]{0:T(128)S(1)} %copy-done.7, f32[4,2,32,128]{3,2,1,0:T(8,128)S(1)} %get-tuple-element.28.cur_ref, ...), custom_call_target="tpu_custom_call" | custom-call | flops 100000 | bytes 262144 | tf_op jit(solution)/shard_map/place/pallas_call | solution.py:506
  44.2 0.6 %copy.23 = f32[4,3,256]{2,0,1:T(4,128)} copy(f32[4,3,256]{2,1,0:T(4,128)S(1)} %get-tuple-element.44) | data formatting | bytes 24576
  (25 shorter events, 0.1 us)
Async XLA Ops:
  0.6 0.7 %copy-start.11 = (f32[4,3,256]{2,0,1:T(4,128)S(1)}, f32[4,3,256]{2,0,1:T(4,128)}, u32[]{:S(2)}) copy-start(f32[4,3,256]{2,0,1:T(4,128)} %param.15) | copy-start | bytes 36868
  1.4 0.7 %copy-start.4 = (s32[4,2,128]{2,1,0:T(2,128)S(1)}, s32[4,2,128]{2,1,0:T(2,128)}, u32[]{:S(2)}) copy-start(s32[4,2,128]{2,1,0:T(2,128)} %order_ref.5) | copy-start | bytes 12292
  1.4 0.7 %copy-start.5 = (s32[4,2,32]{2,1,0:T(2,128)S(1)}, s32[4,2,32]{2,1,0:T(2,128)}, u32[]{:S(2)}) copy-start(s32[4,2,32]{2,1,0:T(2,128)} %flags_ref.5) | copy-start | bytes 3076
  1.4 0.7 %copy-start.7 = (s32[4]{0:T(128)S(1)}, s32[4]{0:T(128)}, u32[]{:S(2)}) copy-start(s32[4]{0:T(128)} %counts_ref.7) | copy-start | bytes 52
  2.1 2.3 %copy-start.6 = (f32[3,1024]{1,0:T(4,128)S(1)}, f32[3,1024]{1,0:T(4,128)}, u32[]{:S(2)}) copy-start(f32[3,1024]{1,0:T(4,128)} %cen_ref.1) | copy-start | bytes 36868
  4.4 0.7 %copy-start.8 = (f32[1024]{0:T(1024)S(1)}, f32[1024]{0:T(1024)}, u32[]{:S(2)}) copy-start(f32[1024]{0:T(1024)} %param.21) | copy-start | bytes 12292
  5.1 0.9 %copy-start = (f32[4,2,32,128]{3,2,1,0:T(8,128)S(1)}, f32[4,2,32,128]{3,2,1,0:T(8,128)}, u32[]{:S(2)}) copy-start(f32[4,2,32,128]{3,2,1,0:T(8,128)} %inv_ref.3) | copy-start | bytes 393220
  6.0 0.9 %copy-start.2 = (f32[2,32,1024]{2,1,0:T(8,128)S(1)}, f32[2,32,1024]{2,1,0:T(8,128)}, u32[]{:S(2)}) copy-start(f32[2,32,1024]{2,1,0:T(8,128)} %orb_ref.1) | copy-start | bytes 786436
  6.9 0.9 %copy-start.3 = (f32[4,2,32,128]{3,2,1,0:T(8,128)S(1)}, f32[4,2,32,128]{3,2,1,0:T(8,128)}, u32[]{:S(2)}) copy-start(f32[4,2,32,128]{3,2,1,0:T(8,128)} %sla_ref.1) | copy-start | bytes 393220
  12.9 5.9 %collective-permute-start = (f32[256,128]{1,0:T(8,128)S(1)}, f32[256,128]{1,0:T(8,128)S(1)}, u32[]{:S(2)}, u32[]{:S(2)}) collective-permute-start(f32[256,128]{1,0:T(8,128)S(1)} %get-tuple-element.26.mine_ref), channel_id=1, source_target_pairs={{0,1},{1,0},{2,3},{3,2},{4,5},{5,4},{6,7},{7,6},{8,9},{9,8},{10,11... | collective-permute-start | bytes 393224 | tf_op jit(solution)/shard_map/ppermute | solution.py:469
  12.9 15.5 %copy-start.1 = (f32[4,2,32,128]{3,2,1,0:T(8,128)S(1)}, f32[4,2,32,128]{3,2,1,0:T(8,128)}, u32[]{:S(2)}) copy-start(f32[4,2,32,128]{3,2,1,0:T(8,128)} %inv_ref.3) | copy-start | bytes 393220
  12.9 0.8 %collective-permute-start.1 = (f32[8,128]{1,0:T(8,128)S(1)}, f32[8,128]{1,0:T(8,128)S(1)}, u32[]{:S(2)}, u32[]{:S(2)}) collective-permute-start(f32[8,128]{1,0:T(8,128)S(1)} %get-tuple-element.27), channel_id=1, source_target_pairs={{0,0},{1,9},{2,18},{3,27},{4,4},{5,13},{6,22},{7,31},{8,8},{9,1},{... | collective-permute-start | bytes 12296 | tf_op jit(solution)/shard_map/ppermute | solution.py:445
  13.8 5.0 %collective-permute-start.2 = (f32[8,128]{1,0:T(8,128)S(1)}, f32[8,128]{1,0:T(8,128)S(1)}, u32[]{:S(2)}, u32[]{:S(2)}) collective-permute-start(f32[8,128]{1,0:T(8,128)S(1)} %collective-permute-done.1.info_ref), channel_id=1, source_target_pairs={{0,1},{1,0},{2,3},{3,2},{4,5},{5,4},{6,7},{7,6},{8,9},{9,8},{10,11... | collective-permute-start | bytes 12296 | tf_op jit(solution)/shard_map/ppermute | solution.py:470
  18.8 9.7 %collective-permute-start.3 = (f32[264,128]{1,0:T(8,128)S(1)}, f32[264,128]{1,0:T(8,128)S(1)}, u32[]{:S(2)}, u32[]{:S(2)}) collective-permute-start(f32[264,128]{1,0:T(8,128)S(1)} %add.1.sum_ref), channel_id=1, source_target_pairs={{0,2},{1,3},{2,0},{3,1},{4,6},{5,7},{6,4},{7,5},{8,10},{9,11},{10,... | collective-permute-start | bytes 405512 | tf_op jit(solution)/shard_map/ppermute | solution.py:479
  22.2 4.0 %copy-start.9 = (f32[4]{0:T(128)S(1)}, f32[4]{0:T(128)}, u32[]{:S(2)}) copy-start(f32[4]{0:T(128)} %jas_ref.1) | copy-start | bytes 52
  22.2 15.2 %collective-permute-start.4 = (f32[144,128]{1,0:T(8,128)S(1)}, f32[144,128]{1,0:T(8,128)S(1)}, u32[]{:S(2)}, u32[]{:S(2)}) collective-permute-start(f32[144,128]{1,0:T(8,128)S(1)} %get-tuple-element.32), channel_id=1, source_target_pairs={{0,4},{4,0},{8,12},{12,8},{16,20},{20,16},{24,28},{28,24},{1,5},{5... | collective-permute-start | bytes 221192 | tf_op jit(solution)/shard_map/ppermute | solution.py:486
  23.8 4.7 %copy-start.10 = (f32[4]{0:T(128)S(1)}, f32[4]{0:T(128)}, u32[]{:S(2)}) copy-start(f32[4]{0:T(128)} %amp_ref.1) | copy-start | bytes 52
  23.8 13.7 %collective-permute-start.5 = (f32[144,128]{1,0:T(8,128)S(1)}, f32[144,128]{1,0:T(8,128)S(1)}, u32[]{:S(2)}, u32[]{:S(2)}) collective-permute-start(f32[144,128]{1,0:T(8,128)S(1)} %get-tuple-element.33), channel_id=1, source_target_pairs={{4,8},{12,16},{20,24},{8,4},{16,12},{24,20},{5,9},{13,17},{21,25},... | collective-permute-start | bytes 221192 | tf_op jit(solution)/shard_map/ppermute | solution.py:487
  32.8 5.0 %collective-permute-start.6 = (f32[144,128]{1,0:T(8,128)S(1)}, f32[144,128]{1,0:T(8,128)S(1)}, u32[]{:S(2)}, u32[]{:S(2)}) collective-permute-start(f32[144,128]{1,0:T(8,128)S(1)} %get-tuple-element.34), channel_id=1, source_target_pairs={{0,4},{4,0},{8,12},{12,8},{16,20},{20,16},{24,28},{28,24},{1,5},{5... | collective-permute-start | bytes 221192 | tf_op jit(solution)/shard_map/ppermute | solution.py:503
  35.6 7.1 %collective-permute-start.7 = (f32[144,128]{1,0:T(8,128)S(1)}, f32[144,128]{1,0:T(8,128)S(1)}, u32[]{:S(2)}, u32[]{:S(2)}) collective-permute-start(f32[144,128]{1,0:T(8,128)S(1)} %get-tuple-element.35), channel_id=1, source_target_pairs={{4,8},{12,16},{20,24},{8,4},{16,12},{24,20},{5,9},{13,17},{21,25},... | collective-permute-start | bytes 221192 | tf_op jit(solution)/shard_map/ppermute | solution.py:504

commit v2 on v1

--- a/solution.py
+++ b/solution.py
@@ -88,21 +88,36 @@
     return total
 
 
-def energy_kernel(pos_ref, dis_ref, order_ref, flags_ref, counts_ref, now_ref, energy_ref, info_ref):
-    walkers, _, both = pos_ref.shape
+def in_rows(rows):
+    return [r[:, at : at + LANES] for at in range(0, rows[0].shape[1], LANES) for r in rows]
+
+
+def energy_kernel(
+    pos_ref, dis_ref, order_ref, flags_ref, counts_ref, spots_ref, info_ref,
+):
+    _, walkers, both = pos_ref.shape
     nel = both // 2
     cols, keep = moves_of(order_ref, flags_ref)
     hots = one_hots(cols, nel)
+    applied = jnp.concatenate(
+        [
+            jnp.concatenate(
+                [
+                    jnp.sum(hots[2 * w + s] * keep[2 * w + s], axis=0, keepdims=True)
+                    for s in (0, 1)
+                ],
+                axis=1,
+            )
+            for w in range(walkers)
+        ],
+        axis=0,
+    )
+    now = [pos_ref[c] + dis_ref[c] * applied for c in range(3)]
+    turn = turned(jnp.concatenate(now, axis=0))
     weighted = jnp.zeros((1, 1), F32)
     for w in range(walkers):
-        applied = [
-            jnp.sum(hots[2 * w + s] * keep[2 * w + s], axis=0, keepdims=True) for s in (0, 1)
-        ]
-        now = pos_ref[w] + dis_ref[w] * jnp.concatenate(applied, axis=1)
-        now_ref[w] = now
-        turn = turned(jnp.concatenate([now, jnp.zeros((5, both), F32)], axis=0))
-        ncols = [turn[:, c : c + 1] for c in range(3)]
-        nrows = [now[c : c + 1] for c in range(3)]
+        ncols = [turn[:, c * walkers + w : c * walkers + w + 1] for c in range(3)]
+        nrows = [now[c][w : w + 1] for c in range(3)]
         soft = jnp.zeros((8, nel), F32)
         for a, b, weight in blocks_of(nel):
             squares = squares_of(ncols, nrows, a, b, nel)
@@ -111,7 +126,11 @@
             soft = soft + (part if weight == 1.0 else part * weight)
         whole = jnp.sum(jnp.sum(soft, axis=0, keepdims=True), axis=1, keepdims=True)
         energy = (whole - 1.0 * both) / (1.0 * both * (both - 1))
-        energy_ref[w : w + 1, :] = jnp.broadcast_to(energy, (1, energy_ref.shape[1]))
+        wide = [jnp.broadcast_to(energy, (1, LANES)), jnp.zeros((7 - 3 * (both // LANES), LANES), F32)]
+        spots_ref[w, :8] = jnp.concatenate(in_rows(nrows) + wide[: 1 + (3 * (both // LANES) < 7)], axis=0)
+        spots_ref[w, 8 : 8 + 3 * (both // LANES)] = jnp.concatenate(
+            in_rows([pos_ref[c, w : w + 1] for c in range(3)]), axis=0
+        )
         weighted = weighted + energy * counts_ref[w].astype(F32)
     me = lax.axis_index("walkers")
     lanes = lax.broadcasted_iota(jnp.int32, info_ref.shape, 1)
@@ -124,72 +143,71 @@
     )
 
 
-def jastrow_kernel(pos_ref, now_ref, jas_ref, out_ref):
-    walkers, _, both = pos_ref.shape
-    nel = both // 2
-    for w in range(walkers):
-        old = pos_ref[w]
-        new = now_ref[w]
-        turn = turned(jnp.concatenate([old, new, jnp.zeros((2, both), F32)], axis=0))
-        ocols = [turn[:, c : c + 1] for c in range(3)]
-        ncols = [turn[:, 3 + c : 4 + c] for c in range(3)]
-        orows = [old[c : c + 1] for c in range(3)]
-        nrows = [new[c : c + 1] for c in range(3)]
+def jastrow_kernel(spots_ref, jas_ref, out_ref):
+    walkers = spots_ref.shape[0]
+    nel = LANES
+    parts = max(lax.axis_size("orb") // 2, 1)
+    share = walkers // parts
+    first = lax.div(lax.axis_index("orb"), lax.axis_size("orb") // parts) * share
+    out_ref[...] = jnp.zeros(out_ref.shape, F32)
+    for w in range(share):
+        rows = spots_ref[first + w]
+        turn = turned(rows)
+        new, old = (
+            [
+                [rows[base + 3 * h + c : base + 3 * h + c + 1] for c in range(3)]
+                for h in (0, 1)
+            ]
+            for base in (0, 8)
+        )
+        newt, oldt = (
+            [
+                [turn[:, base + 3 * h + c : base + 3 * h + c + 1] for c in range(3)]
+                for h in (0, 1)
+            ]
+            for base in (0, 8)
+        )
         total = jnp.zeros((8, nel), F32)
         for a, b, weight in blocks_of(nel):
             kind = 0 if a == b else 1
             fall = jas_ref[2 + kind]
-            osq = squares_of(ocols, orows, a, b, nel)
-            nsq = squares_of(ncols, nrows, a, b, nel)
+            osq = squares_of(oldt[a // nel], old[b // nel], 0, 0, nel)
+            nsq = squares_of(newt[a // nel], new[b // nel], 0, 0, nel)
             od = jnp.sqrt(osq)
             nd = jnp.sqrt(nsq)
             terms = (nd - od) / ((1.0 + fall * nd) * (1.0 + fall * od))
             part = jnp.sum(terms.reshape(nel // 8, 8, nel), axis=0)
             total = total + part * (jas_ref[kind] * weight)
         whole = jnp.sum(jnp.sum(total, axis=0, keepdims=True), axis=1, keepdims=True)
-        out_ref[w : w + 1, :] = jnp.broadcast_to(0.5 * whole, (1, out_ref.shape[1]))
-
-
-def partial_kernel(
-    pos_ref, dis_ref, order_ref, flags_ref, counts_ref, cen_ref, exp_ref, orb_ref, inv_ref,
-    sla_ref, now_ref, energy_ref, part_ref, done_ref, pair_ref, odd_ref, differ_ref,
-):
-    walkers, _, both = pos_ref.shape
+        out_ref[pl.ds(2 + first + w, 1), :] = jnp.broadcast_to(
+            0.5 * whole, (1, out_ref.shape[1])
+        )
+
+
+def shift_kernel(pos_ref, dis_ref, order_ref, flags_ref, cen_ref, exp_ref, orb_ref, shift_ref, differ_ref):
+    _, walkers, both = pos_ref.shape
     nel = both // 2
     moves = flags_ref.shape[2]
     basis = cen_ref.shape[1]
-    orbs = inv_ref.shape[2]
-    cols, keep = moves_of(order_ref, flags_ref)
+    cols, _ = moves_of(order_ref, flags_ref)
     hots = one_hots(cols, nel)
+    rows = [ref[c] for ref in (pos_ref, dis_ref) for c in range(3)]
+    rows = jnp.concatenate(rows + [jnp.zeros((-6 * walkers % 8, both), F32)] * (6 * walkers % 8 > 0), axis=0)
     for s in (0, 1):
-        table = jnp.concatenate(
-            [
-                jnp.concatenate(
-                    [
-                        pos_ref[w, :, s * nel : (s + 1) * nel],
-                        dis_ref[w, :, s * nel : (s + 1) * nel],
-                        jnp.zeros((2, nel), F32),
-                    ],
-                    axis=0,
-                )
-                for w in range(walkers)
-            ],
-            axis=0,
-        )
-        points = nt(jnp.concatenate([hots[2 * w + s] for w in range(walkers)], axis=0), table)
+        points = nt(
+            jnp.concatenate([hots[2 * w + s] for w in range(walkers)], axis=0),
+            rows[:, s * nel : (s + 1) * nel],
+        )
         for w in range(walkers):
             mine = points[w * moves : (w + 1) * moves]
-            old = [
-                jnp.broadcast_to(mine[:, 8 * w + c : 8 * w + c + 1], (moves, LANES))
-                for c in range(3)
-            ]
-            new = [
-                jnp.broadcast_to(
-                    mine[:, 8 * w + c : 8 * w + c + 1] + mine[:, 8 * w + 3 + c : 8 * w + 4 + c],
-                    (moves, LANES),
-                )
-                for c in range(3)
-            ]
+            old = []
+            new = []
+            for c in range(3):
+                at = c * walkers + w
+                to = (3 + c) * walkers + w
+                spot = mine[:, at : at + 1]
+                old.append(jnp.broadcast_to(spot, (moves, LANES)))
+                new.append(jnp.broadcast_to(spot + mine[:, to : to + 1], (moves, LANES)))
             for j in range(0, basis, LANES):
                 osq = None
                 nsq = None
@@ -204,10 +222,22 @@
                     rate * nsq
                 ) - jnp.exp(rate * osq)
     for s in (0, 1):
-        shift = nt(differ_ref[s], orb_ref[s])
+        shift_ref[s] = nt(differ_ref[s], orb_ref[s])
+
+
+def partial_kernel(
+    shift_ref, order_ref, flags_ref, counts_ref, inv_ref, sla_ref, spots_ref, info_ref,
+    part_ref, done_ref, pair_ref, odd_ref,
+):
+    walkers, _, orbs, nel = inv_ref.shape
+    moves = flags_ref.shape[2]
+    cols, keep = moves_of(order_ref, flags_ref)
+    hots = one_hots(cols, nel)
+    part_ref[2 * walkers * moves :, :] = info_ref[...]
+    for s in (0, 1):
         for w in range(walkers):
             i = 2 * w + s
-            mine = shift[w * moves : (w + 1) * moves]
+            mine = shift_ref[s, w * moves : (w + 1) * moves, :]
             proposed = mine + nt(hots[i], sla_ref[w, s])
             part = nn(proposed, inv_ref[w, s])
             part_ref[i * moves : (i + 1) * moves, :] = part * keep[i]
@@ -215,32 +245,25 @@
     half = walkers // 2
     per = 2 * orbs
     tail = half * per
-    width = both // LANES
     parity = lax.rem(lax.axis_index("walkers"), 2)
     number = total_of(counts_ref)
     for pay, goes_up in ((pair_ref, parity == 0), (odd_ref, parity == 1)):
-        pay[tail:, :] = jnp.zeros((pay.shape[0] - tail, LANES), F32)
         for j in range(half):
             index = jnp.where(goes_up, number - half + j, j)
             source = pick(counts_ref, index)
             for s in (0, 1):
                 pay[j * per + s * orbs : j * per + (s + 1) * orbs, :] = done_ref[source, s]
-            spot = now_ref[source]
-            for h in range(width):
-                at = tail + (j * width + h) * 3
-                pay[at : at + 3, :] = spot[:, h * LANES : (h + 1) * LANES]
-            at = tail + half * width * 3 + j
-            pay[at : at + 1, :] = energy_ref[pl.ds(source, 1), :]
-
-
-def add_kernel(mine_ref, other_ref, info_ref, info_other_ref, out_ref):
-    rows = mine_ref.shape[0]
-    out_ref[:rows, :] = mine_ref[...] + other_ref[...]
-    out_ref[rows:, :] = info_ref[...] + info_other_ref[...]
+            pay[tail + 8 * j : tail + 8 * j + 8, :] = spots_ref[source, :8]
+
+
+def add_kernel(mine_ref, other_ref, change_ref, out_ref):
+    rows = mine_ref.shape[0] - change_ref.shape[0]
+    out_ref[:rows, :] = mine_ref[:rows, :] + other_ref[:rows, :]
+    out_ref[rows:, :] = mine_ref[rows:, :] + other_ref[rows:, :] + change_ref[...]
 
 
 def update_kernel(
-    sum_ref, got_ref, inv_ref, order_ref, flags_ref, counts_ref, amp_ref, jas_ref,
+    sum_ref, got_ref, inv_ref, order_ref, flags_ref, counts_ref, amp_ref,
     cur_ref, log_ref, info_ref, pair_ref, odd_ref,
 ):
     walkers, _, orbs, nel = inv_ref.shape
@@ -294,7 +317,7 @@
         both = jnp.log(jnp.abs(pivots[2 * w])) + jnp.log(jnp.abs(pivots[2 * w + 1]))
         log_ref[w : w + 1, :] = (
             jnp.broadcast_to(jnp.sum(both, axis=1, keepdims=True), (1, nel))
-            + jas_ref[w : w + 1, :]
+            + info_ref[2 + w : 3 + w, :nel]
             + amp_ref[w]
         )
     half = walkers // 2
@@ -315,13 +338,12 @@
 
 
 def place_kernel(
-    counts_ref, cur_ref, done_ref, now_ref, energy_ref, log_ref, info_ref,
+    counts_ref, cur_ref, done_ref, spots_ref, log_ref, info_ref,
     pair_s_ref, odd_s_ref, pair_i_ref, odd_i_ref,
     inv_out, sla_out, pos_out, log_out, energy_out, mean_out,
 ):
     walkers, _, orbs, nel = cur_ref.shape
-    both = now_ref.shape[2]
-    width = both // LANES
+    width = pos_out.shape[2] // LANES
     half = walkers // 2
     per = 2 * orbs
     tail = half * per
@@ -334,16 +356,19 @@
     mean = jnp.sum(info[1:2], axis=1, keepdims=True)
     mean_out[...] = mean / (1.0 * walkers * groups)
     number = total_of(counts_ref)
-    spots = lax.broadcasted_iota(jnp.int32, (1, walkers), 1)
-
-    def put(j, inverse, slater, spot, log, energy):
+    slots = lax.broadcasted_iota(jnp.int32, (1, walkers), 1)
+
+    def put(j, inverse, slater, spot, log):
         for s in (0, 1):
             inv_out[j, s] = inverse(s)
             sla_out[j, s] = slater(s)
-        for h in range(width):
-            pos_out[j, :, h * LANES : (h + 1) * LANES] = spot(h)
-        log_out[...] = jnp.where(spots == j, log[:, :walkers], log_out[...])
-        energy_out[...] = jnp.where(spots == j, energy[:, :walkers], energy_out[...])
+        for c in range(3):
+            for h in range(width):
+                pos_out[c, j : j + 1, h * LANES : (h + 1) * LANES] = spot[3 * h + c : 3 * h + c + 1]
+        log_out[...] = jnp.where(slots == j, log[:, :walkers], log_out[...])
+        energy_out[...] = jnp.where(
+            slots == j, spot[3 * width : 3 * width + 1, :walkers], energy_out[...]
+        )
 
     log_out[...] = jnp.zeros(log_out.shape, F32)
     energy_out[...] = jnp.zeros(energy_out.shape, F32)
@@ -359,20 +384,18 @@
                 j,
                 lambda s: cur_ref[w, s],
                 lambda s: done_ref[w, s],
-                lambda h: now_ref[w, :, h * LANES : (h + 1) * LANES],
+                spots_ref[w, :8],
                 log_ref[pl.ds(w, 1), :],
-                energy_ref[pl.ds(w, 1), :],
             )
 
         def received(late, early):
             i = jnp.clip(jnp.where(low, index + half, index - number), 0, half - 1)
             put(
                 j,
-                lambda s: late[pl.ds(i * per + s * orbs, orbs), :],
-                lambda s: early[pl.ds(i * per + s * orbs, orbs), :],
-                lambda h: early[pl.ds(tail + (i * width + h) * 3, 3), :],
+                lambda s: late[pl.ds(pl.multiple_of(i * per + s * orbs, 8), orbs), :],
+                lambda s: early[pl.ds(pl.multiple_of(i * per + s * orbs, 8), orbs), :],
+                early[pl.ds(pl.multiple_of(tail + i * 8, 8), 8), :],
                 late[pl.ds(tail + INFO + i, 1), :],
-                early[pl.ds(tail + half * width * 3 + i, 1), :],
             )
 
         on_pair = (low & (parity == 1)) | (high & (parity == 0))
@@ -386,7 +409,7 @@
             received(odd_i_ref, odd_s_ref)
 
 
-def call(kernel, outs, in_specs, scratch=(), flops=0, name=None):
+def call(kernel, outs, in_specs, scratch=(), us=1.0, name=None):
     return pl.pallas_call(
         kernel,
         out_shape=outs,
@@ -394,7 +417,7 @@
         out_specs=jax.tree.map(lambda _: VMEM, outs),
         scratch_shapes=list(scratch),
         compiler_params=pltpu.CompilerParams(vmem_limit_bytes=32 * 2**20),
-        cost_estimate=pl.CostEstimate(flops=flops, bytes_accessed=2**18, transcendentals=0),
+        cost_estimate=pl.CostEstimate(flops=int(us * 1.1e9), bytes_accessed=2**18, transcendentals=0),
         name=name,
     )
 
@@ -423,13 +446,18 @@
     odds = [(i, i + 1) for i in range(1, groups - 1, 2)]
     odds = odds + [(b, a) for a, b in odds]
 
-    now, energy, info = call(
+    places = positions.transpose(1, 0, 2)
+    steps = displacements.transpose(1, 0, 2)
+    spots, info = call(
         energy_kernel,
-        (shape(walkers, 3, both), shape(walkers, LANES), shape(INFO, wide)),
+        (
+            shape(walkers, 16, LANES),
+            shape(INFO, wide),
+        ),
         [VMEM, VMEM, VMEM, VMEM, SMEM],
-        flops=10**6,
+        us=2,
         name="energy",
-    )(positions, displacements, move_order, accepted, counts)
+    )(places, steps, move_order, accepted, counts)
 
     hops = members * 2
     step = hops
@@ -444,44 +472,47 @@
     ]
     info = lax.ppermute(info, ("walkers", "orb"), joint)
 
+    shift = call(
+        shift_kernel,
+        shape(2, walkers * moves, orbs),
+        [VMEM] * 7,
+        scratch=[pltpu.VMEM((2, walkers * moves, basis), F32)],
+        us=3,
+        name="shift",
+    )(places, steps, move_order, accepted, centers, exponents.reshape(1, basis), orbitals)
+
     part, done, pair_s, odd_s = call(
         partial_kernel,
         (
-            shape(count * moves, nel),
+            shape(count * moves + INFO, nel),
             shape(walkers, 2, orbs, nel),
             shape(tall, LANES),
             shape(tall, LANES),
         ),
-        [VMEM, VMEM, VMEM, VMEM, SMEM] + [VMEM] * 7,
-        scratch=[pltpu.VMEM((2, walkers * moves, basis), F32)],
-        flops=10**6,
+        [VMEM, VMEM, VMEM, SMEM] + [VMEM] * 4,
+        us=2,
         name="partial",
-    )(
-        positions, displacements, move_order, accepted, counts, centers,
-        exponents.reshape(1, basis), orbitals, inverse, slater, now, energy,
-    )
+    )(shift, move_order, accepted, counts, inverse, slater, spots, info)
+
+    change = call(
+        jastrow_kernel, shape(INFO, wide), [VMEM, SMEM], us=1.2, name="jastrow"
+    )(spots, jastrow)
 
     total = part
+    got = jnp.zeros_like(part)
     step = 1
     while step < members:
         partner = [(o, o ^ step) for o in range(members)]
-        if step == 1:
-            other = lax.ppermute(part, "orb", partner)
-            info_other = lax.ppermute(info, "orb", partner)
+        got = lax.ppermute(total, "orb", partner)
+        if 2 * step < members:
             total = call(
                 add_kernel,
                 shape(count * moves + INFO, nel),
-                [VMEM] * 4,
-                flops=10**5,
+                [VMEM] * 3,
+                us=0.7,
                 name="add",
-            )(part, other, info, info_other)
-        else:
-            got = lax.ppermute(total, "orb", partner)
+            )(total, got, change if step == 1 else jnp.zeros_like(change))
         step *= 2
-
-    change = call(
-        jastrow_kernel, shape(walkers, LANES), [VMEM, VMEM, SMEM], flops=10**6, name="jastrow"
-    )(positions, now, jastrow)
 
     pair_s = lax.ppermute(pair_s, "walkers", pairs)
     odd_s = lax.ppermute(odd_s, "walkers", odds)
@@ -495,10 +526,10 @@
             shape(tall, LANES),
             shape(tall, LANES),
         ),
-        [VMEM] * 5 + [SMEM, SMEM, VMEM],
-        flops=10**6,
+        [VMEM] * 5 + [SMEM, SMEM],
+        us=4,
         name="update",
-    )(total, got, inverse, move_order, accepted, counts, log_amp, change)
+    )(total, got, inverse, move_order, accepted, counts, log_amp)
 
     pair_i = lax.ppermute(pair_i, "walkers", pairs)
     odd_i = lax.ppermute(odd_i, "walkers", odds)
@@ -508,19 +539,19 @@
         (
             shape(walkers, 2, orbs, nel),
             shape(walkers, 2, orbs, nel),
-            shape(walkers, 3, both),
+            shape(3, walkers, both),
             shape(1, walkers),
             shape(1, walkers),
             shape(1, 1),
         ),
-        [SMEM] + [VMEM] * 10,
-        flops=10**5,
+        [SMEM] + [VMEM] * 9,
+        us=1.5,
         name="place",
-    )(counts, current, done, now, energy, logs, info, pair_s, odd_s, pair_i, odd_i)
+    )(counts, current, done, spots, logs, info, pair_s, odd_s, pair_i, odd_i)
     return (
         inv_new,
         sla_new,
-        pos_new,
+        pos_new.transpose(1, 0, 2),
         log_new.reshape(walkers),
         energy_new.reshape(walkers),
         mean.reshape(()),

time: 45.2 us -> 37.5 us (0.83)
  Pallas kernels: 15.5 us -> 12.9 us
  starting transfers between devices: 17 us -> 15 us
  local copies, waits for them, and re-layouts: 5.46 us -> 3.48 us
  waiting for transfers between devices: 6.03 us -> 4.9 us
    ppermute x2 -> x0, starting transfers between devices: 4.22 us -> none  [the longest x1 4.15 us: body(): info_other = lax.ppermute(info, 'orb', partner)]
    pallas_call x4 -> x5, Pallas kernels: 9.55 us -> 6.98 us  [the longest x1 2.19 us: body(): call(shift_kernel, shape(2, walkers * moves, orbs), [VMEM] * 7, scratch=[...]
    ppermute x1 -> x2, starting transfers between devices: 3.47 us -> 6.04 us  [body(): got = lax.ppermute(total, 'orb', partner)]
    unnamed x27 -> x28, local copies, waits for them, and re-layouts: 5.46 us -> 3.48 us
    ppermute x2 -> x0, waiting for transfers between devices: 0.83 us -> none  [the longest x1 0.82 us: body(): info_other = lax.ppermute(info, 'orb', partner)]
  transfers between devices with their start and end apart: 8 -> 7, of which waited for: 3 -> 2; matrix products, arithmetic and copies ran while one was open for 0% -> 0% of each run, Pallas kernels for 15% -> 22%
where the time goes in v2:
time: 37.5 us; the launch traced here: 37.1 us
  starting transfers between devices  15 us (40%)
  Pallas kernels  12.9 us (34%)
  waiting for transfers between devices  4.9 us (13%)
  local copies, waits for them, and re-layouts  3.48 us (9%)
  between operations  0.84 us (2%)
    ppermute x2, starting transfers between devices, body(): got = lax.ppermute(total, 'orb', partner)  6.04 us
    ppermute x1, waiting for transfers between devices, body(): odd_i = lax.ppermute(odd_i, 'walkers', odds)  4.8 us
    pallas_call x1, Pallas kernels, body(): call(update_kernel, (shape(walkers, 2, orbs, nel), shape(8, nel), shape(I...  4.42 us
    unnamed x28, local copies, waits for them, and re-layouts  3.48 us
    ppermute x1, starting transfers between devices, body(): pair_i = lax.ppermute(pair_i, 'walkers', pairs)  2.3 us
    ppermute x1, starting transfers between devices, body(): odd_s = lax.ppermute(odd_s, 'walkers', odds)  2.29 us
    ppermute x1, starting transfers between devices, body(): odd_i = lax.ppermute(odd_i, 'walkers', odds)  2.22 us
    pallas_call x1, Pallas kernels, body(): call(shift_kernel, shape(2, walkers * moves, orbs), [VMEM] * 7, scratch=[...  2.19 us
  transfers between devices with their start and end apart: 7, of which 2 were waited for; matrix products, arithmetic and copies ran while one was open for 0% of the time, Pallas kernels for 22%

profile of v2, /device:TPU:8, one launch (start us, length us, event | category | flops | bytes accessed | tf_op | source)
XLA Modules:
  0.0 37.1 jit_solution(14793242777097955786)
XLA Ops:
  0.6 0.6 %copy-done.13 = s32[4]{0:T(128)S(1)} copy-done((s32[4]{0:T(128)S(1)}, s32[4]{0:T(128)}, u32[]{:S(2)}) %copy-start.13) | copy-done | bytes 40
  1.3 0.7 %copy-done.4 = f32[4,3,256]{2,0,1:T(4,128)S(1)} copy-done((f32[4,3,256]{2,0,1:T(4,128)S(1)}, f32[4,3,256]{2,0,1:T(4,128)}, u32[]{:S(2)}) %copy-start.4) | copy-done | bytes 12312
  2.0 0.7 %copy-done.5 = f32[4,3,256]{2,0,1:T(4,128)S(1)} copy-done((f32[4,3,256]{2,0,1:T(4,128)S(1)}, f32[4,3,256]{2,0,1:T(4,128)}, u32[]{:S(2)}) %copy-start.5) | copy-done | bytes 12312
  2.7 0.7 %copy-done.7 = s32[4,2,128]{2,1,0:T(2,128)S(1)} copy-done((s32[4,2,128]{2,1,0:T(2,128)S(1)}, s32[4,2,128]{2,1,0:T(2,128)}, u32[]{:S(2)}) %copy-start.7) | copy-done | bytes 4120
  3.4 0.7 %copy-done.9 = s32[4,2,32]{2,1,0:T(2,128)S(1)} copy-done((s32[4,2,32]{2,1,0:T(2,128)S(1)}, s32[4,2,32]{2,1,0:T(2,128)}, u32[]{:S(2)}) %copy-start.9) | copy-done | bytes 1048
  4.1 1.7 %energy.1 = (f32[4,16,128]{2,1,0:T(8,128)S(1)}, f32[8,128]{1,0:T(8,128)S(1)}) custom-call(f32[3,4,256]{2,1,0:T(4,128)S(1)} %bitcast.7, f32[3,4,256]{2,1,0:T(4,128)S(1)} %bitcast.9, s32[4,2,128]{2,1,0:T(2,128)S(1)} %copy-done.7, s32[4,2,32]{2,1,0:T(2,128)S(1)} %copy-done.9, s32[4]{0:T(128)S(1)} %copy-done.13), custom_call_target="tpu_custom_call" | custom-call | flops 2200000000 | bytes 262144 | tf_op jit(solution)/shard_map/energy/pallas_call | solution.py:451
  5.8 0.7 %collective-permute-start = (f32[8,128]{1,0:T(8,128)S(1)}, f32[8,128]{1,0:T(8,128)S(1)}, u32[]{:S(2)}, u32[]{:S(2)}) collective-permute-start(f32[8,128]{1,0:T(8,128)S(1)} %get-tuple-element.24), channel_id=1, source_target_pairs={{0,0},{1,9},{2,18},{3,27},{4,4},{5,13},{6,22},{7,31},{8,8},{9,1},{... | collective-permute-start | bytes 12296 | tf_op jit(solution)/shard_map/ppermute | solution.py:473
  6.5 0.0 copy-start.1
  6.5 0.0 copy-start.8
  6.5 0.0 copy-start.10
  6.5 2.2 %shift.1.shift_ref = f32[2,128,32]{2,1,0:T(8,128)S(1)} custom-call(f32[3,4,256]{2,1,0:T(4,128)S(1)} %bitcast.8, f32[3,4,256]{2,1,0:T(4,128)S(1)} %bitcast.10, s32[4,2,128]{2,1,0:T(2,128)S(1)} %copy-done.7, s32[4,2,32]{2,1,0:T(2,128)S(1)} %copy-done.9, f32[3,1024]{1,0:T(4,128)S(1)} %copy-done.3, f32[1,1024]{1,0:T(1,128)S(1)} %bitcast.11, ...), custom_call_target="tpu_custom_call" | custom-call | flops 3300000000 | bytes 262144 | tf_op jit(solution)/shard_map/shift/pallas_call | solution.py:475
  8.8 1.6 %partial.1 = (f32[264,128]{1,0:T(8,128)S(1)}, f32[4,2,32,128]{3,2,1,0:T(8,128)S(1)}, f32[144,128]{1,0:T(8,128)S(1)}, f32[144,128]{1,0:T(8,128)S(1)}) custom-call(f32[2,128,32]{2,1,0:T(8,128)S(1)} %shift.1.shift_ref, s32[4,2,128]{2,1,0:T(2,128)S(1)} %copy-done.8, s32[4,2,32]{2,1,0:T(2,128)S(1)} %copy-done.10, s32[4]{0:T(128)S(1)} %copy-done.13, ...), custom_call_target="tpu_custom_call" | custom-call | flops 2200000000 | bytes 262144 | tf_op jit(solution)/shard_map/partial/pallas_call | solution.py:484
  10.4 0.0 copy-start.11
  10.4 1.3 %collective-permute-start.1 = (f32[264,128]{1,0:T(8,128)S(1)}, f32[264,128]{1,0:T(8,128)S(1)}, u32[]{:S(2)}, u32[]{:S(2)}) collective-permute-start(f32[264,128]{1,0:T(8,128)S(1)} %get-tuple-element.25.mine_ref), channel_id=1, source_target_pairs={{0,1},{1,0},{2,3},{3,2},{4,5},{5,4},{6,7},{7,6},{8,9},{9,8},{10,11... | collective-permute-start | bytes 405512 | tf_op jit(solution)/shard_map/ppermute | solution.py:506
  11.7 1.5 %jastrow.1.change_ref = f32[8,128]{1,0:T(8,128)S(1)} custom-call(f32[4,16,128]{2,1,0:T(8,128)S(1)} %get-tuple-element.23.spots_ref, f32[4]{0:T(128)S(1)} %copy-done.11), custom_call_target="tpu_custom_call" | custom-call | flops 1320000000 | bytes 262144 | tf_op jit(solution)/shard_map/jastrow/pallas_call | solution.py:497
  13.2 4.8 %collective-permute-start.2 = (f32[264,128]{1,0:T(8,128)S(1)}, f32[264,128]{1,0:T(8,128)S(1)}, u32[]{:S(2)}, u32[]{:S(2)}) collective-permute-start(f32[264,128]{1,0:T(8,128)S(1)} %add.1.sum_ref), channel_id=1, source_target_pairs={{0,2},{1,3},{2,0},{3,1},{4,6},{5,7},{6,4},{7,5},{8,10},{9,11},{10,... | collective-permute-start | bytes 405512 | tf_op jit(solution)/shard_map/ppermute | solution.py:506
  17.9 1.5 %collective-permute-start.3 = (f32[144,128]{1,0:T(8,128)S(1)}, f32[144,128]{1,0:T(8,128)S(1)}, u32[]{:S(2)}, u32[]{:S(2)}) collective-permute-start(f32[144,128]{1,0:T(8,128)S(1)} %get-tuple-element.30), channel_id=1, source_target_pairs={{0,4},{4,0},{8,12},{12,8},{16,20},{20,16},{24,28},{28,24},{1,5},{5... | collective-permute-start | bytes 221192 | tf_op jit(solution)/shard_map/ppermute | solution.py:517
  19.5 2.3 %collective-permute-start.4 = (f32[144,128]{1,0:T(8,128)S(1)}, f32[144,128]{1,0:T(8,128)S(1)}, u32[]{:S(2)}, u32[]{:S(2)}) collective-permute-start(f32[144,128]{1,0:T(8,128)S(1)} %get-tuple-element.31), channel_id=1, source_target_pairs={{4,8},{12,16},{20,24},{8,4},{16,12},{24,20},{5,9},{13,17},{21,25},... | collective-permute-start | bytes 221192 | tf_op jit(solution)/shard_map/ppermute | solution.py:518
  21.8 4.4 %update.1 = (f32[4,2,32,128]{3,2,1,0:T(8,128)S(1)}, f32[8,128]{1,0:T(8,128)S(1)}, f32[8,128]{1,0:T(8,128)S(1)}, f32[144,128]{1,0:T(8,128)S(1)}, f32[144,128]{1,0:T(8,128)S(1)}) custom-call(f32[264,128]{1,0:T(8,128)S(1)} %add.1.sum_ref, f32[264,128]{1,0:T(8,128)S(1)} %collective-permute-done.2.got_ref, f32[4,2,32,128]{3,2,1,0:T(8,128)S(1)} %copy-done.2, ...), custom_call_target="tpu_custom_call" | custom-call | flops 4400000000 | bytes 262144 | tf_op jit(solution)/shard_map/update/pallas_call | solution.py:520
  26.2 2.3 %collective-permute-start.5 = (f32[144,128]{1,0:T(8,128)S(1)}, f32[144,128]{1,0:T(8,128)S(1)}, u32[]{:S(2)}, u32[]{:S(2)}) collective-permute-start(f32[144,128]{1,0:T(8,128)S(1)} %get-tuple-element.32), channel_id=1, source_target_pairs={{0,4},{4,0},{8,12},{12,8},{16,20},{20,16},{24,28},{28,24},{1,5},{5... | collective-permute-start | bytes 221192 | tf_op jit(solution)/shard_map/ppermute | solution.py:534
  28.5 2.2 %collective-permute-start.6 = (f32[144,128]{1,0:T(8,128)S(1)}, f32[144,128]{1,0:T(8,128)S(1)}, u32[]{:S(2)}, u32[]{:S(2)}) collective-permute-start(f32[144,128]{1,0:T(8,128)S(1)} %get-tuple-element.33), channel_id=1, source_target_pairs={{4,8},{12,16},{20,24},{8,4},{16,12},{24,20},{5,9},{13,17},{21,25},... | collective-permute-start | bytes 221192 | tf_op jit(solution)/shard_map/ppermute | solution.py:535
  30.7 0.1 collective-permute-done.5.pair_i_ref
  30.8 4.8 %collective-permute-done.6.odd_i_ref = f32[144,128]{1,0:T(8,128)S(1)} collective-permute-done((f32[144,128]{1,0:T(8,128)S(1)}, f32[144,128]{1,0:T(8,128)S(1)}, u32[]{:S(2)}, u32[]{:S(2)}) %collective-permute-start.6) | collective-permute-done | bytes 73760 | tf_op jit(solution)/shard_map/ppermute | solution.py:535
  35.6 1.5 %place.1 = (f32[4,2,32,128]{3,2,1,0:T(8,128)}, f32[4,2,32,128]{3,2,1,0:T(8,128)}, f32[3,4,256]{2,1,0:T(4,128)}, f32[1,4]{1,0:T(1,128)}, f32[1,4]{1,0:T(1,128)}, /*index=5*/f32[1,1]{1,0:T(1,128)}) custom-call(s32[4]{0:T(128)S(1)} %copy-done.13, f32[4,2,32,128]{3,2,1,0:T(8,128)S(1)} %get-tuple-element.26.cur_ref, ...), custom_call_target="tpu_custom_call" | custom-call | flops 1650000000 | bytes 262144 | tf_op jit(solution)/shard_map/place/pallas_call | solution.py:537
  (25 shorter events, 0.1 us)
Async XLA Ops:
  0.6 0.7 %copy-start.13 = (s32[4]{0:T(128)S(1)}, s32[4]{0:T(128)}, u32[]{:S(2)}) copy-start(s32[4]{0:T(128)} %counts_ref.7) | copy-start | bytes 52
  1.3 0.7 %copy-start.4 = (f32[4,3,256]{2,0,1:T(4,128)S(1)}, f32[4,3,256]{2,0,1:T(4,128)}, u32[]{:S(2)}) copy-start(f32[4,3,256]{2,0,1:T(4,128)} %param.14) | copy-start | bytes 36868
  2.0 0.7 %copy-start.5 = (f32[4,3,256]{2,0,1:T(4,128)S(1)}, f32[4,3,256]{2,0,1:T(4,128)}, u32[]{:S(2)}) copy-start(f32[4,3,256]{2,0,1:T(4,128)} %param.15) | copy-start | bytes 36868
  2.7 0.7 %copy-start.7 = (s32[4,2,128]{2,1,0:T(2,128)S(1)}, s32[4,2,128]{2,1,0:T(2,128)}, u32[]{:S(2)}) copy-start(s32[4,2,128]{2,1,0:T(2,128)} %order_ref.7) | copy-start | bytes 12292
  3.4 0.7 %copy-start.9 = (s32[4,2,32]{2,1,0:T(2,128)S(1)}, s32[4,2,32]{2,1,0:T(2,128)}, u32[]{:S(2)}) copy-start(s32[4,2,32]{2,1,0:T(2,128)} %flags_ref.7) | copy-start | bytes 3076
  4.1 2.4 %copy-start = (f32[2,32,1024]{2,1,0:T(8,128)S(1)}, f32[2,32,1024]{2,1,0:T(8,128)}, u32[]{:S(2)}) copy-start(f32[2,32,1024]{2,1,0:T(8,128)} %orb_ref.1) | copy-start | bytes 786436
  4.1 2.4 %copy-start.3 = (f32[3,1024]{1,0:T(4,128)S(1)}, f32[3,1024]{1,0:T(4,128)}, u32[]{:S(2)}) copy-start(f32[3,1024]{1,0:T(4,128)} %cen_ref.1) | copy-start | bytes 36868
  4.1 2.4 %copy-start.6 = (f32[1024]{0:T(1024)S(1)}, f32[1024]{0:T(1024)}, u32[]{:S(2)}) copy-start(f32[1024]{0:T(1024)} %param.21) | copy-start | bytes 12292
  5.8 2.9 %collective-permute-start = (f32[8,128]{1,0:T(8,128)S(1)}, f32[8,128]{1,0:T(8,128)S(1)}, u32[]{:S(2)}, u32[]{:S(2)}) collective-permute-start(f32[8,128]{1,0:T(8,128)S(1)} %get-tuple-element.24), channel_id=1, source_target_pairs={{0,0},{1,9},{2,18},{3,27},{4,4},{5,13},{6,22},{7,31},{8,8},{9,1},{... | collective-permute-start | bytes 12296 | tf_op jit(solution)/shard_map/ppermute | solution.py:473
  6.5 2.3 %copy-start.1 = (f32[4,2,32,128]{3,2,1,0:T(8,128)S(1)}, f32[4,2,32,128]{3,2,1,0:T(8,128)}, u32[]{:S(2)}) copy-start(f32[4,2,32,128]{3,2,1,0:T(8,128)} %sla_ref.1) | copy-start | bytes 393220
  6.5 2.3 %copy-start.2 = (f32[4,2,32,128]{3,2,1,0:T(8,128)S(1)}, f32[4,2,32,128]{3,2,1,0:T(8,128)}, u32[]{:S(2)}) copy-start(f32[4,2,32,128]{3,2,1,0:T(8,128)} %inv_ref.3) | copy-start | bytes 393220
  6.5 2.3 %copy-start.8 = (s32[4,2,128]{2,1,0:T(2,128)S(1)}, s32[4,2,128]{2,1,0:T(2,128)}, u32[]{:S(2)}) copy-start(s32[4,2,128]{2,1,0:T(2,128)} %order_ref.7) | copy-start | bytes 12292
  6.5 2.3 %copy-start.10 = (s32[4,2,32]{2,1,0:T(2,128)S(1)}, s32[4,2,32]{2,1,0:T(2,128)}, u32[]{:S(2)}) copy-start(s32[4,2,32]{2,1,0:T(2,128)} %flags_ref.7) | copy-start | bytes 3076
  10.4 1.3 %copy-start.11 = (f32[4]{0:T(128)S(1)}, f32[4]{0:T(128)}, u32[]{:S(2)}) copy-start(f32[4]{0:T(128)} %jas_ref.1) | copy-start | bytes 52
  10.4 2.8 %collective-permute-start.1 = (f32[264,128]{1,0:T(8,128)S(1)}, f32[264,128]{1,0:T(8,128)S(1)}, u32[]{:S(2)}, u32[]{:S(2)}) collective-permute-start(f32[264,128]{1,0:T(8,128)S(1)} %get-tuple-element.25.mine_ref), channel_id=1, source_target_pairs={{0,1},{1,0},{2,3},{3,2},{4,5},{5,4},{6,7},{7,6},{8,9},{9,8},{10,11... | collective-permute-start | bytes 405512 | tf_op jit(solution)/shard_map/ppermute | solution.py:506
  13.2 8.6 %collective-permute-start.2 = (f32[264,128]{1,0:T(8,128)S(1)}, f32[264,128]{1,0:T(8,128)S(1)}, u32[]{:S(2)}, u32[]{:S(2)}) collective-permute-start(f32[264,128]{1,0:T(8,128)S(1)} %add.1.sum_ref), channel_id=1, source_target_pairs={{0,2},{1,3},{2,0},{3,1},{4,6},{5,7},{6,4},{7,5},{8,10},{9,11},{10,... | collective-permute-start | bytes 405512 | tf_op jit(solution)/shard_map/ppermute | solution.py:506
  17.9 3.8 %copy-start.12 = (f32[4]{0:T(128)S(1)}, f32[4]{0:T(128)}, u32[]{:S(2)}) copy-start(f32[4]{0:T(128)} %amp_ref.1) | copy-start | bytes 52
  17.9 12.8 %collective-permute-start.3 = (f32[144,128]{1,0:T(8,128)S(1)}, f32[144,128]{1,0:T(8,128)S(1)}, u32[]{:S(2)}, u32[]{:S(2)}) collective-permute-start(f32[144,128]{1,0:T(8,128)S(1)} %get-tuple-element.30), channel_id=1, source_target_pairs={{0,4},{4,0},{8,12},{12,8},{16,20},{20,16},{24,28},{28,24},{1,5},{5... | collective-permute-start | bytes 221192 | tf_op jit(solution)/shard_map/ppermute | solution.py:517
  19.5 11.3 %collective-permute-start.4 = (f32[144,128]{1,0:T(8,128)S(1)}, f32[144,128]{1,0:T(8,128)S(1)}, u32[]{:S(2)}, u32[]{:S(2)}) collective-permute-start(f32[144,128]{1,0:T(8,128)S(1)} %get-tuple-element.31), channel_id=1, source_target_pairs={{4,8},{12,16},{20,24},{8,4},{16,12},{24,20},{5,9},{13,17},{21,25},... | collective-permute-start | bytes 221192 | tf_op jit(solution)/shard_map/ppermute | solution.py:518
  26.2 4.6 %collective-permute-start.5 = (f32[144,128]{1,0:T(8,128)S(1)}, f32[144,128]{1,0:T(8,128)S(1)}, u32[]{:S(2)}, u32[]{:S(2)}) collective-permute-start(f32[144,128]{1,0:T(8,128)S(1)} %get-tuple-element.32), channel_id=1, source_target_pairs={{0,4},{4,0},{8,12},{12,8},{16,20},{20,16},{24,28},{28,24},{1,5},{5... | collective-permute-start | bytes 221192 | tf_op jit(solution)/shard_map/ppermute | solution.py:534
  28.5 7.1 %collective-permute-start.6 = (f32[144,128]{1,0:T(8,128)S(1)}, f32[144,128]{1,0:T(8,128)S(1)}, u32[]{:S(2)}, u32[]{:S(2)}) collective-permute-start(f32[144,128]{1,0:T(8,128)S(1)} %get-tuple-element.33), channel_id=1, source_target_pairs={{4,8},{12,16},{20,24},{8,4},{16,12},{24,20},{5,9},{13,17},{21,25},... | collective-permute-start | bytes 221192 | tf_op jit(solution)/shard_map/ppermute | solution.py:535

commit v3 on v2

--- a/solution.py
+++ b/solution.py
@@ -6,6 +6,7 @@
 from jax.sharding import PartitionSpec as P
 
 F32 = jnp.float32
+BF16 = jnp.bfloat16
 highest = lax.Precision.HIGHEST
 VMEM = pl.BlockSpec(memory_space=pltpu.VMEM)
 SMEM = pl.BlockSpec(memory_space=pltpu.SMEM)
@@ -29,6 +30,22 @@
     return lax.dot_general(
         a, b, (((0,), (0,)), ((), ())), precision=highest, preferred_element_type=F32
     )
+
+
+def thirds(x):
+    high = x.astype(BF16)
+    rest = x - high.astype(F32)
+    middle = rest.astype(BF16)
+    low = (rest - middle.astype(F32)).astype(BF16)
+    return jnp.concatenate([high, middle, low], axis=0)
+
+
+def taken(x, hot):
+    rows = x.shape[0]
+    parts = lax.dot_general(
+        thirds(x), hot.astype(BF16), (((1,), (1,)), ((), ())), preferred_element_type=F32
+    )
+    return parts[:rows] + parts[rows : 2 * rows] + parts[2 * rows :]
 
 
 def turned(rows):
@@ -76,16 +93,57 @@
     return total
 
 
-def blocks_of(nel):
-    return ((0, 0, 1.0), (nel, nel, 1.0), (0, nel, 2.0))
-
-
-def squares_of(cols, rows, a, b, nel):
-    total = None
-    for c in range(3):
-        offset = cols[c][a : a + nel] - rows[c][:, b : b + nel]
-        total = offset * offset if total is None else total + offset * offset
-    return total
+def pair_tiles(turns, rows, nel, kinds):
+    sums = [None, None]
+    for h in (0, 1):
+        for t in range(nel // 8):
+            wide = [
+                [
+                    jnp.broadcast_to(turn[h][c][8 * t : 8 * t + 8], (8, nel))
+                    for c in range(3)
+                ]
+                for turn in turns
+            ]
+            for g in range(h, 2):
+                squares = []
+                for i, row in enumerate(rows):
+                    total = None
+                    for c in range(3):
+                        offset = wide[i][c] - row[g][c]
+                        total = offset * offset if total is None else total + offset * offset
+                    squares.append(total)
+                kind = int(g != h)
+                term = kinds[kind](*squares)
+                sums[kind] = term if sums[kind] is None else sums[kind] + term
+    return sums
+
+
+def summed(tile):
+    return jnp.sum(jnp.sum(tile, axis=0, keepdims=True), axis=1, keepdims=True)
+
+
+def jastrow_of(spots, turn, jas_ref, nel):
+    rows, turns = (
+        [
+            [
+                [cut(base + 3 * h + c) for c in range(3)]
+                for h in (0, 1)
+            ]
+            for base in (0, 8)
+        ]
+        for cut in (lambda r: spots[r : r + 1], lambda r: turn[:, r : r + 1])
+    )
+
+    def change(fall):
+        def term(new, old):
+            nd = jnp.sqrt(new)
+            od = jnp.sqrt(old)
+            return (nd - od) / ((1.0 + fall * nd) * (1.0 + fall * od))
+
+        return term
+
+    same, other = pair_tiles(turns, rows, nel, [change(jas_ref[2]), change(jas_ref[3])])
+    return summed(same * (0.5 * jas_ref[0]) + other * jas_ref[1])
 
 
 def in_rows(rows):
@@ -116,15 +174,17 @@
     turn = turned(jnp.concatenate(now, axis=0))
     weighted = jnp.zeros((1, 1), F32)
     for w in range(walkers):
-        ncols = [turn[:, c * walkers + w : c * walkers + w + 1] for c in range(3)]
         nrows = [now[c][w : w + 1] for c in range(3)]
-        soft = jnp.zeros((8, nel), F32)
-        for a, b, weight in blocks_of(nel):
-            squares = squares_of(ncols, nrows, a, b, nel)
-            terms = lax.rsqrt(squares + 1.0)
-            part = jnp.sum(terms.reshape(nel // 8, 8, nel), axis=0)
-            soft = soft + (part if weight == 1.0 else part * weight)
-        whole = jnp.sum(jnp.sum(soft, axis=0, keepdims=True), axis=1, keepdims=True)
+        halves = [[r[:, h * nel : (h + 1) * nel] for r in nrows] for h in (0, 1)]
+        tall = [
+            [
+                turn[h * nel : (h + 1) * nel, c * walkers + w : c * walkers + w + 1]
+                for c in range(3)
+            ]
+            for h in (0, 1)
+        ]
+        same, other = pair_tiles([tall], [halves], nel, [lambda q: lax.rsqrt(q + 1.0)] * 2)
+        whole = summed(same + 2.0 * other)
         energy = (whole - 1.0 * both) / (1.0 * both * (both - 1))
         wide = [jnp.broadcast_to(energy, (1, LANES)), jnp.zeros((7 - 3 * (both // LANES), LANES), F32)]
         spots_ref[w, :8] = jnp.concatenate(in_rows(nrows) + wide[: 1 + (3 * (both // LANES) < 7)], axis=0)
@@ -141,47 +201,6 @@
         jnp.where(rows == 0, number, jnp.where(rows == 1, weighted, 0.0)),
         0.0,
     )
-
-
-def jastrow_kernel(spots_ref, jas_ref, out_ref):
-    walkers = spots_ref.shape[0]
-    nel = LANES
-    parts = max(lax.axis_size("orb") // 2, 1)
-    share = walkers // parts
-    first = lax.div(lax.axis_index("orb"), lax.axis_size("orb") // parts) * share
-    out_ref[...] = jnp.zeros(out_ref.shape, F32)
-    for w in range(share):
-        rows = spots_ref[first + w]
-        turn = turned(rows)
-        new, old = (
-            [
-                [rows[base + 3 * h + c : base + 3 * h + c + 1] for c in range(3)]
-                for h in (0, 1)
-            ]
-            for base in (0, 8)
-        )
-        newt, oldt = (
-            [
-                [turn[:, base + 3 * h + c : base + 3 * h + c + 1] for c in range(3)]
-                for h in (0, 1)
-            ]
-            for base in (0, 8)
-        )
-        total = jnp.zeros((8, nel), F32)
-        for a, b, weight in blocks_of(nel):
-            kind = 0 if a == b else 1
-            fall = jas_ref[2 + kind]
-            osq = squares_of(oldt[a // nel], old[b // nel], 0, 0, nel)
-            nsq = squares_of(newt[a // nel], new[b // nel], 0, 0, nel)
-            od = jnp.sqrt(osq)
-            nd = jnp.sqrt(nsq)
-            terms = (nd - od) / ((1.0 + fall * nd) * (1.0 + fall * od))
-            part = jnp.sum(terms.reshape(nel // 8, 8, nel), axis=0)
-            total = total + part * (jas_ref[kind] * weight)
-        whole = jnp.sum(jnp.sum(total, axis=0, keepdims=True), axis=1, keepdims=True)
-        out_ref[pl.ds(2 + first + w, 1), :] = jnp.broadcast_to(
-            0.5 * whole, (1, out_ref.shape[1])
-        )
 
 
 def shift_kernel(pos_ref, dis_ref, order_ref, flags_ref, cen_ref, exp_ref, orb_ref, shift_ref, differ_ref):
@@ -226,14 +245,24 @@
 
 
 def partial_kernel(
-    shift_ref, order_ref, flags_ref, counts_ref, inv_ref, sla_ref, spots_ref, info_ref,
+    shift_ref, order_ref, flags_ref, counts_ref, inv_ref, sla_ref, spots_ref, info_ref, jas_ref,
     part_ref, done_ref, pair_ref, odd_ref,
 ):
     walkers, _, orbs, nel = inv_ref.shape
     moves = flags_ref.shape[2]
     cols, keep = moves_of(order_ref, flags_ref)
     hots = one_hots(cols, nel)
-    part_ref[2 * walkers * moves :, :] = info_ref[...]
+    members = lax.axis_size("orb")
+    share = walkers // members
+    first = lax.axis_index("orb") * share
+    tail = 2 * walkers * moves
+    part_ref[tail:, :] = info_ref[...]
+    for w in range(share):
+        mine = spots_ref[first + w]
+        at = tail + 2 + first + w
+        part_ref[pl.ds(at, 1), :] = jnp.broadcast_to(
+            jastrow_of(mine, turned(mine), jas_ref, nel), (1, part_ref.shape[1])
+        )
     for s in (0, 1):
         for w in range(walkers):
             i = 2 * w + s
@@ -256,10 +285,8 @@
             pay[tail + 8 * j : tail + 8 * j + 8, :] = spots_ref[source, :8]
 
 
-def add_kernel(mine_ref, other_ref, change_ref, out_ref):
-    rows = mine_ref.shape[0] - change_ref.shape[0]
-    out_ref[:rows, :] = mine_ref[:rows, :] + other_ref[:rows, :]
-    out_ref[rows:, :] = mine_ref[rows:, :] + other_ref[rows:, :] + change_ref[...]
+def add_kernel(mine_ref, other_ref, out_ref):
+    out_ref[...] = mine_ref[...] + other_ref[...]
 
 
 def update_kernel(
@@ -282,8 +309,8 @@
     for i in range(count):
         at = slice(i * moves, (i + 1) * moves)
         change = sum_ref[at, :] + got_ref[at, :] - hots[i] * keep[i]
-        coupling = nt(change, hots[i]) + eye
-        columns.append(nt(inv_ref[i // 2, i % 2], hots[i]))
+        coupling = taken(change, hots[i]) + eye
+        columns.append(taken(inv_ref[i // 2, i % 2], hots[i]))
         left.append([coupling[8 * t : 8 * t + 8] for t in range(tiles)])
         right.append([change[8 * t : 8 * t + 8] for t in range(tiles)])
     info_ref[...] = sum_ref[count * moves :, :] + got_ref[count * moves :, :]
@@ -409,14 +436,14 @@
             received(odd_i_ref, odd_s_ref)
 
 
-def call(kernel, outs, in_specs, scratch=(), us=1.0, name=None):
+def call(kernel, outs, in_specs, scratch=(), us=1.0, name=None, vmem=32 * 2**20):
     return pl.pallas_call(
         kernel,
         out_shape=outs,
         in_specs=in_specs,
         out_specs=jax.tree.map(lambda _: VMEM, outs),
         scratch_shapes=list(scratch),
-        compiler_params=pltpu.CompilerParams(vmem_limit_bytes=32 * 2**20),
+        compiler_params=pltpu.CompilerParams(vmem_limit_bytes=vmem),
         cost_estimate=pl.CostEstimate(flops=int(us * 1.1e9), bytes_accessed=2**18, transcendentals=0),
         name=name,
     )
@@ -456,6 +483,7 @@
         ),
         [VMEM, VMEM, VMEM, VMEM, SMEM],
         us=2,
+        vmem=61 * 2**20,
         name="energy",
     )(places, steps, move_order, accepted, counts)
 
@@ -489,14 +517,10 @@
             shape(tall, LANES),
             shape(tall, LANES),
         ),
-        [VMEM, VMEM, VMEM, SMEM] + [VMEM] * 4,
+        [VMEM, VMEM, VMEM, SMEM] + [VMEM] * 4 + [SMEM],
         us=2,
         name="partial",
-    )(shift, move_order, accepted, counts, inverse, slater, spots, info)
-
-    change = call(
-        jastrow_kernel, shape(INFO, wide), [VMEM, SMEM], us=1.2, name="jastrow"
-    )(spots, jastrow)
+    )(shift, move_order, accepted, counts, inverse, slater, spots, info, jastrow)
 
     total = part
     got = jnp.zeros_like(part)
@@ -508,10 +532,10 @@
             total = call(
                 add_kernel,
                 shape(count * moves + INFO, nel),
-                [VMEM] * 3,
-                us=0.7,
+                [VMEM] * 2,
+                us=0.5,
                 name="add",
-            )(total, got, change if step == 1 else jnp.zeros_like(change))
+            )(total, got)
         step *= 2
 
     pair_s = lax.ppermute(pair_s, "walkers", pairs)

time: 37.5 us -> 34.1 us (0.909)
  local copies, waits for them, and re-layouts: 3.48 us -> 0.67 us
  Pallas kernels: 12.9 us -> 12.1 us
  waiting for transfers between devices: 4.9 us -> 5.5 us
    unnamed x28 -> x26, local copies, waits for them, and re-layouts: 3.48 us -> 0.67 us
    pallas_call x2 -> x1, Pallas kernels: 1.49 us -> 0.02 us  [body(): call(add_kernel, shape(count * moves + INFO, nel), [VMEM] * 2, us=0.5, na...]
    ppermute x2, waiting for transfers between devices: 0.01 us -> 0.99 us  [body(): got = lax.ppermute(total, 'orb', partner)]
    pallas_call x1, Pallas kernels: 1.69 us -> 2.68 us  [body(): call(energy_kernel, (shape(walkers, 16, LANES), shape(INFO, wide)), [VMEM...]
    ppermute x2, starting transfers between devices: 6.04 us -> 5.16 us  [body(): got = lax.ppermute(total, 'orb', partner)]
    ppermute x1, starting transfers between devices: 0.65 us -> 1.34 us  [body(): info = lax.ppermute(info, ('walkers', 'orb'), joint)]
    ppermute x1, starting transfers between devices: 2.3 us -> 1.69 us  [body(): pair_i = lax.ppermute(pair_i, 'walkers', pairs)]
    ppermute x1, waiting for transfers between devices: 4.8 us -> 4.41 us  [body(): odd_i = lax.ppermute(odd_i, 'walkers', odds)]
  transfers between devices with their start and end apart: 7 -> 7, of which waited for: 2 -> 3; matrix products, arithmetic and copies ran while one was open for 0% -> 0% of each run, Pallas kernels for 22% -> 18%
where the time goes in v3:
time: 34.1 us; the launch traced here: 33.9 us
  starting transfers between devices  14.8 us (43%)
  Pallas kernels  12.1 us (35%)
  waiting for transfers between devices  5.5 us (16%)
  between operations  0.86 us (3%)
  local copies, waits for them, and re-layouts  0.67 us (2%)
    ppermute x2, starting transfers between devices, body(): got = lax.ppermute(total, 'orb', partner)  5.16 us
    ppermute x1, waiting for transfers between devices, body(): odd_i = lax.ppermute(odd_i, 'walkers', odds)  4.41 us
    pallas_call x1, Pallas kernels, body(): call(update_kernel, (shape(walkers, 2, orbs, nel), shape(8, nel), shape(I...  4.06 us
    pallas_call x1, Pallas kernels, body(): call(energy_kernel, (shape(walkers, 16, LANES), shape(INFO, wide)), [VMEM...  2.68 us
    ppermute x1, starting transfers between devices, body(): odd_i = lax.ppermute(odd_i, 'walkers', odds)  2.61 us
    ppermute x1, starting transfers between devices, body(): odd_s = lax.ppermute(odd_s, 'walkers', odds)  2.51 us
    pallas_call x1, Pallas kernels, body(): call(shift_kernel, shape(2, walkers * moves, orbs), [VMEM] * 7, scratch=[...  2.16 us
    ppermute x1, starting transfers between devices, body(): pair_i = lax.ppermute(pair_i, 'walkers', pairs)  1.69 us
  transfers between devices with their start and end apart: 7, of which 3 were waited for; matrix products, arithmetic and copies ran while one was open for 0% of the time, Pallas kernels for 18%

profile of v3, /device:TPU:8, one launch (start us, length us, event | category | flops | bytes accessed | tf_op | source)
XLA Modules:
  0.0 33.9 jit_solution(4917233993191650747)
XLA Ops:
  0.7 2.7 %energy.1 = (f32[4,16,128]{2,1,0:T(8,128)}, f32[8,128]{1,0:T(8,128)}) custom-call(f32[3,4,256]{2,1,0:T(4,128)} %bitcast.7, f32[3,4,256]{2,1,0:T(4,128)} %bitcast.9, s32[4,2,128]{2,1,0:T(2,128)} %order_ref.7, s32[4,2,32]{2,1,0:T(2,128)} %flags_ref.7, s32[4]{0:T(128)} %counts_ref.7), custom_call_target="tpu_custom_call" | custom-call | flops 2200000000 | bytes 262144 | tf_op jit(solution)/shard_map/energy/pallas_call | solution.py:478
  3.4 1.3 %collective-permute-start = (f32[8,128]{1,0:T(8,128)}, f32[8,128]{1,0:T(8,128)S(1)}, u32[]{:S(2)}, u32[]{:S(2)}) collective-permute-start(f32[8,128]{1,0:T(8,128)} %get-tuple-element.24), channel_id=1, source_target_pairs={{0,0},{1,9},{2,18},{3,27},{4,4},{5,13},{6,22},{7,31},{8,8},{9,1},{... | collective-permute-start | bytes 12296 | tf_op jit(solution)/shard_map/ppermute | solution.py:501
  4.8 0.0 copy-start.1
  4.8 0.0 copy-start.2
  4.8 0.0 copy-start.12
  4.8 2.2 %shift.1.shift_ref = f32[2,128,32]{2,1,0:T(8,128)S(1)} custom-call(f32[3,4,256]{2,1,0:T(4,128)S(1)} %bitcast.8, f32[3,4,256]{2,1,0:T(4,128)S(1)} %bitcast.10, s32[4,2,128]{2,1,0:T(2,128)S(1)} %copy-done.7, s32[4,2,32]{2,1,0:T(2,128)S(1)} %copy-done.8, f32[3,1024]{1,0:T(4,128)S(1)} %copy-done.3, f32[1,1024]{1,0:T(1,128)S(1)} %bitcast.11, ...), custom_call_target="tpu_custom_call" | custom-call | flops 3300000000 | bytes 262144 | tf_op jit(solution)/shard_map/shift/pallas_call | solution.py:503
  7.0 0.0 copy-start.9
  7.0 0.0 copy-start.11
  7.0 0.6 %copy-done.9 = f32[4]{0:T(128)S(1)} copy-done((f32[4]{0:T(128)S(1)}, f32[4]{0:T(128)}, u32[]{:S(2)}) %copy-start.9) | copy-done | bytes 40
  7.6 0.0 copy-done.11
  7.6 1.6 %partial.1 = (f32[264,128]{1,0:T(8,128)S(1)}, f32[4,2,32,128]{3,2,1,0:T(8,128)S(1)}, f32[144,128]{1,0:T(8,128)S(1)}, f32[144,128]{1,0:T(8,128)S(1)}) custom-call(f32[2,128,32]{2,1,0:T(8,128)S(1)} %shift.1.shift_ref, s32[4,2,128]{2,1,0:T(2,128)S(1)} %copy-done.7, s32[4,2,32]{2,1,0:T(2,128)S(1)} %copy-done.8, s32[4]{0:T(128)S(1)} %copy-done.11, ...), custom_call_target="tpu_custom_call" | custom-call | flops 2200000000 | bytes 262144 | tf_op jit(solution)/shard_map/partial/pallas_call | solution.py:512
  9.3 0.5 %collective-permute-start.1 = (f32[264,128]{1,0:T(8,128)S(1)}, f32[264,128]{1,0:T(8,128)S(1)}, u32[]{:S(2)}, u32[]{:S(2)}) collective-permute-start(f32[264,128]{1,0:T(8,128)S(1)} %get-tuple-element.25.mine_ref), channel_id=1, source_target_pairs={{0,1},{1,0},{2,3},{3,2},{4,5},{5,4},{6,7},{7,6},{8,9},{9,8},{10,11... | collective-permute-start | bytes 405512 | tf_op jit(solution)/shard_map/ppermute | solution.py:530
  9.8 1.0 %collective-permute-done.1.other_ref = f32[264,128]{1,0:T(8,128)S(1)} collective-permute-done((f32[264,128]{1,0:T(8,128)S(1)}, f32[264,128]{1,0:T(8,128)S(1)}, u32[]{:S(2)}, u32[]{:S(2)}) %collective-permute-start.1) | collective-permute-done | bytes 135200 | tf_op jit(solution)/shard_map/ppermute | solution.py:530
  10.8 4.7 %collective-permute-start.2 = (f32[264,128]{1,0:T(8,128)S(1)}, f32[264,128]{1,0:T(8,128)S(1)}, u32[]{:S(2)}, u32[]{:S(2)}) collective-permute-start(f32[264,128]{1,0:T(8,128)S(1)} %add.1.sum_ref), channel_id=1, source_target_pairs={{0,2},{1,3},{2,0},{3,1},{4,6},{5,7},{6,4},{7,5},{8,10},{9,11},{10,... | collective-permute-start | bytes 405512 | tf_op jit(solution)/shard_map/ppermute | solution.py:530
  15.5 1.5 %collective-permute-start.3 = (f32[144,128]{1,0:T(8,128)S(1)}, f32[144,128]{1,0:T(8,128)S(1)}, u32[]{:S(2)}, u32[]{:S(2)}) collective-permute-start(f32[144,128]{1,0:T(8,128)S(1)} %get-tuple-element.30), channel_id=1, source_target_pairs={{0,4},{4,0},{8,12},{12,8},{16,20},{20,16},{24,28},{28,24},{1,5},{5... | collective-permute-start | bytes 221192 | tf_op jit(solution)/shard_map/ppermute | solution.py:541
  17.0 2.5 %collective-permute-start.4 = (f32[144,128]{1,0:T(8,128)S(1)}, f32[144,128]{1,0:T(8,128)S(1)}, u32[]{:S(2)}, u32[]{:S(2)}) collective-permute-start(f32[144,128]{1,0:T(8,128)S(1)} %get-tuple-element.31), channel_id=1, source_target_pairs={{4,8},{12,16},{20,24},{8,4},{16,12},{24,20},{5,9},{13,17},{21,25},... | collective-permute-start | bytes 221192 | tf_op jit(solution)/shard_map/ppermute | solution.py:542
  19.5 0.0 collective-permute-done.2.got_ref
  19.5 4.1 %update.1 = (f32[4,2,32,128]{3,2,1,0:T(8,128)S(1)}, f32[8,128]{1,0:T(8,128)S(1)}, f32[8,128]{1,0:T(8,128)S(1)}, f32[144,128]{1,0:T(8,128)S(1)}, f32[144,128]{1,0:T(8,128)S(1)}) custom-call(f32[264,128]{1,0:T(8,128)S(1)} %add.1.sum_ref, f32[264,128]{1,0:T(8,128)S(1)} %collective-permute-done.2.got_ref, f32[4,2,32,128]{3,2,1,0:T(8,128)S(1)} %copy-done.2, ...), custom_call_target="tpu_custom_call" | custom-call | flops 4400000000 | bytes 262144 | tf_op jit(solution)/shard_map/update/pallas_call | solution.py:544
  23.6 1.7 %collective-permute-start.5 = (f32[144,128]{1,0:T(8,128)S(1)}, f32[144,128]{1,0:T(8,128)S(1)}, u32[]{:S(2)}, u32[]{:S(2)}) collective-permute-start(f32[144,128]{1,0:T(8,128)S(1)} %get-tuple-element.32), channel_id=1, source_target_pairs={{0,4},{4,0},{8,12},{12,8},{16,20},{20,16},{24,28},{28,24},{1,5},{5... | collective-permute-start | bytes 221192 | tf_op jit(solution)/shard_map/ppermute | solution.py:558
  25.3 2.6 %collective-permute-start.6 = (f32[144,128]{1,0:T(8,128)S(1)}, f32[144,128]{1,0:T(8,128)S(1)}, u32[]{:S(2)}, u32[]{:S(2)}) collective-permute-start(f32[144,128]{1,0:T(8,128)S(1)} %get-tuple-element.33), channel_id=1, source_target_pairs={{4,8},{12,16},{20,24},{8,4},{16,12},{24,20},{5,9},{13,17},{21,25},... | collective-permute-start | bytes 221192 | tf_op jit(solution)/shard_map/ppermute | solution.py:559
  27.9 0.0 collective-permute-done.4.odd_s_ref
  27.9 0.1 collective-permute-done.5.pair_i_ref
  28.0 4.4 %collective-permute-done.6.odd_i_ref = f32[144,128]{1,0:T(8,128)S(1)} collective-permute-done((f32[144,128]{1,0:T(8,128)S(1)}, f32[144,128]{1,0:T(8,128)S(1)}, u32[]{:S(2)}, u32[]{:S(2)}) %collective-permute-start.6) | collective-permute-done | bytes 73760 | tf_op jit(solution)/shard_map/ppermute | solution.py:559
  32.4 1.5 %place.1 = (f32[4,2,32,128]{3,2,1,0:T(8,128)}, f32[4,2,32,128]{3,2,1,0:T(8,128)}, f32[3,4,256]{2,1,0:T(4,128)}, f32[1,4]{1,0:T(1,128)}, f32[1,4]{1,0:T(1,128)}, /*index=5*/f32[1,1]{1,0:T(1,128)}) custom-call(s32[4]{0:T(128)S(1)} %copy-done.11, f32[4,2,32,128]{3,2,1,0:T(8,128)S(1)} %get-tuple-element.26.cur_ref, ...), custom_call_target="tpu_custom_call" | custom-call | flops 1650000000 | bytes 262144 | tf_op jit(solution)/shard_map/place/pallas_call | solution.py:561
  (22 shorter events, 0.1 us)
Async XLA Ops:
  0.6 4.1 %copy-start = (f32[2,32,1024]{2,1,0:T(8,128)S(1)}, f32[2,32,1024]{2,1,0:T(8,128)}, u32[]{:S(2)}) copy-start(f32[2,32,1024]{2,1,0:T(8,128)} %orb_ref.1) | copy-start | bytes 786436
  0.6 4.1 %copy-start.3 = (f32[3,1024]{1,0:T(4,128)S(1)}, f32[3,1024]{1,0:T(4,128)}, u32[]{:S(2)}) copy-start(f32[3,1024]{1,0:T(4,128)} %cen_ref.1) | copy-start | bytes 36868
  0.7 4.1 %copy-start.4 = (f32[4,3,256]{2,0,1:T(4,128)S(1)}, f32[4,3,256]{2,0,1:T(4,128)}, u32[]{:S(2)}) copy-start(f32[4,3,256]{2,0,1:T(4,128)} %param.14) | copy-start | bytes 36868
  0.7 4.1 %copy-start.5 = (f32[4,3,256]{2,0,1:T(4,128)S(1)}, f32[4,3,256]{2,0,1:T(4,128)}, u32[]{:S(2)}) copy-start(f32[4,3,256]{2,0,1:T(4,128)} %param.15) | copy-start | bytes 36868
  0.7 4.1 %copy-start.6 = (f32[1024]{0:T(1024)S(1)}, f32[1024]{0:T(1024)}, u32[]{:S(2)}) copy-start(f32[1024]{0:T(1024)} %param.21) | copy-start | bytes 12292
  0.7 4.1 %copy-start.7 = (s32[4,2,128]{2,1,0:T(2,128)S(1)}, s32[4,2,128]{2,1,0:T(2,128)}, u32[]{:S(2)}) copy-start(s32[4,2,128]{2,1,0:T(2,128)} %order_ref.7) | copy-start | bytes 12292
  0.7 4.1 %copy-start.8 = (s32[4,2,32]{2,1,0:T(2,128)S(1)}, s32[4,2,32]{2,1,0:T(2,128)}, u32[]{:S(2)}) copy-start(s32[4,2,32]{2,1,0:T(2,128)} %flags_ref.7) | copy-start | bytes 3076
  3.4 3.6 %collective-permute-start = (f32[8,128]{1,0:T(8,128)}, f32[8,128]{1,0:T(8,128)S(1)}, u32[]{:S(2)}, u32[]{:S(2)}) collective-permute-start(f32[8,128]{1,0:T(8,128)} %get-tuple-element.24), channel_id=1, source_target_pairs={{0,0},{1,9},{2,18},{3,27},{4,4},{5,13},{6,22},{7,31},{8,8},{9,1},{... | collective-permute-start | bytes 12296 | tf_op jit(solution)/shard_map/ppermute | solution.py:501
  4.8 2.2 %copy-start.1 = (f32[4,2,32,128]{3,2,1,0:T(8,128)S(1)}, f32[4,2,32,128]{3,2,1,0:T(8,128)}, u32[]{:S(2)}) copy-start(f32[4,2,32,128]{3,2,1,0:T(8,128)} %sla_ref.1) | copy-start | bytes 393220
  4.8 2.2 %copy-start.2 = (f32[4,2,32,128]{3,2,1,0:T(8,128)S(1)}, f32[4,2,32,128]{3,2,1,0:T(8,128)}, u32[]{:S(2)}) copy-start(f32[4,2,32,128]{3,2,1,0:T(8,128)} %inv_ref.3) | copy-start | bytes 393220
  4.8 2.2 %copy-start.12 = (f32[4,16,128]{2,1,0:T(8,128)S(1)}, f32[4,16,128]{2,1,0:T(8,128)}, u32[]{:S(2)}) copy-start(f32[4,16,128]{2,1,0:T(8,128)} %get-tuple-element.23.spots_ref) | copy-start | bytes 98308
  7.0 0.7 %copy-start.9 = (f32[4]{0:T(128)S(1)}, f32[4]{0:T(128)}, u32[]{:S(2)}) copy-start(f32[4]{0:T(128)} %jas_ref.1) | copy-start | bytes 52
  7.0 0.7 %copy-start.11 = (s32[4]{0:T(128)S(1)}, s32[4]{0:T(128)}, u32[]{:S(2)}) copy-start(s32[4]{0:T(128)} %counts_ref.7) | copy-start | bytes 52
  9.3 1.5 %collective-permute-start.1 = (f32[264,128]{1,0:T(8,128)S(1)}, f32[264,128]{1,0:T(8,128)S(1)}, u32[]{:S(2)}, u32[]{:S(2)}) collective-permute-start(f32[264,128]{1,0:T(8,128)S(1)} %get-tuple-element.25.mine_ref), channel_id=1, source_target_pairs={{0,1},{1,0},{2,3},{3,2},{4,5},{5,4},{6,7},{7,6},{8,9},{9,8},{10,11... | collective-permute-start | bytes 405512 | tf_op jit(solution)/shard_map/ppermute | solution.py:530
  10.8 8.7 %collective-permute-start.2 = (f32[264,128]{1,0:T(8,128)S(1)}, f32[264,128]{1,0:T(8,128)S(1)}, u32[]{:S(2)}, u32[]{:S(2)}) collective-permute-start(f32[264,128]{1,0:T(8,128)S(1)} %add.1.sum_ref), channel_id=1, source_target_pairs={{0,2},{1,3},{2,0},{3,1},{4,6},{5,7},{6,4},{7,5},{8,10},{9,11},{10,... | collective-permute-start | bytes 405512 | tf_op jit(solution)/shard_map/ppermute | solution.py:530
  15.5 4.0 %copy-start.10 = (f32[4]{0:T(128)S(1)}, f32[4]{0:T(128)}, u32[]{:S(2)}) copy-start(f32[4]{0:T(128)} %amp_ref.1) | copy-start | bytes 52
  15.5 12.4 %collective-permute-start.3 = (f32[144,128]{1,0:T(8,128)S(1)}, f32[144,128]{1,0:T(8,128)S(1)}, u32[]{:S(2)}, u32[]{:S(2)}) collective-permute-start(f32[144,128]{1,0:T(8,128)S(1)} %get-tuple-element.30), channel_id=1, source_target_pairs={{0,4},{4,0},{8,12},{12,8},{16,20},{20,16},{24,28},{28,24},{1,5},{5... | collective-permute-start | bytes 221192 | tf_op jit(solution)/shard_map/ppermute | solution.py:541
  17.0 10.9 %collective-permute-start.4 = (f32[144,128]{1,0:T(8,128)S(1)}, f32[144,128]{1,0:T(8,128)S(1)}, u32[]{:S(2)}, u32[]{:S(2)}) collective-permute-start(f32[144,128]{1,0:T(8,128)S(1)} %get-tuple-element.31), channel_id=1, source_target_pairs={{4,8},{12,16},{20,24},{8,4},{16,12},{24,20},{5,9},{13,17},{21,25},... | collective-permute-start | bytes 221192 | tf_op jit(solution)/shard_map/ppermute | solution.py:542
  23.6 4.4 %collective-permute-start.5 = (f32[144,128]{1,0:T(8,128)S(1)}, f32[144,128]{1,0:T(8,128)S(1)}, u32[]{:S(2)}, u32[]{:S(2)}) collective-permute-start(f32[144,128]{1,0:T(8,128)S(1)} %get-tuple-element.32), channel_id=1, source_target_pairs={{0,4},{4,0},{8,12},{12,8},{16,20},{20,16},{24,28},{28,24},{1,5},{5... | collective-permute-start | bytes 221192 | tf_op jit(solution)/shard_map/ppermute | solution.py:558
  25.3 7.1 %collective-permute-start.6 = (f32[144,128]{1,0:T(8,128)S(1)}, f32[144,128]{1,0:T(8,128)S(1)}, u32[]{:S(2)}, u32[]{:S(2)}) collective-permute-start(f32[144,128]{1,0:T(8,128)S(1)} %get-tuple-element.33), channel_id=1, source_target_pairs={{4,8},{12,16},{20,24},{8,4},{16,12},{24,20},{5,9},{13,17},{21,25},... | collective-permute-start | bytes 221192 | tf_op jit(solution)/shard_map/ppermute | solution.py:559

commit v4 on v3

--- a/solution.py
+++ b/solution.py
@@ -9,26 +9,15 @@
 BF16 = jnp.bfloat16
 highest = lax.Precision.HIGHEST
 VMEM = pl.BlockSpec(memory_space=pltpu.VMEM)
+HBM = pl.BlockSpec(memory_space=pl.ANY)
 SMEM = pl.BlockSpec(memory_space=pltpu.SMEM)
 LANES = 128
 INFO = 8
 
 
-def nn(a, b):
-    return lax.dot_general(
-        a, b, (((1,), (0,)), ((), ())), precision=highest, preferred_element_type=F32
-    )
-
-
 def nt(a, b):
     return lax.dot_general(
         a, b, (((1,), (1,)), ((), ())), precision=highest, preferred_element_type=F32
-    )
-
-
-def tn(a, b):
-    return lax.dot_general(
-        a, b, (((0,), (0,)), ((), ())), precision=highest, preferred_element_type=F32
     )
 
 
@@ -38,6 +27,53 @@
     middle = rest.astype(BF16)
     low = (rest - middle.astype(F32)).astype(BF16)
     return jnp.concatenate([high, middle, low], axis=0)
+
+
+def parted(x):
+    high = x.astype(BF16)
+    return jnp.concatenate([high, (x - high.astype(F32)).astype(BF16)], axis=0)
+
+
+def product(a, b):
+    rows = a.shape[0]
+    inner = b.shape[0]
+    left = parted(a)
+    right = parted(b)
+    whole = None
+    for part in (right[:inner], right[inner:]):
+        both = lax.dot_general(
+            left, part, (((1,), (0,)), ((), ())), preferred_element_type=F32
+        )
+        both = both[:rows] + both[rows:]
+        whole = both if whole is None else whole + both
+    return whole
+
+
+def product_nt(a, b):
+    rows, cols = a.shape[0], b.shape[0]
+    both = lax.dot_general(
+        parted(a), parted(b), (((1,), (1,)), ((), ())), preferred_element_type=F32
+    )
+    both = both[:rows] + both[rows:]
+    return both[:, :cols] + both[:, cols:]
+
+
+def taken_nt(hot, x):
+    rows = x.shape[0]
+    parts = lax.dot_general(
+        hot.astype(BF16), thirds(x), (((1,), (1,)), ((), ())), preferred_element_type=F32
+    )
+    return parts[:, :rows] + parts[:, rows : 2 * rows] + parts[:, 2 * rows :]
+
+
+def spread(x, hot):
+    hot = hot.astype(BF16)
+    return lax.dot_general(
+        thirds(x),
+        jnp.concatenate([hot] * 3, axis=0),
+        (((0,), (0,)), ((), ())),
+        preferred_element_type=F32,
+    )
 
 
 def taken(x, hot):
@@ -241,7 +277,7 @@
                     rate * nsq
                 ) - jnp.exp(rate * osq)
     for s in (0, 1):
-        shift_ref[s] = nt(differ_ref[s], orb_ref[s])
+        shift_ref[s] = product_nt(differ_ref[s], orb_ref[s])
 
 
 def partial_kernel(
@@ -267,10 +303,10 @@
         for w in range(walkers):
             i = 2 * w + s
             mine = shift_ref[s, w * moves : (w + 1) * moves, :]
-            proposed = mine + nt(hots[i], sla_ref[w, s])
-            part = nn(proposed, inv_ref[w, s])
+            proposed = mine + taken_nt(hots[i], sla_ref[w, s])
+            part = product(proposed, inv_ref[w, s])
             part_ref[i * moves : (i + 1) * moves, :] = part * keep[i]
-            done_ref[w, s] = sla_ref[w, s] + tn(mine, hots[i] * keep[i])
+            done_ref[w, s] = sla_ref[w, s] + spread(mine, hots[i] * keep[i])
     half = walkers // 2
     per = 2 * orbs
     tail = half * per
@@ -317,28 +353,43 @@
     lanes = lax.broadcasted_iota(jnp.int32, (1, nel), 1)
     sub = lax.broadcasted_iota(jnp.int32, (8, nel), 0)
     pivots = [jnp.ones((1, nel), F32) for _ in range(count)]
-    for k in range(moves):
+    for k in range(0, moves, 2):
         own, line = k // 8, k % 8
         for i in range(count):
             wide = [
-                jnp.broadcast_to(left[i][t][:, k : k + 1], (8, nel)) for t in range(tiles)
+                [jnp.broadcast_to(left[i][t][:, c : c + 1], (8, nel)) for t in range(tiles)]
+                for c in (k, k + 1)
             ]
-            pivot = wide[own][line : line + 1]
-            pivots[i] = jnp.where(lanes == k, pivot, pivots[i])
-            scale = 1.0 / pivot
-            lrow = left[i][own][line : line + 1] * scale[:, :moves]
-            rrow = right[i][own][line : line + 1] * scale
+            a, b = (wide[c][own][line : line + 1] for c in (0, 1))
+            c, d = (wide[c][own][line + 1 : line + 2] for c in (0, 1))
+            det = a * d - b * c
+            pivots[i] = jnp.where(lanes == k, det, pivots[i])
+            scale = 1.0 / det
+            new = []
+            for side, width in ((left, moves), (right, nel)):
+                upper = side[i][own][line : line + 1]
+                lower = side[i][own][line + 1 : line + 2]
+                new.append(
+                    (
+                        (d[:, :width] * upper - b[:, :width] * lower) * scale[:, :width],
+                        (a[:, :width] * lower - c[:, :width] * upper) * scale[:, :width],
+                    )
+                )
             for t in range(tiles):
-                nl = left[i][t] - wide[t][:, :moves] * lrow
-                nr = right[i][t] - wide[t] * rrow
-                if t == own:
-                    nl = jnp.where(sub[:, :moves] == line, lrow, nl)
-                    nr = jnp.where(sub == line, rrow, nr)
-                left[i][t] = nl
-                right[i][t] = nr
+                for side, width, (upper, lower) in ((left, moves, new[0]), (right, nel, new[1])):
+                    tile = (
+                        side[i][t] - wide[0][t][:, :width] * upper - wide[1][t][:, :width] * lower
+                    )
+                    if t == own:
+                        tile = jnp.where(
+                            sub[:, :width] == line,
+                            upper,
+                            jnp.where(sub[:, :width] == line + 1, lower, tile),
+                        )
+                    side[i][t] = tile
     for i in range(count):
         solved = jnp.concatenate(right[i], axis=0)
-        cur_ref[i // 2, i % 2] = inv_ref[i // 2, i % 2] - nn(columns[i], solved)
+        cur_ref[i // 2, i % 2] = inv_ref[i // 2, i % 2] - product(columns[i], solved)
     log_ref[...] = jnp.zeros(log_ref.shape, F32)
     for w in range(walkers):
         both = jnp.log(jnp.abs(pivots[2 * w])) + jnp.log(jnp.abs(pivots[2 * w + 1]))
@@ -367,7 +418,7 @@
 def place_kernel(
     counts_ref, cur_ref, done_ref, spots_ref, log_ref, info_ref,
     pair_s_ref, odd_s_ref, pair_i_ref, odd_i_ref,
-    inv_out, sla_out, pos_out, log_out, energy_out, mean_out,
+    inv_out, sla_out, pos_out, log_out, energy_out, mean_out, sems,
 ):
     walkers, _, orbs, nel = cur_ref.shape
     width = pos_out.shape[2] // LANES
@@ -387,8 +438,8 @@
 
     def put(j, inverse, slater, spot, log):
         for s in (0, 1):
-            inv_out[j, s] = inverse(s)
-            sla_out[j, s] = slater(s)
+            pltpu.make_async_copy(inverse(s), inv_out.at[j, s], sems.at[j, s, 0]).start()
+            pltpu.make_async_copy(slater(s), sla_out.at[j, s], sems.at[j, s, 1]).start()
         for c in range(3):
             for h in range(width):
                 pos_out[c, j : j + 1, h * LANES : (h + 1) * LANES] = spot[3 * h + c : 3 * h + c + 1]
@@ -409,8 +460,8 @@
             w = pick(counts_ref, index)
             put(
                 j,
-                lambda s: cur_ref[w, s],
-                lambda s: done_ref[w, s],
+                lambda s: cur_ref.at[w, s],
+                lambda s: done_ref.at[w, s],
                 spots_ref[w, :8],
                 log_ref[pl.ds(w, 1), :],
             )
@@ -419,8 +470,8 @@
             i = jnp.clip(jnp.where(low, index + half, index - number), 0, half - 1)
             put(
                 j,
-                lambda s: late[pl.ds(pl.multiple_of(i * per + s * orbs, 8), orbs), :],
-                lambda s: early[pl.ds(pl.multiple_of(i * per + s * orbs, 8), orbs), :],
+                lambda s: late.at[pl.ds(pl.multiple_of(i * per + s * orbs, 8), orbs), :],
+                lambda s: early.at[pl.ds(pl.multiple_of(i * per + s * orbs, 8), orbs), :],
                 early[pl.ds(pl.multiple_of(tail + i * 8, 8), 8), :],
                 late[pl.ds(tail + INFO + i, 1), :],
             )
@@ -435,13 +486,18 @@
         def _():
             received(odd_i_ref, odd_s_ref)
 
-
-def call(kernel, outs, in_specs, scratch=(), us=1.0, name=None, vmem=32 * 2**20):
+    for j in range(walkers):
+        for s in (0, 1):
+            pltpu.make_async_copy(cur_ref.at[0, s], inv_out.at[j, s], sems.at[j, s, 0]).wait()
+            pltpu.make_async_copy(done_ref.at[0, s], sla_out.at[j, s], sems.at[j, s, 1]).wait()
+
+
+def call(kernel, outs, in_specs, scratch=(), us=1.0, name=None, out_specs=None, vmem=32 * 2**20):
     return pl.pallas_call(
         kernel,
         out_shape=outs,
         in_specs=in_specs,
-        out_specs=jax.tree.map(lambda _: VMEM, outs),
+        out_specs=jax.tree.map(lambda _: VMEM, outs) if out_specs is None else out_specs,
         scratch_shapes=list(scratch),
         compiler_params=pltpu.CompilerParams(vmem_limit_bytes=vmem),
         cost_estimate=pl.CostEstimate(flops=int(us * 1.1e9), bytes_accessed=2**18, transcendentals=0),
@@ -569,6 +625,8 @@
             shape(1, 1),
         ),
         [SMEM] + [VMEM] * 9,
+        out_specs=(HBM, HBM, VMEM, VMEM, VMEM, VMEM),
+        scratch=[pltpu.SemaphoreType.DMA((walkers, 2, 2))],
         us=1.5,
         name="place",
     )(counts, current, done, spots, logs, info, pair_s, odd_s, pair_i, odd_i)

time: 34.1 us -> 33.2 us (0.974)
  Pallas kernels: 12.1 us -> 10.7 us
  waiting for transfers between devices: 5.5 us -> 5.91 us
    pallas_call x1, Pallas kernels: 4.06 us -> 2.75 us  [body(): call(update_kernel, (shape(walkers, 2, orbs, nel), shape(8, nel), shape(I...]
    pallas_call x1, Pallas kernels: 1.5 us -> 2.15 us  [body(): call(place_kernel, (shape(walkers, 2, orbs, nel), shape(walkers, 2, orbs,...]
    pallas_call x1, Pallas kernels: 2.16 us -> 1.74 us  [body(): call(shift_kernel, shape(2, walkers * moves, orbs), [VMEM] * 7, scratch=[...]
    ppermute x1, starting transfers between devices: 2.61 us -> 2.2 us  [body(): odd_i = lax.ppermute(odd_i, 'walkers', odds)]
    ppermute x1, starting transfers between devices: 1.69 us -> 2.1 us  [body(): pair_i = lax.ppermute(pair_i, 'walkers', pairs)]
    ppermute x1, waiting for transfers between devices: 4.41 us -> 4.8 us  [body(): odd_i = lax.ppermute(odd_i, 'walkers', odds)]
  transfers between devices with their start and end apart: 7 -> 7, of which waited for: 3 -> 3; matrix products, arithmetic and copies ran while one was open for 0% -> 0% of each run, Pallas kernels for 18% -> 14%
where the time goes in v4:
time: 33.2 us; the launch traced here: 32.9 us
  starting transfers between devices  14.8 us (45%)
  Pallas kernels  10.7 us (32%)
  waiting for transfers between devices  5.91 us (18%)
  between operations  0.86 us (3%)
  local copies, waits for them, and re-layouts  0.67 us (2%)
    ppermute x2, starting transfers between devices, body(): got = lax.ppermute(total, 'orb', partner)  5.12 us
    ppermute x1, waiting for transfers between devices, body(): odd_i = lax.ppermute(odd_i, 'walkers', odds)  4.8 us
    pallas_call x1, Pallas kernels, body(): call(update_kernel, (shape(walkers, 2, orbs, nel), shape(8, nel), shape(I...  2.75 us
    pallas_call x1, Pallas kernels, body(): call(energy_kernel, (shape(walkers, 16, LANES), shape(INFO, wide)), [VMEM...  2.68 us
    ppermute x1, starting transfers between devices, body(): odd_s = lax.ppermute(odd_s, 'walkers', odds)  2.51 us
    ppermute x1, starting transfers between devices, body(): odd_i = lax.ppermute(odd_i, 'walkers', odds)  2.2 us
    pallas_call x1, Pallas kernels, body(): call(place_kernel, (shape(walkers, 2, orbs, nel), shape(walkers, 2, orbs,...  2.15 us
    ppermute x1, starting transfers between devices, body(): pair_i = lax.ppermute(pair_i, 'walkers', pairs)  2.1 us
  transfers between devices with their start and end apart: 7, of which 3 were waited for; matrix products, arithmetic and copies ran while one was open for 0% of the time, Pallas kernels for 14%

profile of v4, /device:TPU:8, one launch (start us, length us, event | category | flops | bytes accessed | tf_op | source)
XLA Modules:
  0.0 32.9 jit_solution(13515542379553773447)
XLA Ops:
  0.7 2.7 %energy.1 = (f32[4,16,128]{2,1,0:T(8,128)}, f32[8,128]{1,0:T(8,128)}) custom-call(f32[3,4,256]{2,1,0:T(4,128)} %bitcast.7, f32[3,4,256]{2,1,0:T(4,128)} %bitcast.9, s32[4,2,128]{2,1,0:T(2,128)} %order_ref.7, s32[4,2,32]{2,1,0:T(2,128)} %flags_ref.7, s32[4]{0:T(128)} %counts_ref.7), custom_call_target="tpu_custom_call" | custom-call | flops 2200000000 | bytes 262144 | tf_op jit(solution)/shard_map/energy/pallas_call | solution.py:534
  3.4 1.3 %collective-permute-start = (f32[8,128]{1,0:T(8,128)}, f32[8,128]{1,0:T(8,128)S(1)}, u32[]{:S(2)}, u32[]{:S(2)}) collective-permute-start(f32[8,128]{1,0:T(8,128)} %get-tuple-element.24), channel_id=1, source_target_pairs={{0,0},{1,9},{2,18},{3,27},{4,4},{5,13},{6,22},{7,31},{8,8},{9,1},{... | collective-permute-start | bytes 12296 | tf_op jit(solution)/shard_map/ppermute | solution.py:557
  4.8 0.0 copy-start.1
  4.8 0.0 copy-start.2
  4.8 0.0 copy-start.12
  4.8 1.7 %shift.1.shift_ref = f32[2,128,32]{2,1,0:T(8,128)S(1)} custom-call(f32[3,4,256]{2,1,0:T(4,128)S(1)} %bitcast.8, f32[3,4,256]{2,1,0:T(4,128)S(1)} %bitcast.10, s32[4,2,128]{2,1,0:T(2,128)S(1)} %copy-done.7, s32[4,2,32]{2,1,0:T(2,128)S(1)} %copy-done.8, f32[3,1024]{1,0:T(4,128)S(1)} %copy-done.3, f32[1,1024]{1,0:T(1,128)S(1)} %bitcast.11, ...), custom_call_target="tpu_custom_call" | custom-call | flops 3300000000 | bytes 262144 | tf_op jit(solution)/shard_map/shift/pallas_call | solution.py:559
  6.5 0.0 copy-start.9
  6.6 0.0 copy-start.11
  6.6 0.6 %copy-done.9 = f32[4]{0:T(128)S(1)} copy-done((f32[4]{0:T(128)S(1)}, f32[4]{0:T(128)}, u32[]{:S(2)}) %copy-start.9) | copy-done | bytes 40
  7.2 0.0 copy-done.11
  7.2 1.4 %partial.1 = (f32[264,128]{1,0:T(8,128)S(1)}, f32[4,2,32,128]{3,2,1,0:T(8,128)S(1)}, f32[144,128]{1,0:T(8,128)S(1)}, f32[144,128]{1,0:T(8,128)S(1)}) custom-call(f32[2,128,32]{2,1,0:T(8,128)S(1)} %shift.1.shift_ref, s32[4,2,128]{2,1,0:T(2,128)S(1)} %copy-done.7, s32[4,2,32]{2,1,0:T(2,128)S(1)} %copy-done.8, s32[4]{0:T(128)S(1)} %copy-done.11, ...), custom_call_target="tpu_custom_call" | custom-call | flops 2200000000 | bytes 262144 | tf_op jit(solution)/shard_map/partial/pallas_call | solution.py:568
  8.6 0.6 %collective-permute-start.1 = (f32[264,128]{1,0:T(8,128)S(1)}, f32[264,128]{1,0:T(8,128)S(1)}, u32[]{:S(2)}, u32[]{:S(2)}) collective-permute-start(f32[264,128]{1,0:T(8,128)S(1)} %get-tuple-element.25.mine_ref), channel_id=1, source_target_pairs={{0,1},{1,0},{2,3},{3,2},{4,5},{5,4},{6,7},{7,6},{8,9},{9,8},{10,11... | collective-permute-start | bytes 405512 | tf_op jit(solution)/shard_map/ppermute | solution.py:586
  9.2 1.0 %collective-permute-done.1.other_ref = f32[264,128]{1,0:T(8,128)S(1)} collective-permute-done((f32[264,128]{1,0:T(8,128)S(1)}, f32[264,128]{1,0:T(8,128)S(1)}, u32[]{:S(2)}, u32[]{:S(2)}) %collective-permute-start.1) | collective-permute-done | bytes 135200 | tf_op jit(solution)/shard_map/ppermute | solution.py:586
  10.2 4.5 %collective-permute-start.2 = (f32[264,128]{1,0:T(8,128)S(1)}, f32[264,128]{1,0:T(8,128)S(1)}, u32[]{:S(2)}, u32[]{:S(2)}) collective-permute-start(f32[264,128]{1,0:T(8,128)S(1)} %add.1.sum_ref), channel_id=1, source_target_pairs={{0,2},{1,3},{2,0},{3,1},{4,6},{5,7},{6,4},{7,5},{8,10},{9,11},{10,... | collective-permute-start | bytes 405512 | tf_op jit(solution)/shard_map/ppermute | solution.py:586
  14.7 1.5 %collective-permute-start.3 = (f32[144,128]{1,0:T(8,128)S(1)}, f32[144,128]{1,0:T(8,128)S(1)}, u32[]{:S(2)}, u32[]{:S(2)}) collective-permute-start(f32[144,128]{1,0:T(8,128)S(1)} %get-tuple-element.30), channel_id=1, source_target_pairs={{0,4},{4,0},{8,12},{12,8},{16,20},{20,16},{24,28},{28,24},{1,5},{5... | collective-permute-start | bytes 221192 | tf_op jit(solution)/shard_map/ppermute | solution.py:597
  16.3 2.5 %collective-permute-start.4 = (f32[144,128]{1,0:T(8,128)S(1)}, f32[144,128]{1,0:T(8,128)S(1)}, u32[]{:S(2)}, u32[]{:S(2)}) collective-permute-start(f32[144,128]{1,0:T(8,128)S(1)} %get-tuple-element.31), channel_id=1, source_target_pairs={{4,8},{12,16},{20,24},{8,4},{16,12},{24,20},{5,9},{13,17},{21,25},... | collective-permute-start | bytes 221192 | tf_op jit(solution)/shard_map/ppermute | solution.py:598
  18.8 0.0 collective-permute-done.2.got_ref
  18.8 2.8 %update.1 = (f32[4,2,32,128]{3,2,1,0:T(8,128)S(1)}, f32[8,128]{1,0:T(8,128)S(1)}, f32[8,128]{1,0:T(8,128)S(1)}, f32[144,128]{1,0:T(8,128)S(1)}, f32[144,128]{1,0:T(8,128)S(1)}) custom-call(f32[264,128]{1,0:T(8,128)S(1)} %add.1.sum_ref, f32[264,128]{1,0:T(8,128)S(1)} %collective-permute-done.2.got_ref, f32[4,2,32,128]{3,2,1,0:T(8,128)S(1)} %copy-done.2, ...), custom_call_target="tpu_custom_call" | custom-call | flops 4400000000 | bytes 262144 | tf_op jit(solution)/shard_map/update/pallas_call | solution.py:600
  21.6 2.1 %collective-permute-start.5 = (f32[144,128]{1,0:T(8,128)S(1)}, f32[144,128]{1,0:T(8,128)S(1)}, u32[]{:S(2)}, u32[]{:S(2)}) collective-permute-start(f32[144,128]{1,0:T(8,128)S(1)} %get-tuple-element.32), channel_id=1, source_target_pairs={{0,4},{4,0},{8,12},{12,8},{16,20},{20,16},{24,28},{28,24},{1,5},{5... | collective-permute-start | bytes 221192 | tf_op jit(solution)/shard_map/ppermute | solution.py:614
  23.7 2.2 %collective-permute-start.6 = (f32[144,128]{1,0:T(8,128)S(1)}, f32[144,128]{1,0:T(8,128)S(1)}, u32[]{:S(2)}, u32[]{:S(2)}) collective-permute-start(f32[144,128]{1,0:T(8,128)S(1)} %get-tuple-element.33), channel_id=1, source_target_pairs={{4,8},{12,16},{20,24},{8,4},{16,12},{24,20},{5,9},{13,17},{21,25},... | collective-permute-start | bytes 221192 | tf_op jit(solution)/shard_map/ppermute | solution.py:615
  25.9 0.0 collective-permute-done.3.pair_s_ref
  25.9 0.1 collective-permute-done.5.pair_i_ref
  26.0 4.8 %collective-permute-done.6.odd_i_ref = f32[144,128]{1,0:T(8,128)S(1)} collective-permute-done((f32[144,128]{1,0:T(8,128)S(1)}, f32[144,128]{1,0:T(8,128)S(1)}, u32[]{:S(2)}, u32[]{:S(2)}) %collective-permute-start.6) | collective-permute-done | bytes 73760 | tf_op jit(solution)/shard_map/ppermute | solution.py:615
  30.8 2.2 %place.1 = (f32[4,2,32,128]{3,2,1,0:T(8,128)}, f32[4,2,32,128]{3,2,1,0:T(8,128)}, f32[3,4,256]{2,1,0:T(4,128)}, f32[1,4]{1,0:T(1,128)}, f32[1,4]{1,0:T(1,128)}, /*index=5*/f32[1,1]{1,0:T(1,128)}) custom-call(s32[4]{0:T(128)S(1)} %copy-done.11, f32[4,2,32,128]{3,2,1,0:T(8,128)S(1)} %get-tuple-element.26.cur_ref, ...), custom_call_target="tpu_custom_call" | custom-call | flops 1650000000 | bytes 262144 | tf_op jit(solution)/shard_map/place/pallas_call | solution.py:617
  (22 shorter events, 0.1 us)
Async XLA Ops:
  0.6 4.1 %copy-start = (f32[2,32,1024]{2,1,0:T(8,128)S(1)}, f32[2,32,1024]{2,1,0:T(8,128)}, u32[]{:S(2)}) copy-start(f32[2,32,1024]{2,1,0:T(8,128)} %orb_ref.1) | copy-start | bytes 786436
  0.6 4.1 %copy-start.3 = (f32[3,1024]{1,0:T(4,128)S(1)}, f32[3,1024]{1,0:T(4,128)}, u32[]{:S(2)}) copy-start(f32[3,1024]{1,0:T(4,128)} %cen_ref.1) | copy-start | bytes 36868
  0.7 4.1 %copy-start.4 = (f32[4,3,256]{2,0,1:T(4,128)S(1)}, f32[4,3,256]{2,0,1:T(4,128)}, u32[]{:S(2)}) copy-start(f32[4,3,256]{2,0,1:T(4,128)} %param.14) | copy-start | bytes 36868
  0.7 4.1 %copy-start.5 = (f32[4,3,256]{2,0,1:T(4,128)S(1)}, f32[4,3,256]{2,0,1:T(4,128)}, u32[]{:S(2)}) copy-start(f32[4,3,256]{2,0,1:T(4,128)} %param.15) | copy-start | bytes 36868
  0.7 4.1 %copy-start.6 = (f32[1024]{0:T(1024)S(1)}, f32[1024]{0:T(1024)}, u32[]{:S(2)}) copy-start(f32[1024]{0:T(1024)} %param.21) | copy-start | bytes 12292
  0.7 4.1 %copy-start.7 = (s32[4,2,128]{2,1,0:T(2,128)S(1)}, s32[4,2,128]{2,1,0:T(2,128)}, u32[]{:S(2)}) copy-start(s32[4,2,128]{2,1,0:T(2,128)} %order_ref.7) | copy-start | bytes 12292
  0.7 4.1 %copy-start.8 = (s32[4,2,32]{2,1,0:T(2,128)S(1)}, s32[4,2,32]{2,1,0:T(2,128)}, u32[]{:S(2)}) copy-start(s32[4,2,32]{2,1,0:T(2,128)} %flags_ref.7) | copy-start | bytes 3076
  3.4 3.2 %collective-permute-start = (f32[8,128]{1,0:T(8,128)}, f32[8,128]{1,0:T(8,128)S(1)}, u32[]{:S(2)}, u32[]{:S(2)}) collective-permute-start(f32[8,128]{1,0:T(8,128)} %get-tuple-element.24), channel_id=1, source_target_pairs={{0,0},{1,9},{2,18},{3,27},{4,4},{5,13},{6,22},{7,31},{8,8},{9,1},{... | collective-permute-start | bytes 12296 | tf_op jit(solution)/shard_map/ppermute | solution.py:557
  4.8 1.8 %copy-start.1 = (f32[4,2,32,128]{3,2,1,0:T(8,128)S(1)}, f32[4,2,32,128]{3,2,1,0:T(8,128)}, u32[]{:S(2)}) copy-start(f32[4,2,32,128]{3,2,1,0:T(8,128)} %sla_ref.1) | copy-start | bytes 393220
  4.8 1.8 %copy-start.2 = (f32[4,2,32,128]{3,2,1,0:T(8,128)S(1)}, f32[4,2,32,128]{3,2,1,0:T(8,128)}, u32[]{:S(2)}) copy-start(f32[4,2,32,128]{3,2,1,0:T(8,128)} %inv_ref.3) | copy-start | bytes 393220
  4.8 1.8 %copy-start.12 = (f32[4,16,128]{2,1,0:T(8,128)S(1)}, f32[4,16,128]{2,1,0:T(8,128)}, u32[]{:S(2)}) copy-start(f32[4,16,128]{2,1,0:T(8,128)} %get-tuple-element.23.spots_ref) | copy-start | bytes 98308
  6.5 0.7 %copy-start.9 = (f32[4]{0:T(128)S(1)}, f32[4]{0:T(128)}, u32[]{:S(2)}) copy-start(f32[4]{0:T(128)} %jas_ref.1) | copy-start | bytes 52
  6.6 0.7 %copy-start.11 = (s32[4]{0:T(128)S(1)}, s32[4]{0:T(128)}, u32[]{:S(2)}) copy-start(s32[4]{0:T(128)} %counts_ref.7) | copy-start | bytes 52
  8.6 1.6 %collective-permute-start.1 = (f32[264,128]{1,0:T(8,128)S(1)}, f32[264,128]{1,0:T(8,128)S(1)}, u32[]{:S(2)}, u32[]{:S(2)}) collective-permute-start(f32[264,128]{1,0:T(8,128)S(1)} %get-tuple-element.25.mine_ref), channel_id=1, source_target_pairs={{0,1},{1,0},{2,3},{3,2},{4,5},{5,4},{6,7},{7,6},{8,9},{9,8},{10,11... | collective-permute-start | bytes 405512 | tf_op jit(solution)/shard_map/ppermute | solution.py:586
  10.2 8.6 %collective-permute-start.2 = (f32[264,128]{1,0:T(8,128)S(1)}, f32[264,128]{1,0:T(8,128)S(1)}, u32[]{:S(2)}, u32[]{:S(2)}) collective-permute-start(f32[264,128]{1,0:T(8,128)S(1)} %add.1.sum_ref), channel_id=1, source_target_pairs={{0,2},{1,3},{2,0},{3,1},{4,6},{5,7},{6,4},{7,5},{8,10},{9,11},{10,... | collective-permute-start | bytes 405512 | tf_op jit(solution)/shard_map/ppermute | solution.py:586
  14.7 4.1 %copy-start.10 = (f32[4]{0:T(128)S(1)}, f32[4]{0:T(128)}, u32[]{:S(2)}) copy-start(f32[4]{0:T(128)} %amp_ref.1) | copy-start | bytes 52
  14.7 11.1 %collective-permute-start.3 = (f32[144,128]{1,0:T(8,128)S(1)}, f32[144,128]{1,0:T(8,128)S(1)}, u32[]{:S(2)}, u32[]{:S(2)}) collective-permute-start(f32[144,128]{1,0:T(8,128)S(1)} %get-tuple-element.30), channel_id=1, source_target_pairs={{0,4},{4,0},{8,12},{12,8},{16,20},{20,16},{24,28},{28,24},{1,5},{5... | collective-permute-start | bytes 221192 | tf_op jit(solution)/shard_map/ppermute | solution.py:597
  16.3 9.6 %collective-permute-start.4 = (f32[144,128]{1,0:T(8,128)S(1)}, f32[144,128]{1,0:T(8,128)S(1)}, u32[]{:S(2)}, u32[]{:S(2)}) collective-permute-start(f32[144,128]{1,0:T(8,128)S(1)} %get-tuple-element.31), channel_id=1, source_target_pairs={{4,8},{12,16},{20,24},{8,4},{16,12},{24,20},{5,9},{13,17},{21,25},... | collective-permute-start | bytes 221192 | tf_op jit(solution)/shard_map/ppermute | solution.py:598
  21.6 4.4 %collective-permute-start.5 = (f32[144,128]{1,0:T(8,128)S(1)}, f32[144,128]{1,0:T(8,128)S(1)}, u32[]{:S(2)}, u32[]{:S(2)}) collective-permute-start(f32[144,128]{1,0:T(8,128)S(1)} %get-tuple-element.32), channel_id=1, source_target_pairs={{0,4},{4,0},{8,12},{12,8},{16,20},{20,16},{24,28},{28,24},{1,5},{5... | collective-permute-start | bytes 221192 | tf_op jit(solution)/shard_map/ppermute | solution.py:614
  23.7 7.1 %collective-permute-start.6 = (f32[144,128]{1,0:T(8,128)S(1)}, f32[144,128]{1,0:T(8,128)S(1)}, u32[]{:S(2)}, u32[]{:S(2)}) collective-permute-start(f32[144,128]{1,0:T(8,128)S(1)} %get-tuple-element.33), channel_id=1, source_target_pairs={{4,8},{12,16},{20,24},{8,4},{16,12},{24,20},{5,9},{13,17},{21,25},... | collective-permute-start | bytes 221192 | tf_op jit(solution)/shard_map/ppermute | solution.py:615

commit v5 on v4

--- a/solution.py
+++ b/solution.py
@@ -9,8 +9,6 @@
 BF16 = jnp.bfloat16
 highest = lax.Precision.HIGHEST
 VMEM = pl.BlockSpec(memory_space=pltpu.VMEM)
-HBM = pl.BlockSpec(memory_space=pl.ANY)
-SMEM = pl.BlockSpec(memory_space=pltpu.SMEM)
 LANES = 128
 INFO = 8
 
@@ -112,21 +110,39 @@
     return [(c == lanes).astype(F32) for c in cols]
 
 
-def pick(counts_ref, index):
-    walkers = counts_ref.shape[0]
-    total = jnp.int32(0)
-    source = jnp.int32(0)
-    for w in range(walkers):
-        total = total + counts_ref[w]
-        source = source + (total <= index).astype(jnp.int32)
-    return jnp.minimum(source, walkers - 1)
-
-
-def total_of(counts_ref):
-    total = jnp.int32(0)
-    for w in range(counts_ref.shape[0]):
-        total = total + counts_ref[w]
-    return total
+def limits_of(counts_ref):
+    counts = counts_ref[...].astype(F32)
+    limits = [counts[:, :1]]
+    for w in range(1, counts.shape[1]):
+        limits.append(limits[-1] + counts[:, w : w + 1])
+    return limits
+
+
+def picked(limits, index, choices):
+    rows = max(x[0].shape[0] for x in choices)
+    after = [
+        jnp.broadcast_to(limit - index, (rows, choices[0][0].shape[1])) <= 0.0
+        for limit in limits[:-1]
+    ]
+    out = []
+    for some in choices:
+        value = some[0]
+        for w in range(1, len(some)):
+            value = jnp.where(after[w - 1][: value.shape[0]], some[w], value)
+        out.append(value)
+    return out
+
+
+def sent(counts_ref, half, pair_ref, odd_ref):
+    limits = limits_of(counts_ref)
+    parity = lax.rem(lax.axis_index("walkers"), 2)
+    out = []
+    for pay, up in ((pair_ref, parity == 0), (odd_ref, parity == 1)):
+        up = up.astype(F32)
+        out.append(
+            (pay, [(limits, up * (limits[-1] - 1.0 * half) + 1.0 * j) for j in range(half)])
+        )
+    return out
 
 
 def pair_tiles(turns, rows, nel, kinds):
@@ -171,6 +187,8 @@
     )
 
     def change(fall):
+        fall = jnp.broadcast_to(fall, (8, nel))
+
         def term(new, old):
             nd = jnp.sqrt(new)
             od = jnp.sqrt(old)
@@ -178,8 +196,8 @@
 
         return term
 
-    same, other = pair_tiles(turns, rows, nel, [change(jas_ref[2]), change(jas_ref[3])])
-    return summed(same * (0.5 * jas_ref[0]) + other * jas_ref[1])
+    same, other = pair_tiles(turns, rows, nel, [change(jas_ref[:, 2:3]), change(jas_ref[:, 3:4])])
+    return summed(same * (0.5 * jas_ref[:, :1]) + other * jas_ref[:, 1:2])
 
 
 def in_rows(rows):
@@ -209,6 +227,7 @@
     now = [pos_ref[c] + dis_ref[c] * applied for c in range(3)]
     turn = turned(jnp.concatenate(now, axis=0))
     weighted = jnp.zeros((1, 1), F32)
+    counts = counts_ref[...].astype(F32)
     for w in range(walkers):
         nrows = [now[c][w : w + 1] for c in range(3)]
         halves = [[r[:, h * nel : (h + 1) * nel] for r in nrows] for h in (0, 1)]
@@ -227,11 +246,11 @@
         spots_ref[w, 8 : 8 + 3 * (both // LANES)] = jnp.concatenate(
             in_rows([pos_ref[c, w : w + 1] for c in range(3)]), axis=0
         )
-        weighted = weighted + energy * counts_ref[w].astype(F32)
+        weighted = weighted + energy * counts[:, w : w + 1]
     me = lax.axis_index("walkers")
     lanes = lax.broadcasted_iota(jnp.int32, info_ref.shape, 1)
     rows = lax.broadcasted_iota(jnp.int32, info_ref.shape, 0)
-    number = total_of(counts_ref).astype(F32)
+    number = jnp.sum(counts, axis=1, keepdims=True)
     info_ref[...] = jnp.where(
         lanes == me,
         jnp.where(rows == 0, number, jnp.where(rows == 1, weighted, 0.0)),
@@ -239,7 +258,11 @@
     )
 
 
-def shift_kernel(pos_ref, dis_ref, order_ref, flags_ref, cen_ref, exp_ref, orb_ref, shift_ref, differ_ref):
+def shift_kernel(
+    pos_ref, dis_ref, order_ref, flags_ref, counts_ref, jas_ref, cen_ref, exp_ref, orb_ref,
+    shift_ref, differ_ref,
+):
+    del counts_ref, jas_ref
     _, walkers, both = pos_ref.shape
     nel = both // 2
     moves = flags_ref.shape[2]
@@ -310,15 +333,17 @@
     half = walkers // 2
     per = 2 * orbs
     tail = half * per
-    parity = lax.rem(lax.axis_index("walkers"), 2)
-    number = total_of(counts_ref)
-    for pay, goes_up in ((pair_ref, parity == 0), (odd_ref, parity == 1)):
-        for j in range(half):
-            index = jnp.where(goes_up, number - half + j, j)
-            source = pick(counts_ref, index)
+    for pay, indices in sent(counts_ref, half, pair_ref, odd_ref):
+        for j, (limits, index) in enumerate(indices):
+            rows = picked(
+                limits,
+                index,
+                [[done_ref[w, s] for w in range(walkers)] for s in (0, 1)]
+                + [[spots_ref[w, :8] for w in range(walkers)]],
+            )
             for s in (0, 1):
-                pay[j * per + s * orbs : j * per + (s + 1) * orbs, :] = done_ref[source, s]
-            pay[tail + 8 * j : tail + 8 * j + 8, :] = spots_ref[source, :8]
+                pay[j * per + s * orbs : j * per + (s + 1) * orbs, :] = rows[s]
+            pay[tail + 8 * j : tail + 8 * j + 8, :] = rows[2]
 
 
 def add_kernel(mine_ref, other_ref, out_ref):
@@ -396,29 +421,30 @@
         log_ref[w : w + 1, :] = (
             jnp.broadcast_to(jnp.sum(both, axis=1, keepdims=True), (1, nel))
             + info_ref[2 + w : 3 + w, :nel]
-            + amp_ref[w]
+            + amp_ref[:, w : w + 1]
         )
     half = walkers // 2
     per = 2 * orbs
     tail = half * per
-    parity = lax.rem(lax.axis_index("walkers"), 2)
-    number = total_of(counts_ref)
-    for pay, goes_up in ((pair_ref, parity == 0), (odd_ref, parity == 1)):
+    for pay, indices in sent(counts_ref, half, pair_ref, odd_ref):
         pay[tail : tail + INFO, :] = info_ref[...]
         pay[tail + INFO :, :] = jnp.zeros((pay.shape[0] - tail - INFO, LANES), F32)
-        for j in range(half):
-            index = jnp.where(goes_up, number - half + j, j)
-            source = pick(counts_ref, index)
+        for j, (limits, index) in enumerate(indices):
+            rows = picked(
+                limits,
+                index,
+                [[cur_ref[w, s] for w in range(walkers)] for s in (0, 1)]
+                + [[log_ref[w : w + 1, :] for w in range(walkers)]],
+            )
             for s in (0, 1):
-                pay[j * per + s * orbs : j * per + (s + 1) * orbs, :] = cur_ref[source, s]
-            at = tail + INFO + j
-            pay[at : at + 1, :] = log_ref[pl.ds(source, 1), :]
+                pay[j * per + s * orbs : j * per + (s + 1) * orbs, :] = rows[s]
+            pay[tail + INFO + j : tail + INFO + j + 1, :] = rows[2]
 
 
 def place_kernel(
     counts_ref, cur_ref, done_ref, spots_ref, log_ref, info_ref,
     pair_s_ref, odd_s_ref, pair_i_ref, odd_i_ref,
-    inv_out, sla_out, pos_out, log_out, energy_out, mean_out, sems,
+    inv_out, sla_out, pos_out, log_out, energy_out, mean_out,
 ):
     walkers, _, orbs, nel = cur_ref.shape
     width = pos_out.shape[2] // LANES
@@ -429,75 +455,72 @@
     parity = lax.rem(me, 2)
     info = info_ref[...] + pair_i_ref[tail : tail + INFO, :]
     lanes = lax.broadcasted_iota(jnp.int32, (1, info.shape[1]), 1)
-    before = jnp.sum(jnp.where(lanes < me, info[0:1], 0.0)).astype(jnp.int32)
+    before = jnp.sum(jnp.where(lanes < me, info[0:1], 0.0), axis=1, keepdims=True)
     groups = lax.axis_size("walkers")
     mean = jnp.sum(info[1:2], axis=1, keepdims=True)
     mean_out[...] = mean / (1.0 * walkers * groups)
-    number = total_of(counts_ref)
+    limits = limits_of(counts_ref)
     slots = lax.broadcasted_iota(jnp.int32, (1, walkers), 1)
-
-    def put(j, inverse, slater, spot, log):
+    here = [[cur_ref[w, s] for w in range(walkers)] for s in (0, 1)]
+    here += [[done_ref[w, s] for w in range(walkers)] for s in (0, 1)]
+    here += [[spots_ref[w, :8] for w in range(walkers)]]
+    here += [[log_ref[w : w + 1, :] for w in range(walkers)]]
+    odd = parity.astype(F32)
+    log_new = jnp.zeros((1, walkers), F32)
+    energy_new = jnp.zeros((1, walkers), F32)
+    for j in range(walkers):
+        index = (1.0 * walkers) * me.astype(F32) + 1.0 * j - before
+        own = picked(limits, index, here)
+        low = j < half
+        outside = -index if low else index - limits[-1] + 1.0
+        entry = index + 1.0 * half if low else index - limits[-1]
+        on_pair = odd if low else 1.0 - odd
+        shape_here = (orbs, nel)
+        away = jnp.broadcast_to(outside, shape_here) > 0.0
+        second = jnp.broadcast_to(entry, shape_here) > 0.5
+        pair = jnp.broadcast_to(on_pair, shape_here) > 0.5
+
+        def one(late, at, rows):
+            parts = []
+            for i in range(half):
+                start = at(i)
+                a, b = (ref[start : start + rows, :] for ref in late)
+                parts.append(jnp.where(pair[:rows], a, b))
+            value = parts[0]
+            for i in range(1, half):
+                again = second if i == 1 else jnp.broadcast_to(entry, shape_here) > i - 0.5
+                value = jnp.where(again[:rows], parts[i], value)
+            return value
+
+        inverses = (pair_i_ref, odd_i_ref)
+        slaters = (pair_s_ref, odd_s_ref)
+        got = [one(inverses, lambda i, s=s: i * per + s * orbs, orbs) for s in (0, 1)]
+        got += [one(slaters, lambda i, s=s: i * per + s * orbs, orbs) for s in (0, 1)]
+        got += [one(slaters, lambda i: tail + 8 * i, 8)]
+        got += [one(inverses, lambda i: tail + INFO + i, 1)]
+        new = [jnp.where(away[: o.shape[0]], g, o) for o, g in zip(own, got)]
         for s in (0, 1):
-            pltpu.make_async_copy(inverse(s), inv_out.at[j, s], sems.at[j, s, 0]).start()
-            pltpu.make_async_copy(slater(s), sla_out.at[j, s], sems.at[j, s, 1]).start()
+            inv_out[j, s] = new[s]
+            sla_out[j, s] = new[2 + s]
         for c in range(3):
             for h in range(width):
-                pos_out[c, j : j + 1, h * LANES : (h + 1) * LANES] = spot[3 * h + c : 3 * h + c + 1]
-        log_out[...] = jnp.where(slots == j, log[:, :walkers], log_out[...])
-        energy_out[...] = jnp.where(
-            slots == j, spot[3 * width : 3 * width + 1, :walkers], energy_out[...]
+                pos_out[c, j : j + 1, h * LANES : (h + 1) * LANES] = new[4][
+                    3 * h + c : 3 * h + c + 1
+                ]
+        log_new = jnp.where(slots == j, new[5][:, :walkers], log_new)
+        energy_new = jnp.where(
+            slots == j, new[4][3 * width : 3 * width + 1, :walkers], energy_new
         )
-
-    log_out[...] = jnp.zeros(log_out.shape, F32)
-    energy_out[...] = jnp.zeros(energy_out.shape, F32)
-    for j in range(walkers):
-        index = me * walkers + j - before
-        low = index < 0
-        high = index >= number
-
-        @pl.when(jnp.logical_not(low | high))
-        def _():
-            w = pick(counts_ref, index)
-            put(
-                j,
-                lambda s: cur_ref.at[w, s],
-                lambda s: done_ref.at[w, s],
-                spots_ref[w, :8],
-                log_ref[pl.ds(w, 1), :],
-            )
-
-        def received(late, early):
-            i = jnp.clip(jnp.where(low, index + half, index - number), 0, half - 1)
-            put(
-                j,
-                lambda s: late.at[pl.ds(pl.multiple_of(i * per + s * orbs, 8), orbs), :],
-                lambda s: early.at[pl.ds(pl.multiple_of(i * per + s * orbs, 8), orbs), :],
-                early[pl.ds(pl.multiple_of(tail + i * 8, 8), 8), :],
-                late[pl.ds(tail + INFO + i, 1), :],
-            )
-
-        on_pair = (low & (parity == 1)) | (high & (parity == 0))
-
-        @pl.when(on_pair)
-        def _():
-            received(pair_i_ref, pair_s_ref)
-
-        @pl.when((low | high) & jnp.logical_not(on_pair))
-        def _():
-            received(odd_i_ref, odd_s_ref)
-
-    for j in range(walkers):
-        for s in (0, 1):
-            pltpu.make_async_copy(cur_ref.at[0, s], inv_out.at[j, s], sems.at[j, s, 0]).wait()
-            pltpu.make_async_copy(done_ref.at[0, s], sla_out.at[j, s], sems.at[j, s, 1]).wait()
-
-
-def call(kernel, outs, in_specs, scratch=(), us=1.0, name=None, out_specs=None, vmem=32 * 2**20):
+    log_out[...] = log_new
+    energy_out[...] = energy_new
+
+
+def call(kernel, outs, in_specs, scratch=(), us=1.0, name=None, vmem=32 * 2**20):
     return pl.pallas_call(
         kernel,
         out_shape=outs,
         in_specs=in_specs,
-        out_specs=jax.tree.map(lambda _: VMEM, outs) if out_specs is None else out_specs,
+        out_specs=jax.tree.map(lambda _: VMEM, outs),
         scratch_shapes=list(scratch),
         compiler_params=pltpu.CompilerParams(vmem_limit_bytes=vmem),
         cost_estimate=pl.CostEstimate(flops=int(us * 1.1e9), bytes_accessed=2**18, transcendentals=0),
@@ -525,6 +548,10 @@
     count = 2 * walkers
     tall = half * per + 16
 
+    counts = counts.reshape(1, walkers)
+    log_amp = log_amp.reshape(1, walkers)
+    jastrow = jastrow.reshape(1, jastrow.shape[0])
+
     pairs = [(i, i ^ 1) for i in range(groups)]
     odds = [(i, i + 1) for i in range(1, groups - 1, 2)]
     odds = odds + [(b, a) for a, b in odds]
@@ -537,7 +564,7 @@
             shape(walkers, 16, LANES),
             shape(INFO, wide),
         ),
-        [VMEM, VMEM, VMEM, VMEM, SMEM],
+        [VMEM] * 5,
         us=2,
         vmem=61 * 2**20,
         name="energy",
@@ -549,21 +576,25 @@
         info = info + lax.ppermute(info, "walkers", [(i, i ^ step) for i in range(groups)])
         step *= 2
     joint = [
-        (d * members + o, (d ^ (2 * o)) * members + o)
+        (d * members + o, (d ^ (2 * hop)) * members + o)
+        for o in range(members)
+        for hop in [(o + 1) % 3 if members > 3 and o < 3 else o]
         for d in range(groups)
-        for o in range(members)
-        if 2 * o < groups
+        if 2 * hop < groups
     ]
     info = lax.ppermute(info, ("walkers", "orb"), joint)
 
     shift = call(
         shift_kernel,
         shape(2, walkers * moves, orbs),
-        [VMEM] * 7,
+        [VMEM] * 9,
         scratch=[pltpu.VMEM((2, walkers * moves, basis), F32)],
         us=3,
         name="shift",
-    )(places, steps, move_order, accepted, centers, exponents.reshape(1, basis), orbitals)
+    )(
+        places, steps, move_order, accepted, counts, jastrow, centers,
+        exponents.reshape(1, basis), orbitals,
+    )
 
     part, done, pair_s, odd_s = call(
         partial_kernel,
@@ -573,7 +604,7 @@
             shape(tall, LANES),
             shape(tall, LANES),
         ),
-        [VMEM, VMEM, VMEM, SMEM] + [VMEM] * 4 + [SMEM],
+        [VMEM] * 9,
         us=2,
         name="partial",
     )(shift, move_order, accepted, counts, inverse, slater, spots, info, jastrow)
@@ -606,7 +637,7 @@
             shape(tall, LANES),
             shape(tall, LANES),
         ),
-        [VMEM] * 5 + [SMEM, SMEM],
+        [VMEM] * 7,
         us=4,
         name="update",
     )(total, got, inverse, move_order, accepted, counts, log_amp)
@@ -624,9 +655,7 @@
             shape(1, walkers),
             shape(1, 1),
         ),
-        [SMEM] + [VMEM] * 9,
-        out_specs=(HBM, HBM, VMEM, VMEM, VMEM, VMEM),
-        scratch=[pltpu.SemaphoreType.DMA((walkers, 2, 2))],
+        [VMEM] * 10,
         us=1.5,
         name="place",
     )(counts, current, done, spots, logs, info, pair_s, odd_s, pair_i, odd_i)

time: 33.2 us -> 30.8 us (0.928)
  the two profiles are of different devices: /device:TPU:8 before, /device:TPU:16 now
where the time goes in v5:
time: 30.8 us; the launch traced here: 30.5 us
  starting transfers between devices  13.3 us (43%)
  Pallas kernels  8.79 us (29%)
  waiting for transfers between devices  6.94 us (23%)
  between operations  0.88 us (3%)
  local copies, waits for them, and re-layouts  0.63 us (2%)
    ppermute x1, waiting for transfers between devices, body(): odd_i = lax.ppermute(odd_i, 'walkers', odds)  4.6 us
    ppermute x1, starting transfers between devices, body(): info = lax.ppermute(info, ('walkers', 'orb'), joint)  3.6 us
    ppermute x1, starting transfers between devices, body(): odd_s = lax.ppermute(odd_s, 'walkers', odds)  3.04 us
    pallas_call x1, Pallas kernels, body(): call(energy_kernel, (shape(walkers, 16, LANES), shape(INFO, wide)), [VMEM...  3.04 us
    ppermute x1, starting transfers between devices, body(): odd_i = lax.ppermute(odd_i, 'walkers', odds)  2.49 us
    ppermute x1, starting transfers between devices, body(): pair_i = lax.ppermute(pair_i, 'walkers', pairs)  2.44 us
    ppermute x2, waiting for transfers between devices, body(): got = lax.ppermute(total, 'orb', partner)  2.33 us
    pallas_call x1, Pallas kernels, body(): call(update_kernel, (shape(walkers, 2, orbs, nel), shape(8, nel), shape(I...  2.21 us
  transfers between devices with their start and end apart: 7, of which 3 were waited for; matrix products, arithmetic and copies ran while one was open for 0% of the time, Pallas kernels for 13%

profile of v5, /device:TPU:16, one launch (start us, length us, event | category | flops | bytes accessed | tf_op | source)
XLA Modules:
  0.0 30.5 jit_solution(8816192905441511421)
XLA Ops:
  0.6 0.0 copy-start
  0.7 3.0 %energy.1 = (f32[4,16,128]{2,1,0:T(8,128)}, f32[8,128]{1,0:T(8,128)}) custom-call(f32[3,4,256]{2,1,0:T(4,128)} %bitcast.10, f32[3,4,256]{2,1,0:T(4,128)} %bitcast.12, s32[4,2,128]{2,1,0:T(2,128)} %order_ref.7, s32[4,2,32]{2,1,0:T(2,128)} %flags_ref.7, s32[1,4]{1,0:T(1,128)} %bitcast.18), custom_call_target="tpu_custom_call" | custom-call | flops 2200000000 | bytes 262144 | tf_op jit(solution)/shard_map/energy/pallas_call | solution.py:561
  3.7 3.6 %collective-permute-start = (f32[8,128]{1,0:T(8,128)}, f32[8,128]{1,0:T(8,128)S(1)}, u32[]{:S(2)}, u32[]{:S(2)}) collective-permute-start(f32[8,128]{1,0:T(8,128)} %get-tuple-element.24), channel_id=1, source_target_pairs={{0,8},{4,12},{8,0},{12,4},{16,24},{20,28},{24,16},{28,20},{1,17},{... | collective-permute-start | bytes 12296 | tf_op jit(solution)/shard_map/ppermute | solution.py:585
  7.3 0.0 copy-start.9
  7.4 0.0 copy-start.11
  7.4 0.6 %copy-done.9 = f32[4]{0:T(128)S(1)} copy-done((f32[4]{0:T(128)S(1)}, f32[4]{0:T(128)}, u32[]{:S(2)}) %copy-start.9) | copy-done | bytes 40
  8.0 0.0 copy-done.11
  8.0 1.7 %shift.1.shift_ref = f32[2,128,32]{2,1,0:T(8,128)S(1)} custom-call(f32[3,4,256]{2,1,0:T(4,128)S(1)} %bitcast.11, f32[3,4,256]{2,1,0:T(4,128)S(1)} %bitcast.13, s32[4,2,128]{2,1,0:T(2,128)S(1)} %copy-done.7, s32[4,2,32]{2,1,0:T(2,128)S(1)} %copy-done.8, s32[1,4]{1,0:T(1,128)S(1)} %bitcast.19, f32[1,4]{1,0:T(1,128)S(1)} %bitcast.15, f32[3,1024]{1,0:T(4,128)S(1)} %copy-done.3, ...), custom_call_target="tpu_custom_call" | custom-call | flops 3300000000 | bytes 262144 | tf_op jit(solution)/shard_map/shift/pallas_call | solution.py:587
  9.8 0.0 collective-permute-done.info_ref
  9.8 0.9 %partial.1 = (f32[264,128]{1,0:T(8,128)S(1)}, f32[4,2,32,128]{3,2,1,0:T(8,128)S(1)}, f32[144,128]{1,0:T(8,128)S(1)}, f32[144,128]{1,0:T(8,128)S(1)}) custom-call(f32[2,128,32]{2,1,0:T(8,128)S(1)} %shift.1.shift_ref, s32[4,2,128]{2,1,0:T(2,128)S(1)} %copy-done.7, s32[4,2,32]{2,1,0:T(2,128)S(1)} %copy-done.8, s32[1,4]{1,0:T(1,128)S(1)} %bitcast.20, ...), custom_call_target="tpu_custom_call" | custom-call | flops 2200000000 | bytes 262144 | tf_op jit(solution)/shard_map/partial/pallas_call | solution.py:599
  10.7 0.1 collective-permute-start.1
  10.8 1.3 %collective-permute-done.1.other_ref = f32[264,128]{1,0:T(8,128)S(1)} collective-permute-done((f32[264,128]{1,0:T(8,128)S(1)}, f32[264,128]{1,0:T(8,128)S(1)}, u32[]{:S(2)}, u32[]{:S(2)}) %collective-permute-start.1) | collective-permute-done | bytes 135200 | tf_op jit(solution)/shard_map/ppermute | solution.py:617
  12.1 0.1 collective-permute-start.2
  12.2 1.6 %collective-permute-start.3 = (f32[144,128]{1,0:T(8,128)S(1)}, f32[144,128]{1,0:T(8,128)S(1)}, u32[]{:S(2)}, u32[]{:S(2)}) collective-permute-start(f32[144,128]{1,0:T(8,128)S(1)} %get-tuple-element.30), channel_id=1, source_target_pairs={{0,4},{4,0},{8,12},{12,8},{16,20},{20,16},{24,28},{28,24},{1,5},{5... | collective-permute-start | bytes 221192 | tf_op jit(solution)/shard_map/ppermute | solution.py:628
  13.8 3.0 %collective-permute-start.4 = (f32[144,128]{1,0:T(8,128)S(1)}, f32[144,128]{1,0:T(8,128)S(1)}, u32[]{:S(2)}, u32[]{:S(2)}) collective-permute-start(f32[144,128]{1,0:T(8,128)S(1)} %get-tuple-element.31), channel_id=1, source_target_pairs={{4,8},{12,16},{20,24},{8,4},{16,12},{24,20},{5,9},{13,17},{21,25},... | collective-permute-start | bytes 221192 | tf_op jit(solution)/shard_map/ppermute | solution.py:629
  16.8 1.0 %collective-permute-done.2.got_ref = f32[264,128]{1,0:T(8,128)S(1)} collective-permute-done((f32[264,128]{1,0:T(8,128)S(1)}, f32[264,128]{1,0:T(8,128)S(1)}, u32[]{:S(2)}, u32[]{:S(2)}) %collective-permute-start.2) | collective-permute-done | bytes 135200 | tf_op jit(solution)/shard_map/ppermute | solution.py:617
  17.8 2.2 %update.1 = (f32[4,2,32,128]{3,2,1,0:T(8,128)S(1)}, f32[8,128]{1,0:T(8,128)S(1)}, f32[8,128]{1,0:T(8,128)S(1)}, f32[144,128]{1,0:T(8,128)S(1)}, f32[144,128]{1,0:T(8,128)S(1)}) custom-call(f32[264,128]{1,0:T(8,128)S(1)} %add.1.sum_ref, f32[264,128]{1,0:T(8,128)S(1)} %collective-permute-done.2.got_ref, f32[4,2,32,128]{3,2,1,0:T(8,128)S(1)} %copy-done.2, ...), custom_call_target="tpu_custom_call" | custom-call | flops 4400000000 | bytes 262144 | tf_op jit(solution)/shard_map/update/pallas_call | solution.py:631
  20.0 2.4 %collective-permute-start.5 = (f32[144,128]{1,0:T(8,128)S(1)}, f32[144,128]{1,0:T(8,128)S(1)}, u32[]{:S(2)}, u32[]{:S(2)}) collective-permute-start(f32[144,128]{1,0:T(8,128)S(1)} %get-tuple-element.32), channel_id=1, source_target_pairs={{0,4},{4,0},{8,12},{12,8},{16,20},{20,16},{24,28},{28,24},{1,5},{5... | collective-permute-start | bytes 221192 | tf_op jit(solution)/shard_map/ppermute | solution.py:645
  22.5 2.5 %collective-permute-start.6 = (f32[144,128]{1,0:T(8,128)S(1)}, f32[144,128]{1,0:T(8,128)S(1)}, u32[]{:S(2)}, u32[]{:S(2)}) collective-permute-start(f32[144,128]{1,0:T(8,128)S(1)} %get-tuple-element.33), channel_id=1, source_target_pairs={{4,8},{12,16},{20,24},{8,4},{16,12},{24,20},{5,9},{13,17},{21,25},... | collective-permute-start | bytes 221192 | tf_op jit(solution)/shard_map/ppermute | solution.py:646
  25.0 0.0 collective-permute-done.3.pair_s_ref
  25.0 0.0 collective-permute-done.4.odd_s_ref
  25.0 0.0 collective-permute-done.5.pair_i_ref
  25.0 4.6 %collective-permute-done.6.odd_i_ref = f32[144,128]{1,0:T(8,128)S(1)} collective-permute-done((f32[144,128]{1,0:T(8,128)S(1)}, f32[144,128]{1,0:T(8,128)S(1)}, u32[]{:S(2)}, u32[]{:S(2)}) %collective-permute-start.6) | collective-permute-done | bytes 73760 | tf_op jit(solution)/shard_map/ppermute | solution.py:646
  29.6 0.9 %place.1 = (f32[4,2,32,128]{3,2,1,0:T(8,128)}, f32[4,2,32,128]{3,2,1,0:T(8,128)}, f32[3,4,256]{2,1,0:T(4,128)}, f32[1,4]{1,0:T(1,128)}, f32[1,4]{1,0:T(1,128)}, /*index=5*/f32[1,1]{1,0:T(1,128)}) custom-call(s32[1,4]{1,0:T(1,128)S(1)} %bitcast.22, f32[4,2,32,128]{3,2,1,0:T(8,128)S(1)} %get-tuple-element.26.cur_ref, ...), custom_call_target="tpu_custom_call" | custom-call | flops 1650000000 | bytes 262144 | tf_op jit(solution)/shard_map/place/pallas_call | solution.py:648
  (22 shorter events, 0.1 us)
Async XLA Ops:
  0.6 6.7 %copy-start = (f32[2,32,1024]{2,1,0:T(8,128)S(1)}, f32[2,32,1024]{2,1,0:T(8,128)}, u32[]{:S(2)}) copy-start(f32[2,32,1024]{2,1,0:T(8,128)} %orb_ref.1) | copy-start | bytes 786436
  0.6 6.7 %copy-start.3 = (f32[3,1024]{1,0:T(4,128)S(1)}, f32[3,1024]{1,0:T(4,128)}, u32[]{:S(2)}) copy-start(f32[3,1024]{1,0:T(4,128)} %cen_ref.1) | copy-start | bytes 36868
  0.7 6.7 %copy-start.4 = (f32[4,3,256]{2,0,1:T(4,128)S(1)}, f32[4,3,256]{2,0,1:T(4,128)}, u32[]{:S(2)}) copy-start(f32[4,3,256]{2,0,1:T(4,128)} %param.14) | copy-start | bytes 36868
  0.7 6.7 %copy-start.5 = (f32[4,3,256]{2,0,1:T(4,128)S(1)}, f32[4,3,256]{2,0,1:T(4,128)}, u32[]{:S(2)}) copy-start(f32[4,3,256]{2,0,1:T(4,128)} %param.15) | copy-start | bytes 36868
  0.7 6.7 %copy-start.7 = (s32[4,2,128]{2,1,0:T(2,128)S(1)}, s32[4,2,128]{2,1,0:T(2,128)}, u32[]{:S(2)}) copy-start(s32[4,2,128]{2,1,0:T(2,128)} %order_ref.7) | copy-start | bytes 12292
  0.7 6.7 %copy-start.8 = (s32[4,2,32]{2,1,0:T(2,128)S(1)}, s32[4,2,32]{2,1,0:T(2,128)}, u32[]{:S(2)}) copy-start(s32[4,2,32]{2,1,0:T(2,128)} %flags_ref.7) | copy-start | bytes 3076
  3.7 3.7 %copy-start.6 = (f32[1024]{0:T(1024)S(1)}, f32[1024]{0:T(1024)}, u32[]{:S(2)}) copy-start(f32[1024]{0:T(1024)} %param.21) | copy-start | bytes 12292
  3.7 6.0 %collective-permute-start = (f32[8,128]{1,0:T(8,128)}, f32[8,128]{1,0:T(8,128)S(1)}, u32[]{:S(2)}, u32[]{:S(2)}) collective-permute-start(f32[8,128]{1,0:T(8,128)} %get-tuple-element.24), channel_id=1, source_target_pairs={{0,8},{4,12},{8,0},{12,4},{16,24},{20,28},{24,16},{28,20},{1,17},{... | collective-permute-start | bytes 12296 | tf_op jit(solution)/shard_map/ppermute | solution.py:585
  7.3 0.7 %copy-start.9 = (f32[4]{0:T(128)S(1)}, f32[4]{0:T(128)}, u32[]{:S(2)}) copy-start(f32[4]{0:T(128)} %param.23) | copy-start | bytes 52
  7.4 0.7 %copy-start.11 = (s32[4]{0:T(128)S(1)}, s32[4]{0:T(128)}, u32[]{:S(2)}) copy-start(s32[4]{0:T(128)} %param.18) | copy-start | bytes 52
  8.0 1.8 %copy-start.1 = (f32[4,2,32,128]{3,2,1,0:T(8,128)S(1)}, f32[4,2,32,128]{3,2,1,0:T(8,128)}, u32[]{:S(2)}) copy-start(f32[4,2,32,128]{3,2,1,0:T(8,128)} %sla_ref.1) | copy-start | bytes 393220
  8.0 1.8 %copy-start.2 = (f32[4,2,32,128]{3,2,1,0:T(8,128)S(1)}, f32[4,2,32,128]{3,2,1,0:T(8,128)}, u32[]{:S(2)}) copy-start(f32[4,2,32,128]{3,2,1,0:T(8,128)} %inv_ref.3) | copy-start | bytes 393220
  8.0 1.8 %copy-start.12 = (f32[4,16,128]{2,1,0:T(8,128)S(1)}, f32[4,16,128]{2,1,0:T(8,128)}, u32[]{:S(2)}) copy-start(f32[4,16,128]{2,1,0:T(8,128)} %get-tuple-element.23.spots_ref) | copy-start | bytes 98308
  10.7 1.4 %collective-permute-start.1 = (f32[264,128]{1,0:T(8,128)S(1)}, f32[264,128]{1,0:T(8,128)S(1)}, u32[]{:S(2)}, u32[]{:S(2)}) collective-permute-start(f32[264,128]{1,0:T(8,128)S(1)} %get-tuple-element.25.mine_ref), channel_id=1, source_target_pairs={{0,1},{1,0},{2,3},{3,2},{4,5},{5,4},{6,7},{7,6},{8,9},{9,8},{10,11... | collective-permute-start | bytes 405512 | tf_op jit(solution)/shard_map/ppermute | solution.py:617
  12.1 5.7 %collective-permute-start.2 = (f32[264,128]{1,0:T(8,128)S(1)}, f32[264,128]{1,0:T(8,128)S(1)}, u32[]{:S(2)}, u32[]{:S(2)}) collective-permute-start(f32[264,128]{1,0:T(8,128)S(1)} %add.1.sum_ref), channel_id=1, source_target_pairs={{0,2},{1,3},{2,0},{3,1},{4,6},{5,7},{6,4},{7,5},{8,10},{9,11},{10,... | collective-permute-start | bytes 405512 | tf_op jit(solution)/shard_map/ppermute | solution.py:617
  12.2 12.8 %collective-permute-start.3 = (f32[144,128]{1,0:T(8,128)S(1)}, f32[144,128]{1,0:T(8,128)S(1)}, u32[]{:S(2)}, u32[]{:S(2)}) collective-permute-start(f32[144,128]{1,0:T(8,128)S(1)} %get-tuple-element.30), channel_id=1, source_target_pairs={{0,4},{4,0},{8,12},{12,8},{16,20},{20,16},{24,28},{28,24},{1,5},{5... | collective-permute-start | bytes 221192 | tf_op jit(solution)/shard_map/ppermute | solution.py:628
  13.8 4.0 %copy-start.10 = (f32[4]{0:T(128)S(1)}, f32[4]{0:T(128)}, u32[]{:S(2)}) copy-start(f32[4]{0:T(128)} %param.19) | copy-start | bytes 52
  13.8 11.2 %collective-permute-start.4 = (f32[144,128]{1,0:T(8,128)S(1)}, f32[144,128]{1,0:T(8,128)S(1)}, u32[]{:S(2)}, u32[]{:S(2)}) collective-permute-start(f32[144,128]{1,0:T(8,128)S(1)} %get-tuple-element.31), channel_id=1, source_target_pairs={{4,8},{12,16},{20,24},{8,4},{16,12},{24,20},{5,9},{13,17},{21,25},... | collective-permute-start | bytes 221192 | tf_op jit(solution)/shard_map/ppermute | solution.py:629
  20.0 5.0 %collective-permute-start.5 = (f32[144,128]{1,0:T(8,128)S(1)}, f32[144,128]{1,0:T(8,128)S(1)}, u32[]{:S(2)}, u32[]{:S(2)}) collective-permute-start(f32[144,128]{1,0:T(8,128)S(1)} %get-tuple-element.32), channel_id=1, source_target_pairs={{0,4},{4,0},{8,12},{12,8},{16,20},{20,16},{24,28},{28,24},{1,5},{5... | collective-permute-start | bytes 221192 | tf_op jit(solution)/shard_map/ppermute | solution.py:645
  22.5 7.1 %collective-permute-start.6 = (f32[144,128]{1,0:T(8,128)S(1)}, f32[144,128]{1,0:T(8,128)S(1)}, u32[]{:S(2)}, u32[]{:S(2)}) collective-permute-start(f32[144,128]{1,0:T(8,128)S(1)} %get-tuple-element.33), channel_id=1, source_target_pairs={{4,8},{12,16},{20,24},{8,4},{16,12},{24,20},{5,9},{13,17},{21,25},... | collective-permute-start | bytes 221192 | tf_op jit(solution)/shard_map/ppermute | solution.py:646

commit v6 on v5

--- a/solution.py
+++ b/solution.py
@@ -9,6 +9,7 @@
 BF16 = jnp.bfloat16
 highest = lax.Precision.HIGHEST
 VMEM = pl.BlockSpec(memory_space=pltpu.VMEM)
+ANY = pl.BlockSpec(memory_space=pl.ANY)
 LANES = 128
 INFO = 8
 
@@ -110,10 +111,10 @@
     return [(c == lanes).astype(F32) for c in cols]
 
 
-def limits_of(counts_ref):
-    counts = counts_ref[...].astype(F32)
+def limits_of(spots_ref, walkers):
+    counts = spots_ref[walkers, 0:1, :]
     limits = [counts[:, :1]]
-    for w in range(1, counts.shape[1]):
+    for w in range(1, walkers):
         limits.append(limits[-1] + counts[:, w : w + 1])
     return limits
 
@@ -133,8 +134,9 @@
     return out
 
 
-def sent(counts_ref, half, pair_ref, odd_ref):
-    limits = limits_of(counts_ref)
+def sent(spots_ref, walkers, pair_ref, odd_ref):
+    half = walkers // 2
+    limits = limits_of(spots_ref, walkers)
     parity = lax.rem(lax.axis_index("walkers"), 2)
     out = []
     for pay, up in ((pair_ref, parity == 0), (odd_ref, parity == 1)):
@@ -174,7 +176,7 @@
     return jnp.sum(jnp.sum(tile, axis=0, keepdims=True), axis=1, keepdims=True)
 
 
-def jastrow_of(spots, turn, jas_ref, nel):
+def jastrow_of(spots, turn, jas, nel):
     rows, turns = (
         [
             [
@@ -196,8 +198,8 @@
 
         return term
 
-    same, other = pair_tiles(turns, rows, nel, [change(jas_ref[:, 2:3]), change(jas_ref[:, 3:4])])
-    return summed(same * (0.5 * jas_ref[:, :1]) + other * jas_ref[:, 1:2])
+    same, other = pair_tiles(turns, rows, nel, [change(jas[:, 2:3]), change(jas[:, 3:4])])
+    return summed(same * (0.5 * jas[:, :1]) + other * jas[:, 1:2])
 
 
 def in_rows(rows):
@@ -205,8 +207,24 @@
 
 
 def energy_kernel(
-    pos_ref, dis_ref, order_ref, flags_ref, counts_ref, spots_ref, info_ref,
+    pos_in, dis_in, order_in, flags_in, counts_in, jas_in, amp_in, spots_out, info_out,
+    pos_ref, dis_ref, order_ref, flags_ref, counts_ref, jas_ref, amp_ref, spots_ref, info_ref,
+    loads, stores,
 ):
+    operands = (
+        (pos_in, pos_ref),
+        (dis_in, dis_ref),
+        (order_in, order_ref),
+        (flags_in, flags_ref),
+        (counts_in, counts_ref),
+        (jas_in, jas_ref),
+        (amp_in, amp_ref),
+    )
+    copies = [pltpu.make_async_copy(a, b, loads.at[i]) for i, (a, b) in enumerate(operands)]
+    for copy in copies:
+        copy.start()
+    for copy in copies:
+        copy.wait()
     _, walkers, both = pos_ref.shape
     nel = both // 2
     cols, keep = moves_of(order_ref, flags_ref)
@@ -250,19 +268,28 @@
     me = lax.axis_index("walkers")
     lanes = lax.broadcasted_iota(jnp.int32, info_ref.shape, 1)
     rows = lax.broadcasted_iota(jnp.int32, info_ref.shape, 0)
+    spots_ref[walkers] = jnp.zeros(spots_ref.shape[1:], F32)
+    for row, some in enumerate((counts, jas_ref[...], amp_ref[...])):
+        spots_ref[walkers, row : row + 1, : some.shape[1]] = some
     number = jnp.sum(counts, axis=1, keepdims=True)
     info_ref[...] = jnp.where(
         lanes == me,
         jnp.where(rows == 0, number, jnp.where(rows == 1, weighted, 0.0)),
         0.0,
     )
+    copies = [
+        pltpu.make_async_copy(info_ref, info_out, stores.at[0]),
+        pltpu.make_async_copy(spots_ref, spots_out, stores.at[1]),
+    ]
+    for copy in copies:
+        copy.start()
+    for copy in copies:
+        copy.wait()
 
 
 def shift_kernel(
-    pos_ref, dis_ref, order_ref, flags_ref, counts_ref, jas_ref, cen_ref, exp_ref, orb_ref,
-    shift_ref, differ_ref,
+    pos_ref, dis_ref, order_ref, flags_ref, cen_ref, exp_ref, orb_ref, shift_ref, differ_ref,
 ):
-    del counts_ref, jas_ref
     _, walkers, both = pos_ref.shape
     nel = both // 2
     moves = flags_ref.shape[2]
@@ -304,7 +331,7 @@
 
 
 def partial_kernel(
-    shift_ref, order_ref, flags_ref, counts_ref, inv_ref, sla_ref, spots_ref, info_ref, jas_ref,
+    shift_ref, order_ref, flags_ref, inv_ref, sla_ref, spots_ref, info_ref,
     part_ref, done_ref, pair_ref, odd_ref,
 ):
     walkers, _, orbs, nel = inv_ref.shape
@@ -316,11 +343,12 @@
     first = lax.axis_index("orb") * share
     tail = 2 * walkers * moves
     part_ref[tail:, :] = info_ref[...]
+    jas = spots_ref[walkers, 1:2, :]
     for w in range(share):
         mine = spots_ref[first + w]
         at = tail + 2 + first + w
         part_ref[pl.ds(at, 1), :] = jnp.broadcast_to(
-            jastrow_of(mine, turned(mine), jas_ref, nel), (1, part_ref.shape[1])
+            jastrow_of(mine, turned(mine), jas, nel), (1, part_ref.shape[1])
         )
     for s in (0, 1):
         for w in range(walkers):
@@ -333,7 +361,7 @@
     half = walkers // 2
     per = 2 * orbs
     tail = half * per
-    for pay, indices in sent(counts_ref, half, pair_ref, odd_ref):
+    for pay, indices in sent(spots_ref, walkers, pair_ref, odd_ref):
         for j, (limits, index) in enumerate(indices):
             rows = picked(
                 limits,
@@ -351,7 +379,7 @@
 
 
 def update_kernel(
-    sum_ref, got_ref, inv_ref, order_ref, flags_ref, counts_ref, amp_ref,
+    sum_ref, got_ref, inv_ref, order_ref, flags_ref, spots_ref,
     cur_ref, log_ref, info_ref, pair_ref, odd_ref,
 ):
     walkers, _, orbs, nel = inv_ref.shape
@@ -421,12 +449,12 @@
         log_ref[w : w + 1, :] = (
             jnp.broadcast_to(jnp.sum(both, axis=1, keepdims=True), (1, nel))
             + info_ref[2 + w : 3 + w, :nel]
-            + amp_ref[:, w : w + 1]
+            + spots_ref[walkers, 2:3, w : w + 1]
         )
     half = walkers // 2
     per = 2 * orbs
     tail = half * per
-    for pay, indices in sent(counts_ref, half, pair_ref, odd_ref):
+    for pay, indices in sent(spots_ref, walkers, pair_ref, odd_ref):
         pay[tail : tail + INFO, :] = info_ref[...]
         pay[tail + INFO :, :] = jnp.zeros((pay.shape[0] - tail - INFO, LANES), F32)
         for j, (limits, index) in enumerate(indices):
@@ -442,7 +470,7 @@
 
 
 def place_kernel(
-    counts_ref, cur_ref, done_ref, spots_ref, log_ref, info_ref,
+    cur_ref, done_ref, spots_ref, log_ref, info_ref,
     pair_s_ref, odd_s_ref, pair_i_ref, odd_i_ref,
     inv_out, sla_out, pos_out, log_out, energy_out, mean_out,
 ):
@@ -459,7 +487,7 @@
     groups = lax.axis_size("walkers")
     mean = jnp.sum(info[1:2], axis=1, keepdims=True)
     mean_out[...] = mean / (1.0 * walkers * groups)
-    limits = limits_of(counts_ref)
+    limits = limits_of(spots_ref, walkers)
     slots = lax.broadcasted_iota(jnp.int32, (1, walkers), 1)
     here = [[cur_ref[w, s] for w in range(walkers)] for s in (0, 1)]
     here += [[done_ref[w, s] for w in range(walkers)] for s in (0, 1)]
@@ -515,12 +543,12 @@
     energy_out[...] = energy_new
 
 
-def call(kernel, outs, in_specs, scratch=(), us=1.0, name=None, vmem=32 * 2**20):
+def call(kernel, outs, in_specs, scratch=(), us=1.0, name=None, out_specs=None, vmem=32 * 2**20):
     return pl.pallas_call(
         kernel,
         out_shape=outs,
         in_specs=in_specs,
-        out_specs=jax.tree.map(lambda _: VMEM, outs),
+        out_specs=out_specs or jax.tree.map(lambda _: VMEM, outs),
         scratch_shapes=list(scratch),
         compiler_params=pltpu.CompilerParams(vmem_limit_bytes=vmem),
         cost_estimate=pl.CostEstimate(flops=int(us * 1.1e9), bytes_accessed=2**18, transcendentals=0),
@@ -558,17 +586,19 @@
 
     places = positions.transpose(1, 0, 2)
     steps = displacements.transpose(1, 0, 2)
+    operands = (places, steps, move_order, accepted, counts, jastrow, log_amp)
+    made = (shape(walkers + 1, 16, LANES), shape(INFO, wide))
     spots, info = call(
         energy_kernel,
-        (
-            shape(walkers, 16, LANES),
-            shape(INFO, wide),
-        ),
-        [VMEM] * 5,
+        made,
+        [ANY] * len(operands),
+        out_specs=(ANY, ANY),
+        scratch=[pltpu.VMEM(x.shape, x.dtype) for x in operands + made]
+        + [pltpu.SemaphoreType.DMA((len(operands),)), pltpu.SemaphoreType.DMA((len(made),))],
         us=2,
         vmem=61 * 2**20,
         name="energy",
-    )(places, steps, move_order, accepted, counts)
+    )(*operands)
 
     hops = members * 2
     step = hops
@@ -578,7 +608,7 @@
     joint = [
         (d * members + o, (d ^ (2 * hop)) * members + o)
         for o in range(members)
-        for hop in [(o + 1) % 3 if members > 3 and o < 3 else o]
+        for hop in [(1, 3, 0, 2)[o] if members == 4 else o]
         for d in range(groups)
         if 2 * hop < groups
     ]
@@ -587,13 +617,12 @@
     shift = call(
         shift_kernel,
         shape(2, walkers * moves, orbs),
-        [VMEM] * 9,
+        [VMEM] * 7,
         scratch=[pltpu.VMEM((2, walkers * moves, basis), F32)],
         us=3,
         name="shift",
     )(
-        places, steps, move_order, accepted, counts, jastrow, centers,
-        exponents.reshape(1, basis), orbitals,
+        places, steps, move_order, accepted, centers, exponents.reshape(1, basis), orbitals,
     )
 
     part, done, pair_s, odd_s = call(
@@ -604,10 +633,10 @@
             shape(tall, LANES),
             shape(tall, LANES),
         ),
-        [VMEM] * 9,
+        [VMEM] * 7,
         us=2,
         name="partial",
-    )(shift, move_order, accepted, counts, inverse, slater, spots, info, jastrow)
+    )(shift, move_order, accepted, inverse, slater, spots, info)
 
     total = part
     got = jnp.zeros_like(part)
@@ -637,10 +666,10 @@
             shape(tall, LANES),
             shape(tall, LANES),
         ),
-        [VMEM] * 7,
+        [VMEM] * 6,
         us=4,
         name="update",
-    )(total, got, inverse, move_order, accepted, counts, log_amp)
+    )(total, got, inverse, move_order, accepted, spots)
 
     pair_i = lax.ppermute(pair_i, "walkers", pairs)
     odd_i = lax.ppermute(odd_i, "walkers", odds)
@@ -655,10 +684,10 @@
             shape(1, walkers),
             shape(1, 1),
         ),
-        [VMEM] * 10,
+        [VMEM] * 9,
         us=1.5,
         name="place",
-    )(counts, current, done, spots, logs, info, pair_s, odd_s, pair_i, odd_i)
+    )(current, done, spots, logs, info, pair_s, odd_s, pair_i, odd_i)
     return (
         inv_new,
         sla_new,

time: 30.8 us -> 29.9 us (0.971)
  the two profiles are of different devices: /device:TPU:16 before, /device:TPU:8 now
where the time goes in v6:
time: 29.9 us; the launch traced here: 29.4 us
  starting transfers between devices  12.2 us (41%)
  Pallas kernels  8.88 us (30%)
  waiting for transfers between devices  7.47 us (25%)
  between operations  0.86 us (3%)
    ppermute x1, waiting for transfers between devices, body(): odd_i = lax.ppermute(odd_i, 'walkers', odds)  3.75 us
    ppermute x1, starting transfers between devices, body(): odd_i = lax.ppermute(odd_i, 'walkers', odds)  3.34 us
    pallas_call x1, Pallas kernels, body(): call(energy_kernel, made, [ANY] * len(operands), out_specs=(ANY, ANY), sc...  3.14 us
    ppermute x1, starting transfers between devices, body(): odd_s = lax.ppermute(odd_s, 'walkers', odds)  2.29 us
    pallas_call x1, Pallas kernels, body(): call(update_kernel, (shape(walkers, 2, orbs, nel), shape(8, nel), shape(I...  2.2 us
    ppermute x1, waiting for transfers between devices, body(): info = lax.ppermute(info, ('walkers', 'orb'), joint)  1.93 us
    ppermute x1, starting transfers between devices, body(): info = lax.ppermute(info, ('walkers', 'orb'), joint)  1.92 us
    ppermute x2, waiting for transfers between devices, body(): got = lax.ppermute(total, 'orb', partner)  1.78 us
  transfers between devices with their start and end apart: 7, of which 4 were waited for; matrix products, arithmetic and copies ran while one was open for 0% of the time, Pallas kernels for 13%

profile of v6, /device:TPU:8, one launch (start us, length us, event | category | flops | bytes accessed | tf_op | source)
XLA Modules:
  0.0 29.4 jit_solution(13535948264577214920)
XLA Ops:
  0.6 0.0 copy-start
  0.7 3.1 %energy.1 = (f32[5,16,128]{2,1,0:T(8,128)}, f32[8,128]{1,0:T(8,128)}) custom-call(f32[3,4,256]{2,1,0:T(4,128)} %bitcast.10, f32[3,4,256]{2,1,0:T(4,128)} %bitcast.12, s32[4,2,128]{2,1,0:T(2,128)} %order_ref.5, s32[4,2,32]{2,1,0:T(2,128)} %flags_ref.5, s32[1,4]{1,0:T(1,128)} %bitcast.15, f32[1,4]{1,0:T(1,128)} %bitcast.16, f32[1,4]{1,0:T(1,128)} %bitcast.17), custom_call_target="tpu_custom_call" | custom-call | flops 2200000000 | bytes 262144 | tf_op jit(solution)/shard_map/energy/pallas_call | solution.py:591
  3.9 1.9 %collective-permute-start = (f32[8,128]{1,0:T(8,128)}, f32[8,128]{1,0:T(8,128)S(1)}, u32[]{:S(2)}, u32[]{:S(2)}) collective-permute-start(f32[8,128]{1,0:T(8,128)} %get-tuple-element.24), channel_id=1, source_target_pairs={{0,8},{4,12},{8,0},{12,4},{16,24},{20,28},{24,16},{28,20},{1,25},{... | collective-permute-start | bytes 12296 | tf_op jit(solution)/shard_map/ppermute | solution.py:615
  5.9 0.0 copy-start.1
  5.9 0.0 copy-start.2
  5.9 0.0 copy-start.9
  5.9 1.7 %shift.1.shift_ref = f32[2,128,32]{2,1,0:T(8,128)S(1)} custom-call(f32[3,4,256]{2,1,0:T(4,128)S(1)} %bitcast.11, f32[3,4,256]{2,1,0:T(4,128)S(1)} %bitcast.13, s32[4,2,128]{2,1,0:T(2,128)S(1)} %copy-done.7, s32[4,2,32]{2,1,0:T(2,128)S(1)} %copy-done.8, f32[3,1024]{1,0:T(4,128)S(1)} %copy-done.3, f32[1,1024]{1,0:T(1,128)S(1)} %bitcast.14, ...), custom_call_target="tpu_custom_call" | custom-call | flops 3300000000 | bytes 262144 | tf_op jit(solution)/shard_map/shift/pallas_call | solution.py:617
  7.6 1.9 %collective-permute-done.info_ref = f32[8,128]{1,0:T(8,128)S(1)} collective-permute-done((f32[8,128]{1,0:T(8,128)}, f32[8,128]{1,0:T(8,128)S(1)}, u32[]{:S(2)}, u32[]{:S(2)}) %collective-permute-start) | collective-permute-done | bytes 4128 | tf_op jit(solution)/shard_map/ppermute | solution.py:615
  9.6 0.0 copy-done.2
  9.6 0.9 %partial.1 = (f32[264,128]{1,0:T(8,128)S(1)}, f32[4,2,32,128]{3,2,1,0:T(8,128)S(1)}, f32[144,128]{1,0:T(8,128)S(1)}, f32[144,128]{1,0:T(8,128)S(1)}) custom-call(f32[2,128,32]{2,1,0:T(8,128)S(1)} %shift.1.shift_ref, s32[4,2,128]{2,1,0:T(2,128)S(1)} %copy-done.7, s32[4,2,32]{2,1,0:T(2,128)S(1)} %copy-done.8, f32[4,2,32,128]{3,2,1,0:T(8,128)S(1)} %copy-done.2, ...), custom_call_target="tpu_custom_call" | custom-call | flops 2200000000 | bytes 262144 | tf_op jit(solution)/shard_map/partial/pallas_call | solution.py:628
  10.4 0.0 collective-permute-start.1
  10.5 1.3 %collective-permute-done.1.other_ref = f32[264,128]{1,0:T(8,128)S(1)} collective-permute-done((f32[264,128]{1,0:T(8,128)S(1)}, f32[264,128]{1,0:T(8,128)S(1)}, u32[]{:S(2)}, u32[]{:S(2)}) %collective-permute-start.1) | collective-permute-done | bytes 135200 | tf_op jit(solution)/shard_map/ppermute | solution.py:646
  11.8 1.4 %collective-permute-start.2 = (f32[264,128]{1,0:T(8,128)S(1)}, f32[264,128]{1,0:T(8,128)S(1)}, u32[]{:S(2)}, u32[]{:S(2)}) collective-permute-start(f32[264,128]{1,0:T(8,128)S(1)} %add.1.sum_ref), channel_id=1, source_target_pairs={{0,2},{1,3},{2,0},{3,1},{4,6},{5,7},{6,4},{7,5},{8,10},{9,11},{10,... | collective-permute-start | bytes 405512 | tf_op jit(solution)/shard_map/ppermute | solution.py:646
  13.3 1.5 %collective-permute-start.3 = (f32[144,128]{1,0:T(8,128)S(1)}, f32[144,128]{1,0:T(8,128)S(1)}, u32[]{:S(2)}, u32[]{:S(2)}) collective-permute-start(f32[144,128]{1,0:T(8,128)S(1)} %get-tuple-element.30), channel_id=1, source_target_pairs={{0,4},{4,0},{8,12},{12,8},{16,20},{20,16},{24,28},{28,24},{1,5},{5... | collective-permute-start | bytes 221192 | tf_op jit(solution)/shard_map/ppermute | solution.py:657
  14.8 2.3 %collective-permute-start.4 = (f32[144,128]{1,0:T(8,128)S(1)}, f32[144,128]{1,0:T(8,128)S(1)}, u32[]{:S(2)}, u32[]{:S(2)}) collective-permute-start(f32[144,128]{1,0:T(8,128)S(1)} %get-tuple-element.31), channel_id=1, source_target_pairs={{4,8},{12,16},{20,24},{8,4},{16,12},{24,20},{5,9},{13,17},{21,25},... | collective-permute-start | bytes 221192 | tf_op jit(solution)/shard_map/ppermute | solution.py:658
  17.1 0.4 %collective-permute-done.2.got_ref = f32[264,128]{1,0:T(8,128)S(1)} collective-permute-done((f32[264,128]{1,0:T(8,128)S(1)}, f32[264,128]{1,0:T(8,128)S(1)}, u32[]{:S(2)}, u32[]{:S(2)}) %collective-permute-start.2) | collective-permute-done | bytes 135200 | tf_op jit(solution)/shard_map/ppermute | solution.py:646
  17.5 2.2 %update.1 = (f32[4,2,32,128]{3,2,1,0:T(8,128)S(1)}, f32[8,128]{1,0:T(8,128)S(1)}, f32[8,128]{1,0:T(8,128)S(1)}, f32[144,128]{1,0:T(8,128)S(1)}, f32[144,128]{1,0:T(8,128)S(1)}) custom-call(f32[264,128]{1,0:T(8,128)S(1)} %add.1.sum_ref, f32[264,128]{1,0:T(8,128)S(1)} %collective-permute-done.2.got_ref, f32[4,2,32,128]{3,2,1,0:T(8,128)S(1)} %copy-done.2, ...), custom_call_target="tpu_custom_call" | custom-call | flops 4400000000 | bytes 262144 | tf_op jit(solution)/shard_map/update/pallas_call | solution.py:660
  19.7 1.6 %collective-permute-start.5 = (f32[144,128]{1,0:T(8,128)S(1)}, f32[144,128]{1,0:T(8,128)S(1)}, u32[]{:S(2)}, u32[]{:S(2)}) collective-permute-start(f32[144,128]{1,0:T(8,128)S(1)} %get-tuple-element.32), channel_id=1, source_target_pairs={{0,4},{4,0},{8,12},{12,8},{16,20},{20,16},{24,28},{28,24},{1,5},{5... | collective-permute-start | bytes 221192 | tf_op jit(solution)/shard_map/ppermute | solution.py:674
  21.4 3.3 %collective-permute-start.6 = (f32[144,128]{1,0:T(8,128)S(1)}, f32[144,128]{1,0:T(8,128)S(1)}, u32[]{:S(2)}, u32[]{:S(2)}) collective-permute-start(f32[144,128]{1,0:T(8,128)S(1)} %get-tuple-element.33), channel_id=1, source_target_pairs={{4,8},{12,16},{20,24},{8,4},{16,12},{24,20},{5,9},{13,17},{21,25},... | collective-permute-start | bytes 221192 | tf_op jit(solution)/shard_map/ppermute | solution.py:675
  24.7 0.0 collective-permute-done.3.pair_s_ref
  24.7 0.0 collective-permute-done.4.odd_s_ref
  24.8 0.0 collective-permute-done.5.pair_i_ref
  24.8 3.8 %collective-permute-done.6.odd_i_ref = f32[144,128]{1,0:T(8,128)S(1)} collective-permute-done((f32[144,128]{1,0:T(8,128)S(1)}, f32[144,128]{1,0:T(8,128)S(1)}, u32[]{:S(2)}, u32[]{:S(2)}) %collective-permute-start.6) | collective-permute-done | bytes 73760 | tf_op jit(solution)/shard_map/ppermute | solution.py:675
  28.5 0.9 %place.1 = (f32[4,2,32,128]{3,2,1,0:T(8,128)}, f32[4,2,32,128]{3,2,1,0:T(8,128)}, f32[3,4,256]{2,1,0:T(4,128)}, f32[1,4]{1,0:T(1,128)}, f32[1,4]{1,0:T(1,128)}, /*index=5*/f32[1,1]{1,0:T(1,128)}) custom-call(f32[4,2,32,128]{3,2,1,0:T(8,128)S(1)} %get-tuple-element.26.cur_ref, f32[4,2,32,128]{3,2,1,0:T(8,128)S(1)} %get-tuple-element.27.done_ref, ...), custom_call_target="tpu_custom_call" | custom-call | flops 1650000000 | bytes 262144 | tf_op jit(solution)/shard_map/place/pallas_call | solution.py:677
  (16 shorter events, 0.0 us)
Async XLA Ops:
  0.6 5.1 %copy-start = (f32[2,32,1024]{2,1,0:T(8,128)S(1)}, f32[2,32,1024]{2,1,0:T(8,128)}, u32[]{:S(2)}) copy-start(f32[2,32,1024]{2,1,0:T(8,128)} %orb_ref.1) | copy-start | bytes 786436
  0.6 5.1 %copy-start.3 = (f32[3,1024]{1,0:T(4,128)S(1)}, f32[3,1024]{1,0:T(4,128)}, u32[]{:S(2)}) copy-start(f32[3,1024]{1,0:T(4,128)} %cen_ref.1) | copy-start | bytes 36868
  0.7 5.1 %copy-start.4 = (f32[4,3,256]{2,0,1:T(4,128)S(1)}, f32[4,3,256]{2,0,1:T(4,128)}, u32[]{:S(2)}) copy-start(f32[4,3,256]{2,0,1:T(4,128)} %param.14) | copy-start | bytes 36868
  0.7 5.1 %copy-start.5 = (f32[4,3,256]{2,0,1:T(4,128)S(1)}, f32[4,3,256]{2,0,1:T(4,128)}, u32[]{:S(2)}) copy-start(f32[4,3,256]{2,0,1:T(4,128)} %param.15) | copy-start | bytes 36868
  0.7 5.1 %copy-start.6 = (f32[1024]{0:T(1024)S(1)}, f32[1024]{0:T(1024)}, u32[]{:S(2)}) copy-start(f32[1024]{0:T(1024)} %param.21) | copy-start | bytes 12292
  0.7 5.1 %copy-start.7 = (s32[4,2,128]{2,1,0:T(2,128)S(1)}, s32[4,2,128]{2,1,0:T(2,128)}, u32[]{:S(2)}) copy-start(s32[4,2,128]{2,1,0:T(2,128)} %order_ref.5) | copy-start | bytes 12292
  0.7 5.1 %copy-start.8 = (s32[4,2,32]{2,1,0:T(2,128)S(1)}, s32[4,2,32]{2,1,0:T(2,128)}, u32[]{:S(2)}) copy-start(s32[4,2,32]{2,1,0:T(2,128)} %flags_ref.5) | copy-start | bytes 3076
  3.9 5.7 %collective-permute-start = (f32[8,128]{1,0:T(8,128)}, f32[8,128]{1,0:T(8,128)S(1)}, u32[]{:S(2)}, u32[]{:S(2)}) collective-permute-start(f32[8,128]{1,0:T(8,128)} %get-tuple-element.24), channel_id=1, source_target_pairs={{0,8},{4,12},{8,0},{12,4},{16,24},{20,28},{24,16},{28,20},{1,25},{... | collective-permute-start | bytes 12296 | tf_op jit(solution)/shard_map/ppermute | solution.py:615
  5.9 3.7 %copy-start.1 = (f32[4,2,32,128]{3,2,1,0:T(8,128)S(1)}, f32[4,2,32,128]{3,2,1,0:T(8,128)}, u32[]{:S(2)}) copy-start(f32[4,2,32,128]{3,2,1,0:T(8,128)} %sla_ref.1) | copy-start | bytes 393220
  5.9 3.7 %copy-start.2 = (f32[4,2,32,128]{3,2,1,0:T(8,128)S(1)}, f32[4,2,32,128]{3,2,1,0:T(8,128)}, u32[]{:S(2)}) copy-start(f32[4,2,32,128]{3,2,1,0:T(8,128)} %inv_ref.3) | copy-start | bytes 393220
  5.9 3.7 %copy-start.9 = (f32[5,16,128]{2,1,0:T(8,128)S(1)}, f32[5,16,128]{2,1,0:T(8,128)}, u32[]{:S(2)}) copy-start(f32[5,16,128]{2,1,0:T(8,128)} %get-tuple-element.23.spots_ref) | copy-start | bytes 122884
  10.4 1.4 %collective-permute-start.1 = (f32[264,128]{1,0:T(8,128)S(1)}, f32[264,128]{1,0:T(8,128)S(1)}, u32[]{:S(2)}, u32[]{:S(2)}) collective-permute-start(f32[264,128]{1,0:T(8,128)S(1)} %get-tuple-element.25.mine_ref), channel_id=1, source_target_pairs={{0,1},{1,0},{2,3},{3,2},{4,5},{5,4},{6,7},{7,6},{8,9},{9,8},{10,11... | collective-permute-start | bytes 405512 | tf_op jit(solution)/shard_map/ppermute | solution.py:646
  11.8 5.7 %collective-permute-start.2 = (f32[264,128]{1,0:T(8,128)S(1)}, f32[264,128]{1,0:T(8,128)S(1)}, u32[]{:S(2)}, u32[]{:S(2)}) collective-permute-start(f32[264,128]{1,0:T(8,128)S(1)} %add.1.sum_ref), channel_id=1, source_target_pairs={{0,2},{1,3},{2,0},{3,1},{4,6},{5,7},{6,4},{7,5},{8,10},{9,11},{10,... | collective-permute-start | bytes 405512 | tf_op jit(solution)/shard_map/ppermute | solution.py:646
  13.3 11.5 %collective-permute-start.3 = (f32[144,128]{1,0:T(8,128)S(1)}, f32[144,128]{1,0:T(8,128)S(1)}, u32[]{:S(2)}, u32[]{:S(2)}) collective-permute-start(f32[144,128]{1,0:T(8,128)S(1)} %get-tuple-element.30), channel_id=1, source_target_pairs={{0,4},{4,0},{8,12},{12,8},{16,20},{20,16},{24,28},{28,24},{1,5},{5... | collective-permute-start | bytes 221192 | tf_op jit(solution)/shard_map/ppermute | solution.py:657
  14.8 9.9 %collective-permute-start.4 = (f32[144,128]{1,0:T(8,128)S(1)}, f32[144,128]{1,0:T(8,128)S(1)}, u32[]{:S(2)}, u32[]{:S(2)}) collective-permute-start(f32[144,128]{1,0:T(8,128)S(1)} %get-tuple-element.31), channel_id=1, source_target_pairs={{4,8},{12,16},{20,24},{8,4},{16,12},{24,20},{5,9},{13,17},{21,25},... | collective-permute-start | bytes 221192 | tf_op jit(solution)/shard_map/ppermute | solution.py:658
  19.7 5.0 %collective-permute-start.5 = (f32[144,128]{1,0:T(8,128)S(1)}, f32[144,128]{1,0:T(8,128)S(1)}, u32[]{:S(2)}, u32[]{:S(2)}) collective-permute-start(f32[144,128]{1,0:T(8,128)S(1)} %get-tuple-element.32), channel_id=1, source_target_pairs={{0,4},{4,0},{8,12},{12,8},{16,20},{20,16},{24,28},{28,24},{1,5},{5... | collective-permute-start | bytes 221192 | tf_op jit(solution)/shard_map/ppermute | solution.py:674
  21.4 7.1 %collective-permute-start.6 = (f32[144,128]{1,0:T(8,128)S(1)}, f32[144,128]{1,0:T(8,128)S(1)}, u32[]{:S(2)}, u32[]{:S(2)}) collective-permute-start(f32[144,128]{1,0:T(8,128)S(1)} %get-tuple-element.33), channel_id=1, source_target_pairs={{4,8},{12,16},{20,24},{8,4},{16,12},{24,20},{5,9},{13,17},{21,25},... | collective-permute-start | bytes 221192 | tf_op jit(solution)/shard_map/ppermute | solution.py:675

commit v7 on v6

--- a/solution.py
+++ b/solution.py
@@ -244,7 +244,7 @@
     )
     now = [pos_ref[c] + dis_ref[c] * applied for c in range(3)]
     turn = turned(jnp.concatenate(now, axis=0))
-    weighted = jnp.zeros((1, 1), F32)
+    weighted = jnp.zeros((1, nel), F32)
     counts = counts_ref[...].astype(F32)
     for w in range(walkers):
         nrows = [now[c][w : w + 1] for c in range(3)]
@@ -257,14 +257,13 @@
             for h in (0, 1)
         ]
         same, other = pair_tiles([tall], [halves], nel, [lambda q: lax.rsqrt(q + 1.0)] * 2)
-        whole = summed(same + 2.0 * other)
-        energy = (whole - 1.0 * both) / (1.0 * both * (both - 1))
-        wide = [jnp.broadcast_to(energy, (1, LANES)), jnp.zeros((7 - 3 * (both // LANES), LANES), F32)]
+        soft = jnp.sum(same + 2.0 * other, axis=0, keepdims=True)
+        wide = [soft, jnp.zeros((7 - 3 * (both // LANES), LANES), F32)]
         spots_ref[w, :8] = jnp.concatenate(in_rows(nrows) + wide[: 1 + (3 * (both // LANES) < 7)], axis=0)
         spots_ref[w, 8 : 8 + 3 * (both // LANES)] = jnp.concatenate(
             in_rows([pos_ref[c, w : w + 1] for c in range(3)]), axis=0
         )
-        weighted = weighted + energy * counts[:, w : w + 1]
+        weighted = weighted + soft * counts[:, w : w + 1]
     me = lax.axis_index("walkers")
     lanes = lax.broadcasted_iota(jnp.int32, info_ref.shape, 1)
     rows = lax.broadcasted_iota(jnp.int32, info_ref.shape, 0)
@@ -272,11 +271,8 @@
     for row, some in enumerate((counts, jas_ref[...], amp_ref[...])):
         spots_ref[walkers, row : row + 1, : some.shape[1]] = some
     number = jnp.sum(counts, axis=1, keepdims=True)
-    info_ref[...] = jnp.where(
-        lanes == me,
-        jnp.where(rows == 0, number, jnp.where(rows == 1, weighted, 0.0)),
-        0.0,
-    )
+    info_ref[...] = jnp.where((lanes == me) & (rows == 0), number, 0.0)
+    info_ref[1:2, :nel] = weighted
     copies = [
         pltpu.make_async_copy(info_ref, info_out, stores.at[0]),
         pltpu.make_async_copy(spots_ref, spots_out, stores.at[1]),
@@ -485,8 +481,14 @@
     lanes = lax.broadcasted_iota(jnp.int32, (1, info.shape[1]), 1)
     before = jnp.sum(jnp.where(lanes < me, info[0:1], 0.0), axis=1, keepdims=True)
     groups = lax.axis_size("walkers")
-    mean = jnp.sum(info[1:2], axis=1, keepdims=True)
-    mean_out[...] = mean / (1.0 * walkers * groups)
+    both = pos_out.shape[2]
+
+    def energy_of(row, copies):
+        soft = jnp.sum(row, axis=1, keepdims=True)
+        return (soft - 1.0 * both * copies) / (1.0 * both * (both - 1))
+
+    copies = jnp.sum(info[0:1], axis=1, keepdims=True)
+    mean_out[...] = energy_of(info[1:2], copies) / (1.0 * walkers * groups)
     limits = limits_of(spots_ref, walkers)
     slots = lax.broadcasted_iota(jnp.int32, (1, walkers), 1)
     here = [[cur_ref[w, s] for w in range(walkers)] for s in (0, 1)]
@@ -537,7 +539,7 @@
                 ]
         log_new = jnp.where(slots == j, new[5][:, :walkers], log_new)
         energy_new = jnp.where(
-            slots == j, new[4][3 * width : 3 * width + 1, :walkers], energy_new
+            slots == j, energy_of(new[4][3 * width : 3 * width + 1], 1.0), energy_new
         )
     log_out[...] = log_new
     energy_out[...] = energy_new

time: 29.9 us -> 29.4 us (0.983)
  Pallas kernels: 8.88 us -> 8.31 us
    pallas_call x1, Pallas kernels: 3.14 us -> 2.57 us  [body(): call(energy_kernel, made, [ANY] * len(operands), out_specs=(ANY, ANY), sc...]
  transfers between devices with their start and end apart: 7 -> 7, of which waited for: 4 -> 4; matrix products, arithmetic and copies ran while one was open for 0% -> 0% of each run, Pallas kernels for 13% -> 14%
where the time goes in v7:
time: 29.4 us; the launch traced here: 28.9 us
  starting transfers between devices  12.2 us (41%)
  Pallas kernels  8.31 us (28%)
  waiting for transfers between devices  7.47 us (25%)
  between operations  0.86 us (3%)
    ppermute x1, waiting for transfers between devices, body(): odd_i = lax.ppermute(odd_i, 'walkers', odds)  3.75 us
    ppermute x1, starting transfers between devices, body(): odd_i = lax.ppermute(odd_i, 'walkers', odds)  3.34 us
    pallas_call x1, Pallas kernels, body(): call(energy_kernel, made, [ANY] * len(operands), out_specs=(ANY, ANY), sc...  2.57 us
    ppermute x1, starting transfers between devices, body(): odd_s = lax.ppermute(odd_s, 'walkers', odds)  2.29 us
    pallas_call x1, Pallas kernels, body(): call(update_kernel, (shape(walkers, 2, orbs, nel), shape(8, nel), shape(I...  2.2 us
    ppermute x1, waiting for transfers between devices, body(): info = lax.ppermute(info, ('walkers', 'orb'), joint)  1.93 us
    ppermute x1, starting transfers between devices, body(): info = lax.ppermute(info, ('walkers', 'orb'), joint)  1.92 us
    ppermute x2, waiting for transfers between devices, body(): got = lax.ppermute(total, 'orb', partner)  1.78 us
  transfers between devices with their start and end apart: 7, of which 4 were waited for; matrix products, arithmetic and copies ran while one was open for 0% of the time, Pallas kernels for 14%

profile of v7, /device:TPU:8, one launch (start us, length us, event | category | flops | bytes accessed | tf_op | source)
XLA Modules:
  0.0 28.9 jit_solution(11445147482121017795)
XLA Ops:
  0.7 2.6 %energy.1 = (f32[5,16,128]{2,1,0:T(8,128)}, f32[8,128]{1,0:T(8,128)}) custom-call(f32[3,4,256]{2,1,0:T(4,128)} %bitcast.10, f32[3,4,256]{2,1,0:T(4,128)} %bitcast.12, s32[4,2,128]{2,1,0:T(2,128)} %order_ref.5, s32[4,2,32]{2,1,0:T(2,128)} %flags_ref.5, s32[1,4]{1,0:T(1,128)} %bitcast.15, f32[1,4]{1,0:T(1,128)} %bitcast.16, f32[1,4]{1,0:T(1,128)} %bitcast.17), custom_call_target="tpu_custom_call" | custom-call | flops 2200000000 | bytes 262144 | tf_op jit(solution)/shard_map/energy/pallas_call | solution.py:593
  3.3 1.9 %collective-permute-start = (f32[8,128]{1,0:T(8,128)}, f32[8,128]{1,0:T(8,128)S(1)}, u32[]{:S(2)}, u32[]{:S(2)}) collective-permute-start(f32[8,128]{1,0:T(8,128)} %get-tuple-element.24), channel_id=1, source_target_pairs={{0,8},{4,12},{8,0},{12,4},{16,24},{20,28},{24,16},{28,20},{1,25},{... | collective-permute-start | bytes 12296 | tf_op jit(solution)/shard_map/ppermute | solution.py:617
  5.2 0.0 copy-done
  5.2 0.0 copy-done.3
  5.3 0.0 copy-start.1
  5.3 0.0 copy-start.2
  5.3 0.0 copy-start.9
  5.3 1.7 %shift.1.shift_ref = f32[2,128,32]{2,1,0:T(8,128)S(1)} custom-call(f32[3,4,256]{2,1,0:T(4,128)S(1)} %bitcast.11, f32[3,4,256]{2,1,0:T(4,128)S(1)} %bitcast.13, s32[4,2,128]{2,1,0:T(2,128)S(1)} %copy-done.7, s32[4,2,32]{2,1,0:T(2,128)S(1)} %copy-done.8, f32[3,1024]{1,0:T(4,128)S(1)} %copy-done.3, f32[1,1024]{1,0:T(1,128)S(1)} %bitcast.14, ...), custom_call_target="tpu_custom_call" | custom-call | flops 3300000000 | bytes 262144 | tf_op jit(solution)/shard_map/shift/pallas_call | solution.py:619
  7.1 1.9 %collective-permute-done.info_ref = f32[8,128]{1,0:T(8,128)S(1)} collective-permute-done((f32[8,128]{1,0:T(8,128)}, f32[8,128]{1,0:T(8,128)S(1)}, u32[]{:S(2)}, u32[]{:S(2)}) %collective-permute-start) | collective-permute-done | bytes 4128 | tf_op jit(solution)/shard_map/ppermute | solution.py:617
  9.0 0.9 %partial.1 = (f32[264,128]{1,0:T(8,128)S(1)}, f32[4,2,32,128]{3,2,1,0:T(8,128)S(1)}, f32[144,128]{1,0:T(8,128)S(1)}, f32[144,128]{1,0:T(8,128)S(1)}) custom-call(f32[2,128,32]{2,1,0:T(8,128)S(1)} %shift.1.shift_ref, s32[4,2,128]{2,1,0:T(2,128)S(1)} %copy-done.7, s32[4,2,32]{2,1,0:T(2,128)S(1)} %copy-done.8, f32[4,2,32,128]{3,2,1,0:T(8,128)S(1)} %copy-done.2, ...), custom_call_target="tpu_custom_call" | custom-call | flops 2200000000 | bytes 262144 | tf_op jit(solution)/shard_map/partial/pallas_call | solution.py:630
  9.9 0.0 collective-permute-start.1
  9.9 1.3 %collective-permute-done.1.other_ref = f32[264,128]{1,0:T(8,128)S(1)} collective-permute-done((f32[264,128]{1,0:T(8,128)S(1)}, f32[264,128]{1,0:T(8,128)S(1)}, u32[]{:S(2)}, u32[]{:S(2)}) %collective-permute-start.1) | collective-permute-done | bytes 135200 | tf_op jit(solution)/shard_map/ppermute | solution.py:648
  11.3 1.4 %collective-permute-start.2 = (f32[264,128]{1,0:T(8,128)S(1)}, f32[264,128]{1,0:T(8,128)S(1)}, u32[]{:S(2)}, u32[]{:S(2)}) collective-permute-start(f32[264,128]{1,0:T(8,128)S(1)} %add.1.sum_ref), channel_id=1, source_target_pairs={{0,2},{1,3},{2,0},{3,1},{4,6},{5,7},{6,4},{7,5},{8,10},{9,11},{10,... | collective-permute-start | bytes 405512 | tf_op jit(solution)/shard_map/ppermute | solution.py:648
  12.7 1.5 %collective-permute-start.3 = (f32[144,128]{1,0:T(8,128)S(1)}, f32[144,128]{1,0:T(8,128)S(1)}, u32[]{:S(2)}, u32[]{:S(2)}) collective-permute-start(f32[144,128]{1,0:T(8,128)S(1)} %get-tuple-element.30), channel_id=1, source_target_pairs={{0,4},{4,0},{8,12},{12,8},{16,20},{20,16},{24,28},{28,24},{1,5},{5... | collective-permute-start | bytes 221192 | tf_op jit(solution)/shard_map/ppermute | solution.py:659
  14.2 2.3 %collective-permute-start.4 = (f32[144,128]{1,0:T(8,128)S(1)}, f32[144,128]{1,0:T(8,128)S(1)}, u32[]{:S(2)}, u32[]{:S(2)}) collective-permute-start(f32[144,128]{1,0:T(8,128)S(1)} %get-tuple-element.31), channel_id=1, source_target_pairs={{4,8},{12,16},{20,24},{8,4},{16,12},{24,20},{5,9},{13,17},{21,25},... | collective-permute-start | bytes 221192 | tf_op jit(solution)/shard_map/ppermute | solution.py:660
  16.5 0.4 %collective-permute-done.2.got_ref = f32[264,128]{1,0:T(8,128)S(1)} collective-permute-done((f32[264,128]{1,0:T(8,128)S(1)}, f32[264,128]{1,0:T(8,128)S(1)}, u32[]{:S(2)}, u32[]{:S(2)}) %collective-permute-start.2) | collective-permute-done | bytes 135200 | tf_op jit(solution)/shard_map/ppermute | solution.py:648
  17.0 2.2 %update.1 = (f32[4,2,32,128]{3,2,1,0:T(8,128)S(1)}, f32[8,128]{1,0:T(8,128)S(1)}, f32[8,128]{1,0:T(8,128)S(1)}, f32[144,128]{1,0:T(8,128)S(1)}, f32[144,128]{1,0:T(8,128)S(1)}) custom-call(f32[264,128]{1,0:T(8,128)S(1)} %add.1.sum_ref, f32[264,128]{1,0:T(8,128)S(1)} %collective-permute-done.2.got_ref, f32[4,2,32,128]{3,2,1,0:T(8,128)S(1)} %copy-done.2, ...), custom_call_target="tpu_custom_call" | custom-call | flops 4400000000 | bytes 262144 | tf_op jit(solution)/shard_map/update/pallas_call | solution.py:662
  19.2 1.6 %collective-permute-start.5 = (f32[144,128]{1,0:T(8,128)S(1)}, f32[144,128]{1,0:T(8,128)S(1)}, u32[]{:S(2)}, u32[]{:S(2)}) collective-permute-start(f32[144,128]{1,0:T(8,128)S(1)} %get-tuple-element.32), channel_id=1, source_target_pairs={{0,4},{4,0},{8,12},{12,8},{16,20},{20,16},{24,28},{28,24},{1,5},{5... | collective-permute-start | bytes 221192 | tf_op jit(solution)/shard_map/ppermute | solution.py:676
  20.8 3.3 %collective-permute-start.6 = (f32[144,128]{1,0:T(8,128)S(1)}, f32[144,128]{1,0:T(8,128)S(1)}, u32[]{:S(2)}, u32[]{:S(2)}) collective-permute-start(f32[144,128]{1,0:T(8,128)S(1)} %get-tuple-element.33), channel_id=1, source_target_pairs={{4,8},{12,16},{20,24},{8,4},{16,12},{24,20},{5,9},{13,17},{21,25},... | collective-permute-start | bytes 221192 | tf_op jit(solution)/shard_map/ppermute | solution.py:677
  24.2 0.0 collective-permute-done.3.pair_s_ref
  24.2 0.0 collective-permute-done.4.odd_s_ref
  24.2 0.0 collective-permute-done.5.pair_i_ref
  24.2 3.8 %collective-permute-done.6.odd_i_ref = f32[144,128]{1,0:T(8,128)S(1)} collective-permute-done((f32[144,128]{1,0:T(8,128)S(1)}, f32[144,128]{1,0:T(8,128)S(1)}, u32[]{:S(2)}, u32[]{:S(2)}) %collective-permute-start.6) | collective-permute-done | bytes 73760 | tf_op jit(solution)/shard_map/ppermute | solution.py:677
  27.9 0.9 %place.1 = (f32[4,2,32,128]{3,2,1,0:T(8,128)}, f32[4,2,32,128]{3,2,1,0:T(8,128)}, f32[3,4,256]{2,1,0:T(4,128)}, f32[1,4]{1,0:T(1,128)}, f32[1,4]{1,0:T(1,128)}, /*index=5*/f32[1,1]{1,0:T(1,128)}) custom-call(f32[4,2,32,128]{3,2,1,0:T(8,128)S(1)} %get-tuple-element.26.cur_ref, f32[4,2,32,128]{3,2,1,0:T(8,128)S(1)} %get-tuple-element.27.done_ref, ...), custom_call_target="tpu_custom_call" | custom-call | flops 1650000000 | bytes 262144 | tf_op jit(solution)/shard_map/place/pallas_call | solution.py:679
  (16 shorter events, 0.0 us)
Async XLA Ops:
  0.6 4.6 %copy-start = (f32[2,32,1024]{2,1,0:T(8,128)S(1)}, f32[2,32,1024]{2,1,0:T(8,128)}, u32[]{:S(2)}) copy-start(f32[2,32,1024]{2,1,0:T(8,128)} %orb_ref.1) | copy-start | bytes 786436
  0.6 4.6 %copy-start.3 = (f32[3,1024]{1,0:T(4,128)S(1)}, f32[3,1024]{1,0:T(4,128)}, u32[]{:S(2)}) copy-start(f32[3,1024]{1,0:T(4,128)} %cen_ref.1) | copy-start | bytes 36868
  0.7 4.6 %copy-start.4 = (f32[4,3,256]{2,0,1:T(4,128)S(1)}, f32[4,3,256]{2,0,1:T(4,128)}, u32[]{:S(2)}) copy-start(f32[4,3,256]{2,0,1:T(4,128)} %param.14) | copy-start | bytes 36868
  0.7 4.6 %copy-start.5 = (f32[4,3,256]{2,0,1:T(4,128)S(1)}, f32[4,3,256]{2,0,1:T(4,128)}, u32[]{:S(2)}) copy-start(f32[4,3,256]{2,0,1:T(4,128)} %param.15) | copy-start | bytes 36868
  0.7 4.6 %copy-start.6 = (f32[1024]{0:T(1024)S(1)}, f32[1024]{0:T(1024)}, u32[]{:S(2)}) copy-start(f32[1024]{0:T(1024)} %param.21) | copy-start | bytes 12292
  0.7 4.6 %copy-start.7 = (s32[4,2,128]{2,1,0:T(2,128)S(1)}, s32[4,2,128]{2,1,0:T(2,128)}, u32[]{:S(2)}) copy-start(s32[4,2,128]{2,1,0:T(2,128)} %order_ref.5) | copy-start | bytes 12292
  0.7 4.6 %copy-start.8 = (s32[4,2,32]{2,1,0:T(2,128)S(1)}, s32[4,2,32]{2,1,0:T(2,128)}, u32[]{:S(2)}) copy-start(s32[4,2,32]{2,1,0:T(2,128)} %flags_ref.5) | copy-start | bytes 3076
  3.3 5.7 %collective-permute-start = (f32[8,128]{1,0:T(8,128)}, f32[8,128]{1,0:T(8,128)S(1)}, u32[]{:S(2)}, u32[]{:S(2)}) collective-permute-start(f32[8,128]{1,0:T(8,128)} %get-tuple-element.24), channel_id=1, source_target_pairs={{0,8},{4,12},{8,0},{12,4},{16,24},{20,28},{24,16},{28,20},{1,25},{... | collective-permute-start | bytes 12296 | tf_op jit(solution)/shard_map/ppermute | solution.py:617
  5.3 3.7 %copy-start.1 = (f32[4,2,32,128]{3,2,1,0:T(8,128)S(1)}, f32[4,2,32,128]{3,2,1,0:T(8,128)}, u32[]{:S(2)}) copy-start(f32[4,2,32,128]{3,2,1,0:T(8,128)} %sla_ref.1) | copy-start | bytes 393220
  5.3 3.7 %copy-start.2 = (f32[4,2,32,128]{3,2,1,0:T(8,128)S(1)}, f32[4,2,32,128]{3,2,1,0:T(8,128)}, u32[]{:S(2)}) copy-start(f32[4,2,32,128]{3,2,1,0:T(8,128)} %inv_ref.3) | copy-start | bytes 393220
  5.3 3.7 %copy-start.9 = (f32[5,16,128]{2,1,0:T(8,128)S(1)}, f32[5,16,128]{2,1,0:T(8,128)}, u32[]{:S(2)}) copy-start(f32[5,16,128]{2,1,0:T(8,128)} %get-tuple-element.23.spots_ref) | copy-start | bytes 122884
  9.9 1.4 %collective-permute-start.1 = (f32[264,128]{1,0:T(8,128)S(1)}, f32[264,128]{1,0:T(8,128)S(1)}, u32[]{:S(2)}, u32[]{:S(2)}) collective-permute-start(f32[264,128]{1,0:T(8,128)S(1)} %get-tuple-element.25.mine_ref), channel_id=1, source_target_pairs={{0,1},{1,0},{2,3},{3,2},{4,5},{5,4},{6,7},{7,6},{8,9},{9,8},{10,11... | collective-permute-start | bytes 405512 | tf_op jit(solution)/shard_map/ppermute | solution.py:648
  11.3 5.7 %collective-permute-start.2 = (f32[264,128]{1,0:T(8,128)S(1)}, f32[264,128]{1,0:T(8,128)S(1)}, u32[]{:S(2)}, u32[]{:S(2)}) collective-permute-start(f32[264,128]{1,0:T(8,128)S(1)} %add.1.sum_ref), channel_id=1, source_target_pairs={{0,2},{1,3},{2,0},{3,1},{4,6},{5,7},{6,4},{7,5},{8,10},{9,11},{10,... | collective-permute-start | bytes 405512 | tf_op jit(solution)/shard_map/ppermute | solution.py:648
  12.7 11.5 %collective-permute-start.3 = (f32[144,128]{1,0:T(8,128)S(1)}, f32[144,128]{1,0:T(8,128)S(1)}, u32[]{:S(2)}, u32[]{:S(2)}) collective-permute-start(f32[144,128]{1,0:T(8,128)S(1)} %get-tuple-element.30), channel_id=1, source_target_pairs={{0,4},{4,0},{8,12},{12,8},{16,20},{20,16},{24,28},{28,24},{1,5},{5... | collective-permute-start | bytes 221192 | tf_op jit(solution)/shard_map/ppermute | solution.py:659
  14.2 9.9 %collective-permute-start.4 = (f32[144,128]{1,0:T(8,128)S(1)}, f32[144,128]{1,0:T(8,128)S(1)}, u32[]{:S(2)}, u32[]{:S(2)}) collective-permute-start(f32[144,128]{1,0:T(8,128)S(1)} %get-tuple-element.31), channel_id=1, source_target_pairs={{4,8},{12,16},{20,24},{8,4},{16,12},{24,20},{5,9},{13,17},{21,25},... | collective-permute-start | bytes 221192 | tf_op jit(solution)/shard_map/ppermute | solution.py:660
  19.2 5.0 %collective-permute-start.5 = (f32[144,128]{1,0:T(8,128)S(1)}, f32[144,128]{1,0:T(8,128)S(1)}, u32[]{:S(2)}, u32[]{:S(2)}) collective-permute-start(f32[144,128]{1,0:T(8,128)S(1)} %get-tuple-element.32), channel_id=1, source_target_pairs={{0,4},{4,0},{8,12},{12,8},{16,20},{20,16},{24,28},{28,24},{1,5},{5... | collective-permute-start | bytes 221192 | tf_op jit(solution)/shard_map/ppermute | solution.py:676
  20.8 7.1 %collective-permute-start.6 = (f32[144,128]{1,0:T(8,128)S(1)}, f32[144,128]{1,0:T(8,128)S(1)}, u32[]{:S(2)}, u32[]{:S(2)}) collective-permute-start(f32[144,128]{1,0:T(8,128)S(1)} %get-tuple-element.33), channel_id=1, source_target_pairs={{4,8},{12,16},{20,24},{8,4},{16,12},{24,20},{5,9},{13,17},{21,25},... | collective-permute-start | bytes 221192 | tf_op jit(solution)/shard_map/ppermute | solution.py:677

commit v8 on v7

--- a/solution.py
+++ b/solution.py
@@ -327,7 +327,7 @@
 
 
 def partial_kernel(
-    shift_ref, order_ref, flags_ref, inv_ref, sla_ref, spots_ref, info_ref,
+    shift_ref, order_ref, flags_ref, inv_ref, sla_ref, spots_ref,
     part_ref, done_ref, pair_ref, odd_ref,
 ):
     walkers, _, orbs, nel = inv_ref.shape
@@ -338,7 +338,7 @@
     share = walkers // members
     first = lax.axis_index("orb") * share
     tail = 2 * walkers * moves
-    part_ref[tail:, :] = info_ref[...]
+    part_ref[tail:, :] = jnp.zeros((part_ref.shape[0] - tail, part_ref.shape[1]), F32)
     jas = spots_ref[walkers, 1:2, :]
     for w in range(share):
         mine = spots_ref[first + w]
@@ -368,6 +368,12 @@
             for s in (0, 1):
                 pay[j * per + s * orbs : j * per + (s + 1) * orbs, :] = rows[s]
             pay[tail + 8 * j : tail + 8 * j + 8, :] = rows[2]
+
+
+def join_kernel(part_ref, info_ref, out_ref):
+    rows = part_ref.shape[0] - info_ref.shape[0]
+    out_ref[:rows, :] = part_ref[:rows, :]
+    out_ref[rows:, :] = part_ref[rows:, :] + info_ref[...]
 
 
 def add_kernel(mine_ref, other_ref, out_ref):
@@ -635,10 +641,14 @@
             shape(tall, LANES),
             shape(tall, LANES),
         ),
-        [VMEM] * 7,
+        [VMEM] * 6,
         us=2,
         name="partial",
-    )(shift, move_order, accepted, inverse, slater, spots, info)
+    )(shift, move_order, accepted, inverse, slater, spots)
+
+    part = call(
+        join_kernel, shape(count * moves + INFO, nel), [VMEM] * 2, us=0.2, name="join"
+    )(part, info)
 
     total = part
     got = jnp.zeros_like(part)

time: 29.4 us -> 29.1 us (0.990)
  waiting for transfers between devices: 7.47 us -> 6.17 us
  starting transfers between devices: 12.2 us -> 13.3 us
    ppermute x2, starting transfers between devices: 1.48 us -> 2.43 us  [body(): got = lax.ppermute(total, 'orb', partner)]
    ppermute x1, waiting for transfers between devices: 1.93 us -> 1.05 us  [body(): info = lax.ppermute(info, ('walkers', 'orb'), joint)]
  transfers between devices with their start and end apart: 7 -> 7, of which waited for: 4 -> 4; matrix products, arithmetic and copies ran while one was open for 0% -> 0% of each run, Pallas kernels for 14% -> 17%
where the time goes in v8:
time: 29.1 us; the launch traced here: 28.7 us
  starting transfers between devices  13.3 us (46%)
  Pallas kernels  8.31 us (29%)
  waiting for transfers between devices  6.17 us (21%)
  between operations  0.87 us (3%)
    ppermute x1, starting transfers between devices, body(): odd_i = lax.ppermute(odd_i, 'walkers', odds)  3.55 us
    ppermute x1, waiting for transfers between devices, body(): odd_i = lax.ppermute(odd_i, 'walkers', odds)  3.54 us
    pallas_call x1, Pallas kernels, body(): call(energy_kernel, made, [ANY] * len(operands), out_specs=(ANY, ANY), sc...  2.57 us
    ppermute x2, starting transfers between devices, body(): got = lax.ppermute(total, 'orb', partner)  2.43 us
    ppermute x1, starting transfers between devices, body(): odd_s = lax.ppermute(odd_s, 'walkers', odds)  2.29 us
    pallas_call x1, Pallas kernels, body(): call(update_kernel, (shape(walkers, 2, orbs, nel), shape(8, nel), shape(I...  2.2 us
    ppermute x1, starting transfers between devices, body(): info = lax.ppermute(info, ('walkers', 'orb'), joint)  1.92 us
    pallas_call x1, Pallas kernels, body(): call(shift_kernel, shape(2, walkers * moves, orbs), [VMEM] * 7, scratch=[...  1.74 us
  transfers between devices with their start and end apart: 7, of which 4 were waited for; matrix products, arithmetic and copies ran while one was open for 0% of the time, Pallas kernels for 17%

profile of v8, /device:TPU:8, one launch (start us, length us, event | category | flops | bytes accessed | tf_op | source)
XLA Modules:
  0.0 28.7 jit_solution(4811206582907704395)
XLA Ops:
  0.6 0.0 copy-start
  0.6 0.0 copy-start.3
  0.7 2.6 %energy.1 = (f32[5,16,128]{2,1,0:T(8,128)}, f32[8,128]{1,0:T(8,128)}) custom-call(f32[3,4,256]{2,1,0:T(4,128)} %bitcast.10, f32[3,4,256]{2,1,0:T(4,128)} %bitcast.12, s32[4,2,128]{2,1,0:T(2,128)} %order_ref.5, s32[4,2,32]{2,1,0:T(2,128)} %flags_ref.5, s32[1,4]{1,0:T(1,128)} %bitcast.15, f32[1,4]{1,0:T(1,128)} %bitcast.16, f32[1,4]{1,0:T(1,128)} %bitcast.17), custom_call_target="tpu_custom_call" | custom-call | flops 2200000000 | bytes 262144 | tf_op jit(solution)/shard_map/energy/pallas_call | solution.py:599
  3.3 1.9 %collective-permute-start = (f32[8,128]{1,0:T(8,128)}, f32[8,128]{1,0:T(8,128)S(1)}, u32[]{:S(2)}, u32[]{:S(2)}) collective-permute-start(f32[8,128]{1,0:T(8,128)} %get-tuple-element.25), channel_id=1, source_target_pairs={{0,8},{4,12},{8,0},{12,4},{16,24},{20,28},{24,16},{28,20},{1,25},{... | collective-permute-start | bytes 12296 | tf_op jit(solution)/shard_map/ppermute | solution.py:623
  5.3 0.0 copy-start.1
  5.3 0.0 copy-start.2
  5.3 0.0 copy-start.9
  5.3 1.7 %shift.1.shift_ref = f32[2,128,32]{2,1,0:T(8,128)S(1)} custom-call(f32[3,4,256]{2,1,0:T(4,128)S(1)} %bitcast.11, f32[3,4,256]{2,1,0:T(4,128)S(1)} %bitcast.13, s32[4,2,128]{2,1,0:T(2,128)S(1)} %copy-done.7, s32[4,2,32]{2,1,0:T(2,128)S(1)} %copy-done.8, f32[3,1024]{1,0:T(4,128)S(1)} %copy-done.3, f32[1,1024]{1,0:T(1,128)S(1)} %bitcast.14, ...), custom_call_target="tpu_custom_call" | custom-call | flops 3300000000 | bytes 262144 | tf_op jit(solution)/shard_map/shift/pallas_call | solution.py:625
  7.1 0.8 %partial.1 = (f32[264,128]{1,0:T(8,128)S(1)}, f32[4,2,32,128]{3,2,1,0:T(8,128)S(1)}, f32[144,128]{1,0:T(8,128)S(1)}, f32[144,128]{1,0:T(8,128)S(1)}) custom-call(f32[2,128,32]{2,1,0:T(8,128)S(1)} %shift.1.shift_ref, s32[4,2,128]{2,1,0:T(2,128)S(1)} %copy-done.7, s32[4,2,32]{2,1,0:T(2,128)S(1)} %copy-done.8, f32[4,2,32,128]{3,2,1,0:T(8,128)S(1)} %copy-done.2, ...), custom_call_target="tpu_custom_call" | custom-call | flops 2200000000 | bytes 262144 | tf_op jit(solution)/shard_map/partial/pallas_call | solution.py:636
  7.9 1.1 %collective-permute-done.info_ref = f32[8,128]{1,0:T(8,128)S(1)} collective-permute-done((f32[8,128]{1,0:T(8,128)}, f32[8,128]{1,0:T(8,128)S(1)}, u32[]{:S(2)}, u32[]{:S(2)}) %collective-permute-start) | collective-permute-done | bytes 4128 | tf_op jit(solution)/shard_map/ppermute | solution.py:623
  9.0 0.1 collective-permute-start.1
  9.2 1.3 %collective-permute-done.1.other_ref = f32[264,128]{1,0:T(8,128)S(1)} collective-permute-done((f32[264,128]{1,0:T(8,128)S(1)}, f32[264,128]{1,0:T(8,128)S(1)}, u32[]{:S(2)}, u32[]{:S(2)}) %collective-permute-start.1) | collective-permute-done | bytes 135200 | tf_op jit(solution)/shard_map/ppermute | solution.py:658
  10.5 2.3 %collective-permute-start.2 = (f32[264,128]{1,0:T(8,128)S(1)}, f32[264,128]{1,0:T(8,128)S(1)}, u32[]{:S(2)}, u32[]{:S(2)}) collective-permute-start(f32[264,128]{1,0:T(8,128)S(1)} %add.1.sum_ref), channel_id=1, source_target_pairs={{0,2},{1,3},{2,0},{3,1},{4,6},{5,7},{6,4},{7,5},{8,10},{9,11},{10,... | collective-permute-start | bytes 405512 | tf_op jit(solution)/shard_map/ppermute | solution.py:658
  12.7 1.5 %collective-permute-start.3 = (f32[144,128]{1,0:T(8,128)S(1)}, f32[144,128]{1,0:T(8,128)S(1)}, u32[]{:S(2)}, u32[]{:S(2)}) collective-permute-start(f32[144,128]{1,0:T(8,128)S(1)} %get-tuple-element.30), channel_id=1, source_target_pairs={{0,4},{4,0},{8,12},{12,8},{16,20},{20,16},{24,28},{28,24},{1,5},{5... | collective-permute-start | bytes 221192 | tf_op jit(solution)/shard_map/ppermute | solution.py:669
  14.3 2.3 %collective-permute-start.4 = (f32[144,128]{1,0:T(8,128)S(1)}, f32[144,128]{1,0:T(8,128)S(1)}, u32[]{:S(2)}, u32[]{:S(2)}) collective-permute-start(f32[144,128]{1,0:T(8,128)S(1)} %get-tuple-element.31), channel_id=1, source_target_pairs={{4,8},{12,16},{20,24},{8,4},{16,12},{24,20},{5,9},{13,17},{21,25},... | collective-permute-start | bytes 221192 | tf_op jit(solution)/shard_map/ppermute | solution.py:670
  16.6 0.3 collective-permute-done.2.got_ref
  16.8 2.2 %update.1 = (f32[4,2,32,128]{3,2,1,0:T(8,128)S(1)}, f32[8,128]{1,0:T(8,128)S(1)}, f32[8,128]{1,0:T(8,128)S(1)}, f32[144,128]{1,0:T(8,128)S(1)}, f32[144,128]{1,0:T(8,128)S(1)}) custom-call(f32[264,128]{1,0:T(8,128)S(1)} %add.1.sum_ref, f32[264,128]{1,0:T(8,128)S(1)} %collective-permute-done.2.got_ref, f32[4,2,32,128]{3,2,1,0:T(8,128)S(1)} %copy-done.2, ...), custom_call_target="tpu_custom_call" | custom-call | flops 4400000000 | bytes 262144 | tf_op jit(solution)/shard_map/update/pallas_call | solution.py:672
  19.0 1.6 %collective-permute-start.5 = (f32[144,128]{1,0:T(8,128)S(1)}, f32[144,128]{1,0:T(8,128)S(1)}, u32[]{:S(2)}, u32[]{:S(2)}) collective-permute-start(f32[144,128]{1,0:T(8,128)S(1)} %get-tuple-element.32), channel_id=1, source_target_pairs={{0,4},{4,0},{8,12},{12,8},{16,20},{20,16},{24,28},{28,24},{1,5},{5... | collective-permute-start | bytes 221192 | tf_op jit(solution)/shard_map/ppermute | solution.py:686
  20.6 3.6 %collective-permute-start.6 = (f32[144,128]{1,0:T(8,128)S(1)}, f32[144,128]{1,0:T(8,128)S(1)}, u32[]{:S(2)}, u32[]{:S(2)}) collective-permute-start(f32[144,128]{1,0:T(8,128)S(1)} %get-tuple-element.33), channel_id=1, source_target_pairs={{4,8},{12,16},{20,24},{8,4},{16,12},{24,20},{5,9},{13,17},{21,25},... | collective-permute-start | bytes 221192 | tf_op jit(solution)/shard_map/ppermute | solution.py:687
  24.2 0.0 collective-permute-done.3.pair_s_ref
  24.2 0.0 collective-permute-done.4.odd_s_ref
  24.2 0.0 collective-permute-done.5.pair_i_ref
  24.2 3.5 %collective-permute-done.6.odd_i_ref = f32[144,128]{1,0:T(8,128)S(1)} collective-permute-done((f32[144,128]{1,0:T(8,128)S(1)}, f32[144,128]{1,0:T(8,128)S(1)}, u32[]{:S(2)}, u32[]{:S(2)}) %collective-permute-start.6) | collective-permute-done | bytes 73760 | tf_op jit(solution)/shard_map/ppermute | solution.py:687
  27.8 0.9 %place.1 = (f32[4,2,32,128]{3,2,1,0:T(8,128)}, f32[4,2,32,128]{3,2,1,0:T(8,128)}, f32[3,4,256]{2,1,0:T(4,128)}, f32[1,4]{1,0:T(1,128)}, f32[1,4]{1,0:T(1,128)}, /*index=5*/f32[1,1]{1,0:T(1,128)}) custom-call(f32[4,2,32,128]{3,2,1,0:T(8,128)S(1)} %get-tuple-element.26.cur_ref, f32[4,2,32,128]{3,2,1,0:T(8,128)S(1)} %get-tuple-element.27.done_ref, ...), custom_call_target="tpu_custom_call" | custom-call | flops 1650000000 | bytes 262144 | tf_op jit(solution)/shard_map/place/pallas_call | solution.py:689
  (17 shorter events, 0.1 us)
Async XLA Ops:
  0.6 4.6 %copy-start = (f32[2,32,1024]{2,1,0:T(8,128)S(1)}, f32[2,32,1024]{2,1,0:T(8,128)}, u32[]{:S(2)}) copy-start(f32[2,32,1024]{2,1,0:T(8,128)} %orb_ref.1) | copy-start | bytes 786436
  0.6 4.6 %copy-start.3 = (f32[3,1024]{1,0:T(4,128)S(1)}, f32[3,1024]{1,0:T(4,128)}, u32[]{:S(2)}) copy-start(f32[3,1024]{1,0:T(4,128)} %cen_ref.1) | copy-start | bytes 36868
  0.7 4.6 %copy-start.4 = (f32[4,3,256]{2,0,1:T(4,128)S(1)}, f32[4,3,256]{2,0,1:T(4,128)}, u32[]{:S(2)}) copy-start(f32[4,3,256]{2,0,1:T(4,128)} %param.14) | copy-start | bytes 36868
  0.7 4.6 %copy-start.5 = (f32[4,3,256]{2,0,1:T(4,128)S(1)}, f32[4,3,256]{2,0,1:T(4,128)}, u32[]{:S(2)}) copy-start(f32[4,3,256]{2,0,1:T(4,128)} %param.15) | copy-start | bytes 36868
  0.7 4.6 %copy-start.6 = (f32[1024]{0:T(1024)S(1)}, f32[1024]{0:T(1024)}, u32[]{:S(2)}) copy-start(f32[1024]{0:T(1024)} %param.21) | copy-start | bytes 12292
  0.7 4.6 %copy-start.7 = (s32[4,2,128]{2,1,0:T(2,128)S(1)}, s32[4,2,128]{2,1,0:T(2,128)}, u32[]{:S(2)}) copy-start(s32[4,2,128]{2,1,0:T(2,128)} %order_ref.5) | copy-start | bytes 12292
  0.7 4.6 %copy-start.8 = (s32[4,2,32]{2,1,0:T(2,128)S(1)}, s32[4,2,32]{2,1,0:T(2,128)}, u32[]{:S(2)}) copy-start(s32[4,2,32]{2,1,0:T(2,128)} %flags_ref.5) | copy-start | bytes 3076
  3.3 5.7 %collective-permute-start = (f32[8,128]{1,0:T(8,128)}, f32[8,128]{1,0:T(8,128)S(1)}, u32[]{:S(2)}, u32[]{:S(2)}) collective-permute-start(f32[8,128]{1,0:T(8,128)} %get-tuple-element.25), channel_id=1, source_target_pairs={{0,8},{4,12},{8,0},{12,4},{16,24},{20,28},{24,16},{28,20},{1,25},{... | collective-permute-start | bytes 12296 | tf_op jit(solution)/shard_map/ppermute | solution.py:623
  5.3 1.8 %copy-start.1 = (f32[4,2,32,128]{3,2,1,0:T(8,128)S(1)}, f32[4,2,32,128]{3,2,1,0:T(8,128)}, u32[]{:S(2)}) copy-start(f32[4,2,32,128]{3,2,1,0:T(8,128)} %sla_ref.1) | copy-start | bytes 393220
  5.3 1.8 %copy-start.2 = (f32[4,2,32,128]{3,2,1,0:T(8,128)S(1)}, f32[4,2,32,128]{3,2,1,0:T(8,128)}, u32[]{:S(2)}) copy-start(f32[4,2,32,128]{3,2,1,0:T(8,128)} %inv_ref.3) | copy-start | bytes 393220
  5.3 1.8 %copy-start.9 = (f32[5,16,128]{2,1,0:T(8,128)S(1)}, f32[5,16,128]{2,1,0:T(8,128)}, u32[]{:S(2)}) copy-start(f32[5,16,128]{2,1,0:T(8,128)} %get-tuple-element.23.spots_ref) | copy-start | bytes 122884
  9.0 1.4 %collective-permute-start.1 = (f32[264,128]{1,0:T(8,128)S(1)}, f32[264,128]{1,0:T(8,128)S(1)}, u32[]{:S(2)}, u32[]{:S(2)}) collective-permute-start(f32[264,128]{1,0:T(8,128)S(1)} %join.1.mine_ref), channel_id=1, source_target_pairs={{0,1},{1,0},{2,3},{3,2},{4,5},{5,4},{6,7},{7,6},{8,9},{9,8},{10,11... | collective-permute-start | bytes 405512 | tf_op jit(solution)/shard_map/ppermute | solution.py:658
  10.5 6.4 %collective-permute-start.2 = (f32[264,128]{1,0:T(8,128)S(1)}, f32[264,128]{1,0:T(8,128)S(1)}, u32[]{:S(2)}, u32[]{:S(2)}) collective-permute-start(f32[264,128]{1,0:T(8,128)S(1)} %add.1.sum_ref), channel_id=1, source_target_pairs={{0,2},{1,3},{2,0},{3,1},{4,6},{5,7},{6,4},{7,5},{8,10},{9,11},{10,... | collective-permute-start | bytes 405512 | tf_op jit(solution)/shard_map/ppermute | solution.py:658
  12.7 11.4 %collective-permute-start.3 = (f32[144,128]{1,0:T(8,128)S(1)}, f32[144,128]{1,0:T(8,128)S(1)}, u32[]{:S(2)}, u32[]{:S(2)}) collective-permute-start(f32[144,128]{1,0:T(8,128)S(1)} %get-tuple-element.30), channel_id=1, source_target_pairs={{0,4},{4,0},{8,12},{12,8},{16,20},{20,16},{24,28},{28,24},{1,5},{5... | collective-permute-start | bytes 221192 | tf_op jit(solution)/shard_map/ppermute | solution.py:669
  14.3 9.9 %collective-permute-start.4 = (f32[144,128]{1,0:T(8,128)S(1)}, f32[144,128]{1,0:T(8,128)S(1)}, u32[]{:S(2)}, u32[]{:S(2)}) collective-permute-start(f32[144,128]{1,0:T(8,128)S(1)} %get-tuple-element.31), channel_id=1, source_target_pairs={{4,8},{12,16},{20,24},{8,4},{16,12},{24,20},{5,9},{13,17},{21,25},... | collective-permute-start | bytes 221192 | tf_op jit(solution)/shard_map/ppermute | solution.py:670
  19.0 5.2 %collective-permute-start.5 = (f32[144,128]{1,0:T(8,128)S(1)}, f32[144,128]{1,0:T(8,128)S(1)}, u32[]{:S(2)}, u32[]{:S(2)}) collective-permute-start(f32[144,128]{1,0:T(8,128)S(1)} %get-tuple-element.32), channel_id=1, source_target_pairs={{0,4},{4,0},{8,12},{12,8},{16,20},{20,16},{24,28},{28,24},{1,5},{5... | collective-permute-start | bytes 221192 | tf_op jit(solution)/shard_map/ppermute | solution.py:686
  20.6 7.1 %collective-permute-start.6 = (f32[144,128]{1,0:T(8,128)S(1)}, f32[144,128]{1,0:T(8,128)S(1)}, u32[]{:S(2)}, u32[]{:S(2)}) collective-permute-start(f32[144,128]{1,0:T(8,128)S(1)} %get-tuple-element.33), channel_id=1, source_target_pairs={{4,8},{12,16},{20,24},{8,4},{16,12},{24,20},{5,9},{13,17},{21,25},... | collective-permute-start | bytes 221192 | tf_op jit(solution)/shard_map/ppermute | solution.py:687

commit v9 on v8

--- a/solution.py
+++ b/solution.py
@@ -368,6 +368,19 @@
             for s in (0, 1):
                 pay[j * per + s * orbs : j * per + (s + 1) * orbs, :] = rows[s]
             pay[tail + 8 * j : tail + 8 * j + 8, :] = rows[2]
+
+
+def moved_kernel(
+    pos_ref, dis_ref, order_ref, flags_ref, cen_ref, exp_ref, orb_ref, inv_ref, sla_ref, spots_ref,
+    part_ref, done_ref, pair_ref, odd_ref, differ_ref, shift_ref,
+):
+    shift_kernel(
+        pos_ref, dis_ref, order_ref, flags_ref, cen_ref, exp_ref, orb_ref, shift_ref, differ_ref
+    )
+    partial_kernel(
+        shift_ref, order_ref, flags_ref, inv_ref, sla_ref, spots_ref,
+        part_ref, done_ref, pair_ref, odd_ref,
+    )
 
 
 def join_kernel(part_ref, info_ref, out_ref):
@@ -622,29 +635,25 @@
     ]
     info = lax.ppermute(info, ("walkers", "orb"), joint)
 
-    shift = call(
-        shift_kernel,
-        shape(2, walkers * moves, orbs),
-        [VMEM] * 7,
-        scratch=[pltpu.VMEM((2, walkers * moves, basis), F32)],
-        us=3,
-        name="shift",
-    )(
-        places, steps, move_order, accepted, centers, exponents.reshape(1, basis), orbitals,
-    )
-
     part, done, pair_s, odd_s = call(
-        partial_kernel,
+        moved_kernel,
         (
             shape(count * moves + INFO, nel),
             shape(walkers, 2, orbs, nel),
             shape(tall, LANES),
             shape(tall, LANES),
         ),
-        [VMEM] * 6,
-        us=2,
-        name="partial",
-    )(shift, move_order, accepted, inverse, slater, spots)
+        [VMEM] * 10,
+        scratch=[
+            pltpu.VMEM((2, walkers * moves, basis), F32),
+            pltpu.VMEM((2, walkers * moves, orbs), F32),
+        ],
+        us=4,
+        name="moved",
+    )(
+        places, steps, move_order, accepted, centers, exponents.reshape(1, basis), orbitals,
+        inverse, slater, spots,
+    )
 
     part = call(
         join_kernel, shape(count * moves + INFO, nel), [VMEM] * 2, us=0.2, name="join"

time: 29.1 us -> 29.7 us (1.021)
  waiting for transfers between devices: 6.17 us -> 5.34 us
  starting transfers between devices: 13.3 us -> 14.1 us
  local copies, waits for them, and re-layouts: 0.05 us -> 0.82 us
    ppermute x2, starting transfers between devices: 2.43 us -> 3.25 us  [body(): got = lax.ppermute(total, 'orb', partner)]
    unnamed x20 -> x22, local copies, waits for them, and re-layouts: 0.05 us -> 0.82 us
    ppermute x1, waiting for transfers between devices: 1.05 us -> 0.51 us  [body(): info = lax.ppermute(info, ('walkers', 'orb'), joint)]
    pallas_call x2 -> x1, Pallas kernels: 2.59 us -> 2.4 us  [body(): call(moved_kernel, (shape(count * moves + INFO, nel), shape(walkers, 2, o...]
  transfers between devices with their start and end apart: 7 -> 7, of which waited for: 4 -> 4; matrix products, arithmetic and copies ran while one was open for 0% -> 0% of each run, Pallas kernels for 17% -> 16%
where the time goes in v9:
time: 29.7 us; the launch traced here: 29.2 us
  starting transfers between devices  14.1 us (47%)
  Pallas kernels  8.08 us (27%)
  waiting for transfers between devices  5.34 us (18%)
  between operations  0.86 us (3%)
  local copies, waits for them, and re-layouts  0.82 us (3%)
    ppermute x1, starting transfers between devices, body(): odd_i = lax.ppermute(odd_i, 'walkers', odds)  3.55 us
    ppermute x1, waiting for transfers between devices, body(): odd_i = lax.ppermute(odd_i, 'walkers', odds)  3.55 us
    ppermute x2, starting transfers between devices, body(): got = lax.ppermute(total, 'orb', partner)  3.25 us
    pallas_call x1, Pallas kernels, body(): call(energy_kernel, made, [ANY] * len(operands), out_specs=(ANY, ANY), sc...  2.53 us
    pallas_call x1, Pallas kernels, body(): call(moved_kernel, (shape(count * moves + INFO, nel), shape(walkers, 2, o...  2.4 us
    ppermute x1, starting transfers between devices, body(): odd_s = lax.ppermute(odd_s, 'walkers', odds)  2.29 us
    pallas_call x1, Pallas kernels, body(): call(update_kernel, (shape(walkers, 2, orbs, nel), shape(8, nel), shape(I...  2.2 us
    ppermute x1, starting transfers between devices, body(): info = lax.ppermute(info, ('walkers', 'orb'), joint)  1.92 us
  transfers between devices with their start and end apart: 7, of which 4 were waited for; matrix products, arithmetic and copies ran while one was open for 0% of the time, Pallas kernels for 16%

profile of v9, /device:TPU:8, one launch (start us, length us, event | category | flops | bytes accessed | tf_op | source)
XLA Modules:
  0.0 29.2 jit_solution(12008086069446223318)
XLA Ops:
  0.6 0.0 copy-start
  0.6 0.0 copy-start.1
  0.7 2.5 %energy.1 = (f32[5,16,128]{2,1,0:T(8,128)}, f32[8,128]{1,0:T(8,128)}) custom-call(f32[3,4,256]{2,1,0:T(4,128)} %bitcast.10, f32[3,4,256]{2,1,0:T(4,128)} %bitcast.12, s32[4,2,128]{2,1,0:T(2,128)} %order_ref.3, s32[4,2,32]{2,1,0:T(2,128)} %flags_ref.3, s32[1,4]{1,0:T(1,128)} %bitcast.15, f32[1,4]{1,0:T(1,128)} %bitcast.16, f32[1,4]{1,0:T(1,128)} %bitcast.17), custom_call_target="tpu_custom_call" | custom-call | flops 2200000000 | bytes 262144 | tf_op jit(solution)/shard_map/energy/pallas_call | solution.py:612
  3.3 0.0 copy-start.6
  3.3 1.9 %collective-permute-start = (f32[8,128]{1,0:T(8,128)}, f32[8,128]{1,0:T(8,128)S(1)}, u32[]{:S(2)}, u32[]{:S(2)}) collective-permute-start(f32[8,128]{1,0:T(8,128)} %get-tuple-element.25), channel_id=1, source_target_pairs={{0,8},{4,12},{8,0},{12,4},{16,24},{20,28},{24,16},{28,20},{1,25},{... | collective-permute-start | bytes 12296 | tf_op jit(solution)/shard_map/ppermute | solution.py:636
  5.3 0.0 copy-start.9
  5.3 0.8 %copy-done.9 = f32[5,16,128]{2,1,0:T(8,128)S(1)} copy-done((f32[5,16,128]{2,1,0:T(8,128)S(1)}, f32[5,16,128]{2,1,0:T(8,128)}, u32[]{:S(2)}) %copy-start.9) | copy-done | bytes 40984
  6.1 2.4 %moved.1 = (f32[264,128]{1,0:T(8,128)S(1)}, f32[4,2,32,128]{3,2,1,0:T(8,128)S(1)}, f32[144,128]{1,0:T(8,128)S(1)}, f32[144,128]{1,0:T(8,128)S(1)}) custom-call(f32[3,4,256]{2,1,0:T(4,128)S(1)} %bitcast.11, f32[3,4,256]{2,1,0:T(4,128)S(1)} %bitcast.13, s32[4,2,128]{2,1,0:T(2,128)S(1)} %copy-done.7, s32[4,2,32]{2,1,0:T(2,128)S(1)} %copy-done.8, ...), custom_call_target="tpu_custom_call" | custom-call | flops 4400000000 | bytes 262144 | tf_op jit(solution)/shard_map/moved/pallas_call | solution.py:638
  8.5 0.5 %collective-permute-done.info_ref = f32[8,128]{1,0:T(8,128)S(1)} collective-permute-done((f32[8,128]{1,0:T(8,128)}, f32[8,128]{1,0:T(8,128)S(1)}, u32[]{:S(2)}, u32[]{:S(2)}) %collective-permute-start) | collective-permute-done | bytes 4128 | tf_op jit(solution)/shard_map/ppermute | solution.py:636
  9.0 0.0 copy-start.10
  9.0 0.7 %collective-permute-start.1 = (f32[264,128]{1,0:T(8,128)S(1)}, f32[264,128]{1,0:T(8,128)S(1)}, u32[]{:S(2)}, u32[]{:S(2)}) collective-permute-start(f32[264,128]{1,0:T(8,128)S(1)} %join.1.mine_ref), channel_id=1, source_target_pairs={{0,1},{1,0},{2,3},{3,2},{4,5},{5,4},{6,7},{7,6},{8,9},{9,8},{10,11... | collective-permute-start | bytes 405512 | tf_op jit(solution)/shard_map/ppermute | solution.py:667
  9.7 1.0 %collective-permute-done.1.other_ref = f32[264,128]{1,0:T(8,128)S(1)} collective-permute-done((f32[264,128]{1,0:T(8,128)S(1)}, f32[264,128]{1,0:T(8,128)S(1)}, u32[]{:S(2)}, u32[]{:S(2)}) %collective-permute-start.1) | collective-permute-done | bytes 135200 | tf_op jit(solution)/shard_map/ppermute | solution.py:667
  10.7 2.6 %collective-permute-start.2 = (f32[264,128]{1,0:T(8,128)S(1)}, f32[264,128]{1,0:T(8,128)S(1)}, u32[]{:S(2)}, u32[]{:S(2)}) collective-permute-start(f32[264,128]{1,0:T(8,128)S(1)} %add.1.sum_ref), channel_id=1, source_target_pairs={{0,2},{1,3},{2,0},{3,1},{4,6},{5,7},{6,4},{7,5},{8,10},{9,11},{10,... | collective-permute-start | bytes 405512 | tf_op jit(solution)/shard_map/ppermute | solution.py:667
  13.3 1.5 %collective-permute-start.3 = (f32[144,128]{1,0:T(8,128)S(1)}, f32[144,128]{1,0:T(8,128)S(1)}, u32[]{:S(2)}, u32[]{:S(2)}) collective-permute-start(f32[144,128]{1,0:T(8,128)S(1)} %get-tuple-element.30), channel_id=1, source_target_pairs={{0,4},{4,0},{8,12},{12,8},{16,20},{20,16},{24,28},{28,24},{1,5},{5... | collective-permute-start | bytes 221192 | tf_op jit(solution)/shard_map/ppermute | solution.py:678
  14.8 2.3 %collective-permute-start.4 = (f32[144,128]{1,0:T(8,128)S(1)}, f32[144,128]{1,0:T(8,128)S(1)}, u32[]{:S(2)}, u32[]{:S(2)}) collective-permute-start(f32[144,128]{1,0:T(8,128)S(1)} %get-tuple-element.31), channel_id=1, source_target_pairs={{4,8},{12,16},{20,24},{8,4},{16,12},{24,20},{5,9},{13,17},{21,25},... | collective-permute-start | bytes 221192 | tf_op jit(solution)/shard_map/ppermute | solution.py:679
  17.1 0.3 collective-permute-done.2.got_ref
  17.4 2.2 %update.1 = (f32[4,2,32,128]{3,2,1,0:T(8,128)S(1)}, f32[8,128]{1,0:T(8,128)S(1)}, f32[8,128]{1,0:T(8,128)S(1)}, f32[144,128]{1,0:T(8,128)S(1)}, f32[144,128]{1,0:T(8,128)S(1)}) custom-call(f32[264,128]{1,0:T(8,128)S(1)} %add.1.sum_ref, f32[264,128]{1,0:T(8,128)S(1)} %collective-permute-done.2.got_ref, f32[4,2,32,128]{3,2,1,0:T(8,128)S(1)} %copy-done.2, ...), custom_call_target="tpu_custom_call" | custom-call | flops 4400000000 | bytes 262144 | tf_op jit(solution)/shard_map/update/pallas_call | solution.py:681
  19.6 1.6 %collective-permute-start.5 = (f32[144,128]{1,0:T(8,128)S(1)}, f32[144,128]{1,0:T(8,128)S(1)}, u32[]{:S(2)}, u32[]{:S(2)}) collective-permute-start(f32[144,128]{1,0:T(8,128)S(1)} %get-tuple-element.32), channel_id=1, source_target_pairs={{0,4},{4,0},{8,12},{12,8},{16,20},{20,16},{24,28},{28,24},{1,5},{5... | collective-permute-start | bytes 221192 | tf_op jit(solution)/shard_map/ppermute | solution.py:695
  21.2 3.5 %collective-permute-start.6 = (f32[144,128]{1,0:T(8,128)S(1)}, f32[144,128]{1,0:T(8,128)S(1)}, u32[]{:S(2)}, u32[]{:S(2)}) collective-permute-start(f32[144,128]{1,0:T(8,128)S(1)} %get-tuple-element.33), channel_id=1, source_target_pairs={{4,8},{12,16},{20,24},{8,4},{16,12},{24,20},{5,9},{13,17},{21,25},... | collective-permute-start | bytes 221192 | tf_op jit(solution)/shard_map/ppermute | solution.py:696
  24.7 0.0 collective-permute-done.3.pair_s_ref
  24.7 0.0 collective-permute-done.4.odd_s_ref
  24.7 0.0 collective-permute-done.5.pair_i_ref
  24.8 3.5 %collective-permute-done.6.odd_i_ref = f32[144,128]{1,0:T(8,128)S(1)} collective-permute-done((f32[144,128]{1,0:T(8,128)S(1)}, f32[144,128]{1,0:T(8,128)S(1)}, u32[]{:S(2)}, u32[]{:S(2)}) %collective-permute-start.6) | collective-permute-done | bytes 73760 | tf_op jit(solution)/shard_map/ppermute | solution.py:696
  28.3 0.9 %place.1 = (f32[4,2,32,128]{3,2,1,0:T(8,128)}, f32[4,2,32,128]{3,2,1,0:T(8,128)}, f32[3,4,256]{2,1,0:T(4,128)}, f32[1,4]{1,0:T(1,128)}, f32[1,4]{1,0:T(1,128)}, /*index=5*/f32[1,1]{1,0:T(1,128)}) custom-call(f32[4,2,32,128]{3,2,1,0:T(8,128)S(1)} %get-tuple-element.26.cur_ref, f32[4,2,32,128]{3,2,1,0:T(8,128)S(1)} %get-tuple-element.27.done_ref, ...), custom_call_target="tpu_custom_call" | custom-call | flops 1650000000 | bytes 262144 | tf_op jit(solution)/shard_map/place/pallas_call | solution.py:698
  (18 shorter events, 0.1 us)
Async XLA Ops:
  0.6 4.6 %copy-start = (f32[2,32,1024]{2,1,0:T(8,128)S(1)}, f32[2,32,1024]{2,1,0:T(8,128)}, u32[]{:S(2)}) copy-start(f32[2,32,1024]{2,1,0:T(8,128)} %orb_ref.1) | copy-start | bytes 786436
  0.6 4.6 %copy-start.1 = (f32[4,2,32,128]{3,2,1,0:T(8,128)S(1)}, f32[4,2,32,128]{3,2,1,0:T(8,128)}, u32[]{:S(2)}) copy-start(f32[4,2,32,128]{3,2,1,0:T(8,128)} %sla_ref.1) | copy-start | bytes 393220
  0.7 4.6 %copy-start.2 = (f32[4,2,32,128]{3,2,1,0:T(8,128)S(1)}, f32[4,2,32,128]{3,2,1,0:T(8,128)}, u32[]{:S(2)}) copy-start(f32[4,2,32,128]{3,2,1,0:T(8,128)} %inv_ref.3) | copy-start | bytes 393220
  0.7 4.6 %copy-start.3 = (f32[3,1024]{1,0:T(4,128)S(1)}, f32[3,1024]{1,0:T(4,128)}, u32[]{:S(2)}) copy-start(f32[3,1024]{1,0:T(4,128)} %cen_ref.1) | copy-start | bytes 36868
  0.7 4.6 %copy-start.4 = (f32[4,3,256]{2,0,1:T(4,128)S(1)}, f32[4,3,256]{2,0,1:T(4,128)}, u32[]{:S(2)}) copy-start(f32[4,3,256]{2,0,1:T(4,128)} %param.14) | copy-start | bytes 36868
  0.7 4.6 %copy-start.5 = (f32[4,3,256]{2,0,1:T(4,128)S(1)}, f32[4,3,256]{2,0,1:T(4,128)}, u32[]{:S(2)}) copy-start(f32[4,3,256]{2,0,1:T(4,128)} %param.15) | copy-start | bytes 36868
  0.7 4.6 %copy-start.7 = (s32[4,2,128]{2,1,0:T(2,128)S(1)}, s32[4,2,128]{2,1,0:T(2,128)}, u32[]{:S(2)}) copy-start(s32[4,2,128]{2,1,0:T(2,128)} %order_ref.3) | copy-start | bytes 12292
  0.7 4.6 %copy-start.8 = (s32[4,2,32]{2,1,0:T(2,128)S(1)}, s32[4,2,32]{2,1,0:T(2,128)}, u32[]{:S(2)}) copy-start(s32[4,2,32]{2,1,0:T(2,128)} %flags_ref.3) | copy-start | bytes 3076
  3.3 2.0 %copy-start.6 = (f32[1024]{0:T(1024)S(1)}, f32[1024]{0:T(1024)}, u32[]{:S(2)}) copy-start(f32[1024]{0:T(1024)} %param.21) | copy-start | bytes 12292
  3.3 5.7 %collective-permute-start = (f32[8,128]{1,0:T(8,128)}, f32[8,128]{1,0:T(8,128)S(1)}, u32[]{:S(2)}, u32[]{:S(2)}) collective-permute-start(f32[8,128]{1,0:T(8,128)} %get-tuple-element.25), channel_id=1, source_target_pairs={{0,8},{4,12},{8,0},{12,4},{16,24},{20,28},{24,16},{28,20},{1,25},{... | collective-permute-start | bytes 12296 | tf_op jit(solution)/shard_map/ppermute | solution.py:636
  5.3 0.8 %copy-start.9 = (f32[5,16,128]{2,1,0:T(8,128)S(1)}, f32[5,16,128]{2,1,0:T(8,128)}, u32[]{:S(2)}) copy-start(f32[5,16,128]{2,1,0:T(8,128)} %get-tuple-element.23.spots_ref) | copy-start | bytes 122884
  9.0 8.4 %copy-start.10 = (f32[5,16,128]{2,1,0:T(8,128)S(1)}, f32[5,16,128]{2,1,0:T(8,128)}, u32[]{:S(2)}) copy-start(f32[5,16,128]{2,1,0:T(8,128)} %get-tuple-element.23.spots_ref) | copy-start | bytes 122884
  9.0 1.7 %collective-permute-start.1 = (f32[264,128]{1,0:T(8,128)S(1)}, f32[264,128]{1,0:T(8,128)S(1)}, u32[]{:S(2)}, u32[]{:S(2)}) collective-permute-start(f32[264,128]{1,0:T(8,128)S(1)} %join.1.mine_ref), channel_id=1, source_target_pairs={{0,1},{1,0},{2,3},{3,2},{4,5},{5,4},{6,7},{7,6},{8,9},{9,8},{10,11... | collective-permute-start | bytes 405512 | tf_op jit(solution)/shard_map/ppermute | solution.py:667
  10.7 6.7 %collective-permute-start.2 = (f32[264,128]{1,0:T(8,128)S(1)}, f32[264,128]{1,0:T(8,128)S(1)}, u32[]{:S(2)}, u32[]{:S(2)}) collective-permute-start(f32[264,128]{1,0:T(8,128)S(1)} %add.1.sum_ref), channel_id=1, source_target_pairs={{0,2},{1,3},{2,0},{3,1},{4,6},{5,7},{6,4},{7,5},{8,10},{9,11},{10,... | collective-permute-start | bytes 405512 | tf_op jit(solution)/shard_map/ppermute | solution.py:667
  13.3 11.5 %collective-permute-start.3 = (f32[144,128]{1,0:T(8,128)S(1)}, f32[144,128]{1,0:T(8,128)S(1)}, u32[]{:S(2)}, u32[]{:S(2)}) collective-permute-start(f32[144,128]{1,0:T(8,128)S(1)} %get-tuple-element.30), channel_id=1, source_target_pairs={{0,4},{4,0},{8,12},{12,8},{16,20},{20,16},{24,28},{28,24},{1,5},{5... | collective-permute-start | bytes 221192 | tf_op jit(solution)/shard_map/ppermute | solution.py:678
  14.8 9.9 %collective-permute-start.4 = (f32[144,128]{1,0:T(8,128)S(1)}, f32[144,128]{1,0:T(8,128)S(1)}, u32[]{:S(2)}, u32[]{:S(2)}) collective-permute-start(f32[144,128]{1,0:T(8,128)S(1)} %get-tuple-element.31), channel_id=1, source_target_pairs={{4,8},{12,16},{20,24},{8,4},{16,12},{24,20},{5,9},{13,17},{21,25},... | collective-permute-start | bytes 221192 | tf_op jit(solution)/shard_map/ppermute | solution.py:679
  19.6 5.2 %collective-permute-start.5 = (f32[144,128]{1,0:T(8,128)S(1)}, f32[144,128]{1,0:T(8,128)S(1)}, u32[]{:S(2)}, u32[]{:S(2)}) collective-permute-start(f32[144,128]{1,0:T(8,128)S(1)} %get-tuple-element.32), channel_id=1, source_target_pairs={{0,4},{4,0},{8,12},{12,8},{16,20},{20,16},{24,28},{28,24},{1,5},{5... | collective-permute-start | bytes 221192 | tf_op jit(solution)/shard_map/ppermute | solution.py:695
  21.2 7.1 %collective-permute-start.6 = (f32[144,128]{1,0:T(8,128)S(1)}, f32[144,128]{1,0:T(8,128)S(1)}, u32[]{:S(2)}, u32[]{:S(2)}) collective-permute-start(f32[144,128]{1,0:T(8,128)S(1)} %get-tuple-element.33), channel_id=1, source_target_pairs={{4,8},{12,16},{20,24},{8,4},{16,12},{24,20},{5,9},{13,17},{21,25},... | collective-permute-start | bytes 221192 | tf_op jit(solution)/shard_map/ppermute | solution.py:696

commit v10 on v8

--- a/solution.py
+++ b/solution.py
@@ -7,17 +7,10 @@
 
 F32 = jnp.float32
 BF16 = jnp.bfloat16
-highest = lax.Precision.HIGHEST
 VMEM = pl.BlockSpec(memory_space=pltpu.VMEM)
 ANY = pl.BlockSpec(memory_space=pl.ANY)
 LANES = 128
 INFO = 8
-
-
-def nt(a, b):
-    return lax.dot_general(
-        a, b, (((1,), (1,)), ((), ())), precision=highest, preferred_element_type=F32
-    )
 
 
 def thirds(x):
@@ -293,9 +286,9 @@
     cols, _ = moves_of(order_ref, flags_ref)
     hots = one_hots(cols, nel)
     rows = [ref[c] for ref in (pos_ref, dis_ref) for c in range(3)]
-    rows = jnp.concatenate(rows + [jnp.zeros((-6 * walkers % 8, both), F32)] * (6 * walkers % 8 > 0), axis=0)
+    rows = jnp.concatenate(rows + [jnp.zeros((-6 * walkers % 16, both), F32)] * (6 * walkers % 16 > 0), axis=0)
     for s in (0, 1):
-        points = nt(
+        points = taken_nt(
             jnp.concatenate([hots[2 * w + s] for w in range(walkers)], axis=0),
             rows[:, s * nel : (s + 1) * nel],
         )
@@ -431,7 +424,8 @@
                     )
                 )
             for t in range(tiles):
-                for side, width, (upper, lower) in ((left, moves, new[0]), (right, nel, new[1])):
+                sides = ((right, nel, new[1]), (left, moves, new[0]))
+                for side, width, (upper, lower) in sides[: 1 + (k + 2 < moves)]:
                     tile = (
                         side[i][t] - wide[0][t][:, :width] * upper - wide[1][t][:, :width] * lower
                     )

time: 29.1 us -> 29.1 us (level)
  no operation moved by 1% of the time
where the time goes in v10:
time: 29.1 us; the launch traced here: 28.7 us
  starting transfers between devices  13.3 us (46%)
  Pallas kernels  8.31 us (29%)
  waiting for transfers between devices  6.17 us (21%)
  between operations  0.87 us (3%)
    ppermute x1, starting transfers between devices, body(): odd_i = lax.ppermute(odd_i, 'walkers', odds)  3.55 us
    ppermute x1, waiting for transfers between devices, body(): odd_i = lax.ppermute(odd_i, 'walkers', odds)  3.54 us
    pallas_call x1, Pallas kernels, body(): call(energy_kernel, made, [ANY] * len(operands), out_specs=(ANY, ANY), sc...  2.57 us
    ppermute x2, starting transfers between devices, body(): got = lax.ppermute(total, 'orb', partner)  2.42 us
    ppermute x1, starting transfers between devices, body(): odd_s = lax.ppermute(odd_s, 'walkers', odds)  2.29 us
    pallas_call x1, Pallas kernels, body(): call(update_kernel, (shape(walkers, 2, orbs, nel), shape(8, nel), shape(I...  2.2 us
    ppermute x1, starting transfers between devices, body(): info = lax.ppermute(info, ('walkers', 'orb'), joint)  1.92 us
    pallas_call x1, Pallas kernels, body(): call(shift_kernel, shape(2, walkers * moves, orbs), [VMEM] * 7, scratch=[...  1.74 us
  transfers between devices with their start and end apart: 7, of which 4 were waited for; matrix products, arithmetic and copies ran while one was open for 0% of the time, Pallas kernels for 17%

profile of v10, /device:TPU:8, one launch (start us, length us, event | category | flops | bytes accessed | tf_op | source)
XLA Modules:
  0.0 28.7 jit_solution(8860760362509754790)
XLA Ops:
  0.6 0.0 copy-start
  0.6 0.0 copy-start.3
  0.7 2.6 %energy.1 = (f32[5,16,128]{2,1,0:T(8,128)}, f32[8,128]{1,0:T(8,128)}) custom-call(f32[3,4,256]{2,1,0:T(4,128)} %bitcast.10, f32[3,4,256]{2,1,0:T(4,128)} %bitcast.12, s32[4,2,128]{2,1,0:T(2,128)} %order_ref.5, s32[4,2,32]{2,1,0:T(2,128)} %flags_ref.5, s32[1,4]{1,0:T(1,128)} %bitcast.15, f32[1,4]{1,0:T(1,128)} %bitcast.16, f32[1,4]{1,0:T(1,128)} %bitcast.17), custom_call_target="tpu_custom_call" | custom-call | flops 2200000000 | bytes 262144 | tf_op jit(solution)/shard_map/energy/pallas_call | solution.py:593
  3.3 1.9 %collective-permute-start = (f32[8,128]{1,0:T(8,128)}, f32[8,128]{1,0:T(8,128)S(1)}, u32[]{:S(2)}, u32[]{:S(2)}) collective-permute-start(f32[8,128]{1,0:T(8,128)} %get-tuple-element.25), channel_id=1, source_target_pairs={{0,8},{4,12},{8,0},{12,4},{16,24},{20,28},{24,16},{28,20},{1,25},{... | collective-permute-start | bytes 12296 | tf_op jit(solution)/shard_map/ppermute | solution.py:617
  5.3 0.0 copy-start.1
  5.3 0.0 copy-start.2
  5.3 0.0 copy-start.9
  5.3 1.7 %shift.1.shift_ref = f32[2,128,32]{2,1,0:T(8,128)S(1)} custom-call(f32[3,4,256]{2,1,0:T(4,128)S(1)} %bitcast.11, f32[3,4,256]{2,1,0:T(4,128)S(1)} %bitcast.13, s32[4,2,128]{2,1,0:T(2,128)S(1)} %copy-done.7, s32[4,2,32]{2,1,0:T(2,128)S(1)} %copy-done.8, f32[3,1024]{1,0:T(4,128)S(1)} %copy-done.3, f32[1,1024]{1,0:T(1,128)S(1)} %bitcast.14, ...), custom_call_target="tpu_custom_call" | custom-call | flops 3300000000 | bytes 262144 | tf_op jit(solution)/shard_map/shift/pallas_call | solution.py:619
  7.1 0.8 %partial.1 = (f32[264,128]{1,0:T(8,128)S(1)}, f32[4,2,32,128]{3,2,1,0:T(8,128)S(1)}, f32[144,128]{1,0:T(8,128)S(1)}, f32[144,128]{1,0:T(8,128)S(1)}) custom-call(f32[2,128,32]{2,1,0:T(8,128)S(1)} %shift.1.shift_ref, s32[4,2,128]{2,1,0:T(2,128)S(1)} %copy-done.7, s32[4,2,32]{2,1,0:T(2,128)S(1)} %copy-done.8, f32[4,2,32,128]{3,2,1,0:T(8,128)S(1)} %copy-done.2, ...), custom_call_target="tpu_custom_call" | custom-call | flops 2200000000 | bytes 262144 | tf_op jit(solution)/shard_map/partial/pallas_call | solution.py:630
  7.9 1.1 %collective-permute-done.info_ref = f32[8,128]{1,0:T(8,128)S(1)} collective-permute-done((f32[8,128]{1,0:T(8,128)}, f32[8,128]{1,0:T(8,128)S(1)}, u32[]{:S(2)}, u32[]{:S(2)}) %collective-permute-start) | collective-permute-done | bytes 4128 | tf_op jit(solution)/shard_map/ppermute | solution.py:617
  9.0 0.1 collective-permute-start.1
  9.1 1.3 %collective-permute-done.1.other_ref = f32[264,128]{1,0:T(8,128)S(1)} collective-permute-done((f32[264,128]{1,0:T(8,128)S(1)}, f32[264,128]{1,0:T(8,128)S(1)}, u32[]{:S(2)}, u32[]{:S(2)}) %collective-permute-start.1) | collective-permute-done | bytes 135200 | tf_op jit(solution)/shard_map/ppermute | solution.py:652
  10.5 2.3 %collective-permute-start.2 = (f32[264,128]{1,0:T(8,128)S(1)}, f32[264,128]{1,0:T(8,128)S(1)}, u32[]{:S(2)}, u32[]{:S(2)}) collective-permute-start(f32[264,128]{1,0:T(8,128)S(1)} %add.1.sum_ref), channel_id=1, source_target_pairs={{0,2},{1,3},{2,0},{3,1},{4,6},{5,7},{6,4},{7,5},{8,10},{9,11},{10,... | collective-permute-start | bytes 405512 | tf_op jit(solution)/shard_map/ppermute | solution.py:652
  12.7 1.5 %collective-permute-start.3 = (f32[144,128]{1,0:T(8,128)S(1)}, f32[144,128]{1,0:T(8,128)S(1)}, u32[]{:S(2)}, u32[]{:S(2)}) collective-permute-start(f32[144,128]{1,0:T(8,128)S(1)} %get-tuple-element.30), channel_id=1, source_target_pairs={{0,4},{4,0},{8,12},{12,8},{16,20},{20,16},{24,28},{28,24},{1,5},{5... | collective-permute-start | bytes 221192 | tf_op jit(solution)/shard_map/ppermute | solution.py:663
  14.3 2.3 %collective-permute-start.4 = (f32[144,128]{1,0:T(8,128)S(1)}, f32[144,128]{1,0:T(8,128)S(1)}, u32[]{:S(2)}, u32[]{:S(2)}) collective-permute-start(f32[144,128]{1,0:T(8,128)S(1)} %get-tuple-element.31), channel_id=1, source_target_pairs={{4,8},{12,16},{20,24},{8,4},{16,12},{24,20},{5,9},{13,17},{21,25},... | collective-permute-start | bytes 221192 | tf_op jit(solution)/shard_map/ppermute | solution.py:664
  16.6 0.3 collective-permute-done.2.got_ref
  16.8 2.2 %update.1 = (f32[4,2,32,128]{3,2,1,0:T(8,128)S(1)}, f32[8,128]{1,0:T(8,128)S(1)}, f32[8,128]{1,0:T(8,128)S(1)}, f32[144,128]{1,0:T(8,128)S(1)}, f32[144,128]{1,0:T(8,128)S(1)}) custom-call(f32[264,128]{1,0:T(8,128)S(1)} %add.1.sum_ref, f32[264,128]{1,0:T(8,128)S(1)} %collective-permute-done.2.got_ref, f32[4,2,32,128]{3,2,1,0:T(8,128)S(1)} %copy-done.2, ...), custom_call_target="tpu_custom_call" | custom-call | flops 4400000000 | bytes 262144 | tf_op jit(solution)/shard_map/update/pallas_call | solution.py:666
  19.0 1.6 %collective-permute-start.5 = (f32[144,128]{1,0:T(8,128)S(1)}, f32[144,128]{1,0:T(8,128)S(1)}, u32[]{:S(2)}, u32[]{:S(2)}) collective-permute-start(f32[144,128]{1,0:T(8,128)S(1)} %get-tuple-element.32), channel_id=1, source_target_pairs={{0,4},{4,0},{8,12},{12,8},{16,20},{20,16},{24,28},{28,24},{1,5},{5... | collective-permute-start | bytes 221192 | tf_op jit(solution)/shard_map/ppermute | solution.py:680
  20.6 3.6 %collective-permute-start.6 = (f32[144,128]{1,0:T(8,128)S(1)}, f32[144,128]{1,0:T(8,128)S(1)}, u32[]{:S(2)}, u32[]{:S(2)}) collective-permute-start(f32[144,128]{1,0:T(8,128)S(1)} %get-tuple-element.33), channel_id=1, source_target_pairs={{4,8},{12,16},{20,24},{8,4},{16,12},{24,20},{5,9},{13,17},{21,25},... | collective-permute-start | bytes 221192 | tf_op jit(solution)/shard_map/ppermute | solution.py:681
  24.2 0.0 collective-permute-done.3.pair_s_ref
  24.2 0.0 collective-permute-done.4.odd_s_ref
  24.2 0.0 collective-permute-done.5.pair_i_ref
  24.2 3.5 %collective-permute-done.6.odd_i_ref = f32[144,128]{1,0:T(8,128)S(1)} collective-permute-done((f32[144,128]{1,0:T(8,128)S(1)}, f32[144,128]{1,0:T(8,128)S(1)}, u32[]{:S(2)}, u32[]{:S(2)}) %collective-permute-start.6) | collective-permute-done | bytes 73760 | tf_op jit(solution)/shard_map/ppermute | solution.py:681
  27.8 0.9 %place.1 = (f32[4,2,32,128]{3,2,1,0:T(8,128)}, f32[4,2,32,128]{3,2,1,0:T(8,128)}, f32[3,4,256]{2,1,0:T(4,128)}, f32[1,4]{1,0:T(1,128)}, f32[1,4]{1,0:T(1,128)}, /*index=5*/f32[1,1]{1,0:T(1,128)}) custom-call(f32[4,2,32,128]{3,2,1,0:T(8,128)S(1)} %get-tuple-element.26.cur_ref, f32[4,2,32,128]{3,2,1,0:T(8,128)S(1)} %get-tuple-element.27.done_ref, ...), custom_call_target="tpu_custom_call" | custom-call | flops 1650000000 | bytes 262144 | tf_op jit(solution)/shard_map/place/pallas_call | solution.py:683
  (17 shorter events, 0.1 us)
Async XLA Ops:
  0.6 4.6 %copy-start = (f32[2,32,1024]{2,1,0:T(8,128)S(1)}, f32[2,32,1024]{2,1,0:T(8,128)}, u32[]{:S(2)}) copy-start(f32[2,32,1024]{2,1,0:T(8,128)} %orb_ref.1) | copy-start | bytes 786436
  0.6 4.6 %copy-start.3 = (f32[3,1024]{1,0:T(4,128)S(1)}, f32[3,1024]{1,0:T(4,128)}, u32[]{:S(2)}) copy-start(f32[3,1024]{1,0:T(4,128)} %cen_ref.1) | copy-start | bytes 36868
  0.7 4.6 %copy-start.4 = (f32[4,3,256]{2,0,1:T(4,128)S(1)}, f32[4,3,256]{2,0,1:T(4,128)}, u32[]{:S(2)}) copy-start(f32[4,3,256]{2,0,1:T(4,128)} %param.14) | copy-start | bytes 36868
  0.7 4.6 %copy-start.5 = (f32[4,3,256]{2,0,1:T(4,128)S(1)}, f32[4,3,256]{2,0,1:T(4,128)}, u32[]{:S(2)}) copy-start(f32[4,3,256]{2,0,1:T(4,128)} %param.15) | copy-start | bytes 36868
  0.7 4.6 %copy-start.6 = (f32[1024]{0:T(1024)S(1)}, f32[1024]{0:T(1024)}, u32[]{:S(2)}) copy-start(f32[1024]{0:T(1024)} %param.21) | copy-start | bytes 12292
  0.7 4.6 %copy-start.7 = (s32[4,2,128]{2,1,0:T(2,128)S(1)}, s32[4,2,128]{2,1,0:T(2,128)}, u32[]{:S(2)}) copy-start(s32[4,2,128]{2,1,0:T(2,128)} %order_ref.5) | copy-start | bytes 12292
  0.7 4.6 %copy-start.8 = (s32[4,2,32]{2,1,0:T(2,128)S(1)}, s32[4,2,32]{2,1,0:T(2,128)}, u32[]{:S(2)}) copy-start(s32[4,2,32]{2,1,0:T(2,128)} %flags_ref.5) | copy-start | bytes 3076
  3.3 5.7 %collective-permute-start = (f32[8,128]{1,0:T(8,128)}, f32[8,128]{1,0:T(8,128)S(1)}, u32[]{:S(2)}, u32[]{:S(2)}) collective-permute-start(f32[8,128]{1,0:T(8,128)} %get-tuple-element.25), channel_id=1, source_target_pairs={{0,8},{4,12},{8,0},{12,4},{16,24},{20,28},{24,16},{28,20},{1,25},{... | collective-permute-start | bytes 12296 | tf_op jit(solution)/shard_map/ppermute | solution.py:617
  5.3 1.8 %copy-start.1 = (f32[4,2,32,128]{3,2,1,0:T(8,128)S(1)}, f32[4,2,32,128]{3,2,1,0:T(8,128)}, u32[]{:S(2)}) copy-start(f32[4,2,32,128]{3,2,1,0:T(8,128)} %sla_ref.1) | copy-start | bytes 393220
  5.3 1.8 %copy-start.2 = (f32[4,2,32,128]{3,2,1,0:T(8,128)S(1)}, f32[4,2,32,128]{3,2,1,0:T(8,128)}, u32[]{:S(2)}) copy-start(f32[4,2,32,128]{3,2,1,0:T(8,128)} %inv_ref.3) | copy-start | bytes 393220
  5.3 1.8 %copy-start.9 = (f32[5,16,128]{2,1,0:T(8,128)S(1)}, f32[5,16,128]{2,1,0:T(8,128)}, u32[]{:S(2)}) copy-start(f32[5,16,128]{2,1,0:T(8,128)} %get-tuple-element.23.spots_ref) | copy-start | bytes 122884
  9.0 1.4 %collective-permute-start.1 = (f32[264,128]{1,0:T(8,128)S(1)}, f32[264,128]{1,0:T(8,128)S(1)}, u32[]{:S(2)}, u32[]{:S(2)}) collective-permute-start(f32[264,128]{1,0:T(8,128)S(1)} %join.1.mine_ref), channel_id=1, source_target_pairs={{0,1},{1,0},{2,3},{3,2},{4,5},{5,4},{6,7},{7,6},{8,9},{9,8},{10,11... | collective-permute-start | bytes 405512 | tf_op jit(solution)/shard_map/ppermute | solution.py:652
  10.5 6.4 %collective-permute-start.2 = (f32[264,128]{1,0:T(8,128)S(1)}, f32[264,128]{1,0:T(8,128)S(1)}, u32[]{:S(2)}, u32[]{:S(2)}) collective-permute-start(f32[264,128]{1,0:T(8,128)S(1)} %add.1.sum_ref), channel_id=1, source_target_pairs={{0,2},{1,3},{2,0},{3,1},{4,6},{5,7},{6,4},{7,5},{8,10},{9,11},{10,... | collective-permute-start | bytes 405512 | tf_op jit(solution)/shard_map/ppermute | solution.py:652
  12.7 11.5 %collective-permute-start.3 = (f32[144,128]{1,0:T(8,128)S(1)}, f32[144,128]{1,0:T(8,128)S(1)}, u32[]{:S(2)}, u32[]{:S(2)}) collective-permute-start(f32[144,128]{1,0:T(8,128)S(1)} %get-tuple-element.30), channel_id=1, source_target_pairs={{0,4},{4,0},{8,12},{12,8},{16,20},{20,16},{24,28},{28,24},{1,5},{5... | collective-permute-start | bytes 221192 | tf_op jit(solution)/shard_map/ppermute | solution.py:663
  14.3 9.9 %collective-permute-start.4 = (f32[144,128]{1,0:T(8,128)S(1)}, f32[144,128]{1,0:T(8,128)S(1)}, u32[]{:S(2)}, u32[]{:S(2)}) collective-permute-start(f32[144,128]{1,0:T(8,128)S(1)} %get-tuple-element.31), channel_id=1, source_target_pairs={{4,8},{12,16},{20,24},{8,4},{16,12},{24,20},{5,9},{13,17},{21,25},... | collective-permute-start | bytes 221192 | tf_op jit(solution)/shard_map/ppermute | solution.py:664
  19.0 5.2 %collective-permute-start.5 = (f32[144,128]{1,0:T(8,128)S(1)}, f32[144,128]{1,0:T(8,128)S(1)}, u32[]{:S(2)}, u32[]{:S(2)}) collective-permute-start(f32[144,128]{1,0:T(8,128)S(1)} %get-tuple-element.32), channel_id=1, source_target_pairs={{0,4},{4,0},{8,12},{12,8},{16,20},{20,16},{24,28},{28,24},{1,5},{5... | collective-permute-start | bytes 221192 | tf_op jit(solution)/shard_map/ppermute | solution.py:680
  20.6 7.1 %collective-permute-start.6 = (f32[144,128]{1,0:T(8,128)S(1)}, f32[144,128]{1,0:T(8,128)S(1)}, u32[]{:S(2)}, u32[]{:S(2)}) collective-permute-start(f32[144,128]{1,0:T(8,128)S(1)} %get-tuple-element.33), channel_id=1, source_target_pairs={{4,8},{12,16},{20,24},{8,4},{16,12},{24,20},{5,9},{13,17},{21,25},... | collective-permute-start | bytes 221192 | tf_op jit(solution)/shard_map/ppermute | solution.py:681
